TPU v7x, 32 devices: a whole 2x2x4 slice. The times are simulated.
32 devices in a mesh: groups: 2 (over x), ctx: 16 (over z, y, core).
Axes of the slice: x: 2, y: 2, z: 4, core: 2. Of those that a mesh axis runs over, the one named last changes fastest.
Arguments:
- projected: bfloat16 [3, 16384, 4096], P(None, ('groups', 'ctx')), parts along dimension 1, may hold values from -6 to 6
- conv_weight: float32 [3, 4, 4096], replicated, may hold values from -3 to 3
- level_codes: int32 [14, 32, 16384], P(None, None, ('groups', 'ctx')), parts along dimension 2, may hold values from 1 to 16
- out_gain: float32 [4096], replicated, may hold values from 0.25 to 1.75
Outputs:
- mixed: bfloat16 [16384, 4096], P(('groups', 'ctx')), parts along dimension 0
There are 2 independent parts, one for each index of `groups`. A program takes and returns all parts, laid end to end along the dimension named above; an argument that names none is the same for every part. Nothing has to cross between parts.
Inputs may be any that keep to these rules, and one draw needn't show every extreme that they name: `level_codes`: numerators of the level coefficients, which are the values divided by 8.
All inputs are finite; a program needn't handle non-finite values.
Results may differ from a plain program's by a relative error of at most 0.007.
Values may be sent and summed in bfloat16 or wider, within the bound.
No kernel may reach another device: no remote copies, remote signals or barrier semaphores. Data moves between devices by JAX's collectives and lax.ppermute only.
A program may use at most 192 MiB of HBM per device.

v0:
```python
import jax
import jax.numpy as jnp
from jax import lax
from jax.sharding import PartitionSpec as P


def shifted(value, axis, steps):
    count = lax.axis_size(axis)
    leading, last = (max(0, -steps), min(count, count - steps))
    return lax.ppermute(value, axis, [(source, source + steps) for source in range(leading, last)])


def intra_levels(length, bit_count):
    position = lax.iota(jnp.int32, length)
    differ = jnp.bitwise_xor(position[:, None], position[None, :])
    level = jnp.zeros((length, length), jnp.int32)
    for exponent in range(bit_count):
        level = level + (differ >= 2**exponent).astype(jnp.int32)
    causal = position[None, :] <= position[:, None]
    return jnp.stack(
        [(causal & (level == number)).astype(jnp.float32) for number in range(bit_count + 1)]
    )


def on_device(projected, conv_weight, level_codes, out_gain):
    tap_count = conv_weight.shape[1]
    row_count = projected.shape[1]
    model_width = projected.shape[2]
    head_count = level_codes.shape[1]
    head_dim = model_width // head_count
    tok_bits = row_count.bit_length() - 1
    ctx_count = lax.axis_size("ctx")
    ctx_bits = ctx_count.bit_length() - 1
    highest = lax.Precision.HIGHEST
    rim_rows = shifted(projected[:, row_count - tap_count + 1 :, :], "ctx", 1)
    padded = jnp.concatenate([rim_rows, projected], 1).astype(jnp.float32)
    running = jnp.zeros((3, row_count, model_width), jnp.float32)
    for offset in range(tap_count):
        running = (
            running + conv_weight[:, offset, None, :] * padded[:, offset : offset + row_count, :]
        )
    mixed_in = running.astype(jnp.bfloat16)
    query_rows = mixed_in[0].reshape(row_count, head_count, head_dim)
    key_rows = mixed_in[1].reshape(row_count, head_count, head_dim)
    value_rows = mixed_in[2].reshape(row_count, head_count, head_dim)
    level_weight = level_codes.astype(jnp.float32) / 8.0
    states = jnp.einsum("shd,she->hde", key_rows, value_rows, preferred_element_type=jnp.float32)
    outgoing = states.reshape(1, head_count, head_dim, head_dim)
    spread = lax.all_to_all(outgoing, "ctx", split_axis=1, concat_axis=0, tiled=True)
    span_ids = lax.iota(jnp.int32, ctx_count)
    differ = jnp.bitwise_xor(span_ids[:, None], span_ids[None, :])
    earlier = span_ids[None, :] < span_ids[:, None]
    bucket_masks = jnp.stack(
        [
            (earlier & (differ >= 2**bit_index) & (differ < 2 ** (bit_index + 1))).astype(
                jnp.float32
            )
            for bit_index in range(ctx_bits)
        ]
    )
    buckets = jnp.einsum("bcs,spde->bcpde", bucket_masks, spread, precision=highest).astype(
        jnp.bfloat16
    )
    returned = lax.all_to_all(buckets, "ctx", split_axis=1, concat_axis=2, tiled=True)
    fenwick_bf = returned[:, 0]
    onehot = intra_levels(row_count, tok_bits)
    group_size = min(8, head_count)

    def group_block(group_index):
        head_start = group_index * group_size
        query_part = lax.dynamic_slice_in_dim(query_rows, head_start, group_size, 1)
        key_part = lax.dynamic_slice_in_dim(key_rows, head_start, group_size, 1)
        value_part = lax.dynamic_slice_in_dim(value_rows, head_start, group_size, 1)
        level_part = lax.dynamic_slice_in_dim(level_weight, head_start, group_size, 1)[
            : tok_bits + 1
        ]
        scores = jnp.einsum(
            "thd,shd->hts", query_part, key_part, preferred_element_type=jnp.float32
        )
        weight = jnp.einsum("lts,lht->hts", onehot, level_part, precision=highest)
        weights = (scores * weight).astype(jnp.bfloat16)
        return jnp.einsum("hts,shd->thd", weights, value_part, preferred_element_type=jnp.float32)

    blocks = lax.map(group_block, jnp.arange(head_count // group_size, dtype=jnp.int32))
    inside = blocks.transpose(1, 0, 2, 3).reshape(row_count, head_count, head_dim)
    across = jnp.zeros((row_count, head_count, head_dim), jnp.float32)
    for bit_index in range(ctx_bits):
        product = jnp.einsum(
            "thd,hde->the", query_rows, fenwick_bf[bit_index], preferred_element_type=jnp.float32
        )
        across = across + level_weight[tok_bits + 1 + bit_index].T[:, :, None] * product
    combined = inside + across
    inverse = lax.rsqrt(jnp.mean(combined * combined, -1, keepdims=True) + 1e-06)
    normed = combined * inverse * out_gain.reshape(head_count, head_dim)
    return normed.astype(jnp.bfloat16).reshape(row_count, model_width)


def solution(mesh):
    placed = (P(None, ("groups", "ctx"), None), P(), P(None, None, ("groups", "ctx")), P())
    return jax.shard_map(
        on_device, mesh=mesh, in_specs=placed, out_specs=P(("groups", "ctx"), None), check_vma=False
    )
```

profile of v0, /device:TPU:13, one launch (start us, length us, event | category | flops | bytes accessed | tf_op | source)
XLA Modules:
  0.0 414.7 jit_solution(12851691643838151552)
XLA Ops:
  0.0 1.0 slice.69
  1.0 3.7 collective-permute-start
  4.7 11.9 %compare_and_fusion = (pred[1,512,512]{2,0,1:T(4,128)(4,1)}, pred[1,512,512]{2,0,1:T(4,128)(4,1)}) fusion(), kind=kLoop, calls=%fused_computation.29 | loop fusion | flops 8388608 | bytes 524288 | tf_op jit(solution)/shard_map/and | solution.py:21
  16.6 1.6 fusion.56
  18.3 16.6 %copy.58 = bf16[3,512,4096]{1,2,0:T(8,128)(2,1)} copy(bf16[3,512,4096]{2,1,0:T(8,128)(2,1)} %param.6) | data formatting | bytes 25165824 | tf_op args[0]
  34.9 1.6 copy.57
  36.5 16.9 %maximum_convert_fusion = f32[3,515,4096]{1,2,0:T(8,128)} fusion(bf16[3,512,4096]{1,2,0:T(8,128)(2,1)} %copy.58, bf16[3,3,4096]{1,2,0:T(8,128)(2,1)S(1)} %copy.57), kind=kLoop, calls=%fused_computation.18 | loop fusion | flops 25313280 | bytes 37969920 | tf_op jit(solution)/shard_map/convert_element_type | solution.py:36
  53.5 58.4 %fusion.15 = bf16[3,512,4096]{1,2,0:T(8,128)(2,1)} fusion(f32[3,515,4096]{1,2,0:T(8,128)} %maximum_convert_fusion, f32[3,4096]{1,0:T(4,128)S(1)} %get-tuple-element.113, f32[3,4096]{1,0:T(4,128)S(1)} %get-tuple-element.114, f32[3,4096]{1,0:T(4,128)S(1)} %get-tuple-element.115, f32[3,4096]{1,0:T(4,128)S(1)} %get-tuple-element.116), kind=kLoop, calls=%fused_computation.12 | loop fusion | flops 50331648 | bytes 113442816 | tf_op jit(solution)/shard_map/convert_element_type | solution.py:42
  111.9 6.9 %fusion.54 = (bf16[1,512,4096]{1,2,0:T(8,128)(2,1)S(1)}, bf16[1,512,4096]{1,2,0:T(8,128)(2,1)}, bf16[1,512,4096]{1,2,0:T(8,128)(2,1)S(1)}) fusion(bf16[3,512,4096]{1,2,0:T(8,128)(2,1)} %fusion.15), kind=kLoop, calls=%fused_computation.97 | loop fusion | bytes 25165824 | tf_op jit(solution)/shard_map/slice | solution.py:44
  118.8 2.0 copy-done.1
  120.8 1.3 copy-done.2
  122.1 2.6 convolution_bitcast_fusion
  124.8 5.4 %all-to-all-start = ((f32[1,32,128,128]{3,2,0,1:T(8,128)}), f32[1,32,128,128]{3,2,0,1:T(8,128)S(1)}, u32[]{:S(2)}, u32[]{:S(2)}) async-start(f32[1,32,128,128]{3,2,0,1:T(8,128)} %convolution_bitcast_fusion), calls=%async_computation | async-start | bytes 4194304 | tf_op jit(solution)/shard_map/all_to_all | solution.py:49
  130.1 11.8 %compare_and_fusion.2 = (pred[1,512,512]{2,0,1:T(4,128)(4,1)S(1)}, pred[1,512,512]{2,0,1:T(4,128)(4,1)}) fusion(), kind=kLoop, calls=%fused_computation.31 | loop fusion | flops 8388608 | bytes 524288 | tf_op jit(solution)/shard_map/and | solution.py:21
  141.9 11.9 %compare_and_fusion.4 = (pred[1,512,512]{2,0,1:T(4,128)(4,1)}, pred[1,512,512]{2,0,1:T(4,128)(4,1)}) fusion(), kind=kLoop, calls=%fused_computation.33 | loop fusion | flops 8388608 | bytes 524288 | tf_op jit(solution)/shard_map/and | solution.py:21
  153.8 11.9 %compare_and_fusion.6 = (pred[1,512,512]{2,0,1:T(4,128)(4,1)}, pred[1,512,512]{2,0,1:T(4,128)(4,1)}) fusion(), kind=kLoop, calls=%fused_computation.35 | loop fusion | flops 8388608 | bytes 524288 | tf_op jit(solution)/shard_map/and | solution.py:21
  165.7 11.8 %all-to-all-done = f32[1,32,128,128]{3,2,0,1:T(8,128)S(1)} async-done(((f32[1,32,128,128]{3,2,0,1:T(8,128)}), f32[1,32,128,128]{3,2,0,1:T(8,128)S(1)}, u32[]{:S(2)}, u32[]{:S(2)}) %all-to-all-start) | async-done | bytes 2097184 | tf_op jit(solution)/shard_map/all_to_all | solution.py:49
  177.5 3.8 convolution_convert_fusion
  181.3 3.1 copy.65
  184.3 15.2 %all-to-all-start.1 = ((bf16[4,16,2,128,128]{4,3,2,0,1:T(8,128)(2,1)}), bf16[4,16,2,128,128]{4,3,2,0,1:T(8,128)(2,1)}, u32[]{:S(2)}, u32[]{:S(2)}) async-start(bf16[4,16,2,128,128]{4,3,2,0,1:T(8,128)(2,1)} %copy.65), calls=%async_computation.1 | async-start | bytes 8388608 | tf_op jit(solution)/shard_map/all_to_all | solution.py:64
  199.6 11.9 %compare_and_fusion.8 = (pred[1,512,512]{2,0,1:T(4,128)(4,1)}, pred[1,512,512]{2,0,1:T(4,128)(4,1)}) fusion(), kind=kLoop, calls=%fused_computation.37 | loop fusion | flops 8388608 | bytes 524288 | tf_op jit(solution)/shard_map/and | solution.py:21
  211.4 33.7 %stack.10 = pred[10,512,512]{2,0,1:T(8,128)(4,1)} concatenate(pred[1,512,512]{2,0,1:T(4,128)(4,1)} %get-tuple-element.130, pred[1,512,512]{2,0,1:T(4,128)(4,1)} %get-tuple-element.129, pred[1,512,512]{2,0,1:T(4,128)(4,1)} %get-tuple-element.128, pred[1,512,512]{2,0,1:T(4,128)(4,1)} %get-tuple-element.127, pred[1,512,512]{2,0,1:T(4,128)(4,1)} %get-tuple-element.126, ...), dimensions={0} | concatenate | bytes 5242880 | tf_op jit(solution)/shard_map/stack | solution.py:20
  245.1 10.4 %stack.11 = f32[10,512,512]{2,0,1:T(8,128)} convert(pred[10,512,512]{2,0,1:T(8,128)(4,1)} %stack.10) | non-fusion elementwise | flops 2621440 | bytes 13107200 | tf_op jit(solution)/shard_map/stack | solution.py:20
  255.6 112.7 %while.10 = (s32[]{:T(128)}, f32[4,512,8,128]{1,3,2,0:T(8,128)}, s32[4]{0:T(128)S(1)}, bf16[512,32,128]{0,2,1:T(8,128)(2,1)}, bf16[512,32,128]{0,2,1:T(8,128)(2,...) while((s32[]{:T(128)}, f32[4,512,8,128]{1,3,2,0:T(8,128)}, ...), condition=%wide.region_1.2_spmd, body=%wide.region_0.1_spmd.sunk | while | flops 1329594368 | bytes 33327284 | solution.py:84
  255.7 0.6 dynamic_slice.31
  256.9 0.8 copy.116
  257.7 13.8 %fusion.86 = f32[512,8,512]{2,1,0:T(8,128)} fusion(f32[10,8,512]{0,1,2:T(8,128)S(1)} %copy.116, f32[10,512,512]{2,0,1:T(8,128)} %get-tuple-element.211), kind=kOutput, calls=%fused_computation.100.clone.1 | convolution fusion | flops 251658240 | bytes 19038208 | tf_op jit(solution)/shard_map/while/body/eval_jaxpr/lts,lht->hts/dot_general | solution.py:80
  271.5 12.2 %bitcast_dynamic-update-slice_fusion.2 = f32[4,512,8,128]{1,3,2,0:T(8,128)} fusion(f32[4,512,8,128]{1,3,2,0:T(8,128)} %get-tuple-element.193, s32[]{:T(128)} %get-tuple-element.192, f32[512,8,512]{2,1,0:T(8,128)} %fusion.86, bf16[512,32,128]{0,2,1:T(8,128)(2,1)} %get-tuple-element.209, s32[]{:T(128)S(6)} %select_n.3, ...), kind=kOutput, calls=%fused_computation.4.clone.1 | convolution fusion | flops 1077936128 | bytes 13633536 | tf_op jit(solution)/shard_map/while/body/eval_jaxpr/hts,shd->thd/dot_general | solution.py:82
  283.8 0.6 dynamic_slice.31
  285.0 0.8 copy.116
  285.9 13.8 %fusion.86 = f32[512,8,512]{2,1,0:T(8,128)} fusion(f32[10,8,512]{0,1,2:T(8,128)S(1)} %copy.116, f32[10,512,512]{2,0,1:T(8,128)} %get-tuple-element.211), kind=kOutput, calls=%fused_computation.100.clone.1 | convolution fusion | flops 251658240 | bytes 19038208 | tf_op jit(solution)/shard_map/while/body/eval_jaxpr/lts,lht->hts/dot_general | solution.py:80
  299.7 12.2 %bitcast_dynamic-update-slice_fusion.2 = f32[4,512,8,128]{1,3,2,0:T(8,128)} fusion(f32[4,512,8,128]{1,3,2,0:T(8,128)} %get-tuple-element.193, s32[]{:T(128)} %get-tuple-element.192, f32[512,8,512]{2,1,0:T(8,128)} %fusion.86, bf16[512,32,128]{0,2,1:T(8,128)(2,1)} %get-tuple-element.209, s32[]{:T(128)S(6)} %select_n.3, ...), kind=kOutput, calls=%fused_computation.4.clone.1 | convolution fusion | flops 1077936128 | bytes 13633536 | tf_op jit(solution)/shard_map/while/body/eval_jaxpr/hts,shd->thd/dot_general | solution.py:82
  311.9 0.6 dynamic_slice.31
  313.1 0.8 copy.116
  313.9 13.8 %fusion.86 = f32[512,8,512]{2,1,0:T(8,128)} fusion(f32[10,8,512]{0,1,2:T(8,128)S(1)} %copy.116, f32[10,512,512]{2,0,1:T(8,128)} %get-tuple-element.211), kind=kOutput, calls=%fused_computation.100.clone.1 | convolution fusion | flops 251658240 | bytes 19038208 | tf_op jit(solution)/shard_map/while/body/eval_jaxpr/lts,lht->hts/dot_general | solution.py:80
  327.7 12.2 %bitcast_dynamic-update-slice_fusion.2 = f32[4,512,8,128]{1,3,2,0:T(8,128)} fusion(f32[4,512,8,128]{1,3,2,0:T(8,128)} %get-tuple-element.193, s32[]{:T(128)} %get-tuple-element.192, f32[512,8,512]{2,1,0:T(8,128)} %fusion.86, bf16[512,32,128]{0,2,1:T(8,128)(2,1)} %get-tuple-element.209, s32[]{:T(128)S(6)} %select_n.3, ...), kind=kOutput, calls=%fused_computation.4.clone.1 | convolution fusion | flops 1077936128 | bytes 13633536 | tf_op jit(solution)/shard_map/while/body/eval_jaxpr/hts,shd->thd/dot_general | solution.py:82
  340.0 0.6 dynamic_slice.31
  341.2 0.8 copy.116
  342.1 13.8 %fusion.86 = f32[512,8,512]{2,1,0:T(8,128)} fusion(f32[10,8,512]{0,1,2:T(8,128)S(1)} %copy.116, f32[10,512,512]{2,0,1:T(8,128)} %get-tuple-element.211), kind=kOutput, calls=%fused_computation.100.clone.1 | convolution fusion | flops 251658240 | bytes 19038208 | tf_op jit(solution)/shard_map/while/body/eval_jaxpr/lts,lht->hts/dot_general | solution.py:80
  355.9 12.3 %bitcast_dynamic-update-slice_fusion.2 = f32[4,512,8,128]{1,3,2,0:T(8,128)} fusion(f32[4,512,8,128]{1,3,2,0:T(8,128)} %get-tuple-element.193, s32[]{:T(128)} %get-tuple-element.192, f32[512,8,512]{2,1,0:T(8,128)} %fusion.86, bf16[512,32,128]{0,2,1:T(8,128)(2,1)} %get-tuple-element.209, s32[]{:T(128)S(6)} %select_n.3, ...), kind=kOutput, calls=%fused_computation.4.clone.1 | convolution fusion | flops 1077936128 | bytes 13633536 | tf_op jit(solution)/shard_map/while/body/eval_jaxpr/hts,shd->thd/dot_general | solution.py:82
  368.3 2.8 fusion.55
  371.2 0.6 copy-done
  371.8 4.5 %fusion.58 = f32[32,128,512]{2,1,0:T(8,128)} fusion(bf16[32,128,128]{2,1,0:T(8,128)(2,1)S(1)} %bitcast.124, bf16[512,32,128]{0,2,1:T(8,128)(2,1)S(1)} %copy-done), kind=kOutput, calls=%fused_computation.101 | convolution fusion | flops 536870912 | bytes 13631488 | tf_op jit(solution)/shard_map/thd,hde->the/dot_general | solution.py:88
  376.3 4.5 %fusion.59 = f32[32,128,512]{2,1,0:T(8,128)} fusion(bf16[32,128,128]{2,1,0:T(8,128)(2,1)S(1)} %bitcast.123, bf16[512,32,128]{0,2,1:T(8,128)(2,1)S(1)} %copy-done), kind=kOutput, calls=%fused_computation.102 | convolution fusion | flops 536870912 | bytes 13631488 | tf_op jit(solution)/shard_map/thd,hde->the/dot_general | solution.py:88
  380.9 4.5 %fusion.60 = f32[32,128,512]{2,1,0:T(8,128)} fusion(bf16[32,128,128]{2,1,0:T(8,128)(2,1)S(1)} %bitcast.122, bf16[512,32,128]{0,2,1:T(8,128)(2,1)S(1)} %copy-done), kind=kOutput, calls=%fused_computation.103 | convolution fusion | flops 536870912 | bytes 13631488 | tf_op jit(solution)/shard_map/thd,hde->the/dot_general | solution.py:88
  385.4 17.4 %multiply_reduce_fusion = (f32[512,32]{0,1:T(8,128)S(1)}, f32[512,32,128]{0,2,1:T(8,128)}) fusion(bf16[32,128,128]{2,1,0:T(8,128)(2,1)S(1)} %bitcast.121, bf16[512,32,128]{0,2,1:T(8,128)(2,1)} %get-tuple-element.216, f32[512,32]{0,1:T(8,128)S(1)} %get-tuple-element.104, f32[32,128,512]{2,1,0:T(8,128)} %fusion.60, f32[512,32]{0,1:T(8,128)S(1)} %get-tuple-element.105, ...), kind=kOutput, calls=%fused_computation.28 | convolution fusion | flops 557826048 | bytes 47513600 | tf_op jit(solution)/shard_map/thd,hde->the/dot_general | solution.py:88
  402.8 5.3 %multiply_convert_fusion = bf16[512,32,128]{0,2,1:T(8,128)(2,1)} fusion(f32[512,32,128]{0,2,1:T(8,128)} %get-tuple-element.112, f32[32,128]{1,0:T(8,128)S(1)} %bitcast.125, f32[512,32]{0,1:T(8,128)S(1)} %add_rsqrt_fusion), kind=kLoop, calls=%fused_computation.27 | loop fusion | flops 6291456 | bytes 12664832 | tf_op jit(solution)/shard_map/convert_element_type | solution.py:95
  408.1 6.3 %copy.78 = bf16[512,4096]{1,0:T(8,128)(2,1)} copy(bf16[512,4096]{0,1:T(8,128)(2,1)} %bitcast.119) | data formatting | bytes 8388608 | tf_op jit(solution)/shard_map/reshape | solution.py:95
  (26 shorter events, 0.4 us)
Async XLA Ops:
  1.0 34.0 %collective-permute-start = (bf16[3,3,4096]{2,1,0:T(4,128)(2,1)S(1)}, bf16[3,3,4096]{2,1,0:T(4,128)(2,1)S(1)}, u32[]{:S(2)}, u32[]{:S(2)}) collective-permute-start(bf16[3,3,4096]{2,1,0:T(4,128)(2,1)S(1)} %slice.69), channel_id=1, source_target_pairs={{0,1},{1,2},{2,3},{3,4},{4,5},{5,6},{6,7},{7,8},{8,9},{9,10},{10,1... | collective-permute-start | bytes 221192 | tf_op jit(solution)/shard_map/ppermute | solution.py:10
  118.8 2.0 copy-start.1
  118.8 3.3 copy-start.2
  124.8 52.7 %all-to-all-start = ((f32[1,32,128,128]{3,2,0,1:T(8,128)}), f32[1,32,128,128]{3,2,0,1:T(8,128)S(1)}, u32[]{:S(2)}, u32[]{:S(2)}) async-start(f32[1,32,128,128]{3,2,0,1:T(8,128)} %convolution_bitcast_fusion), calls=%async_computation | async-start | bytes 4194304 | tf_op jit(solution)/shard_map/all_to_all | solution.py:49
  181.2 30.2 %copy-start.3 = (pred[1,512,512]{2,0,1:T(4,128)(4,1)S(1)}, pred[1,512,512]{2,0,1:T(4,128)(4,1)}, u32[]{:S(2)}) copy-start(pred[1,512,512]{2,0,1:T(4,128)(4,1)} %get-tuple-element.121) | copy-start | bytes 786436
  181.3 30.2 %copy-start.4 = (pred[1,512,512]{2,0,1:T(4,128)(4,1)S(1)}, pred[1,512,512]{2,0,1:T(4,128)(4,1)}, u32[]{:S(2)}) copy-start(pred[1,512,512]{2,0,1:T(4,128)(4,1)} %get-tuple-element.122) | copy-start | bytes 786436
  184.3 184.0 %all-to-all-start.1 = ((bf16[4,16,2,128,128]{4,3,2,0,1:T(8,128)(2,1)}), bf16[4,16,2,128,128]{4,3,2,0,1:T(8,128)(2,1)}, u32[]{:S(2)}, u32[]{:S(2)}) async-start(bf16[4,16,2,128,128]{4,3,2,0,1:T(8,128)(2,1)} %copy.65), calls=%async_computation.1 | async-start | bytes 8388608 | tf_op jit(solution)/shard_map/all_to_all | solution.py:64
  245.1 10.4 %copy-start.5 = (s32[14,32,512]{2,1,0:T(8,128)S(1)}, s32[14,32,512]{2,1,0:T(8,128)}, u32[]{:S(2)}) copy-start(s32[14,32,512]{2,1,0:T(8,128)} %param.8) | copy-start | bytes 2752516
  368.3 3.5 copy-start
  385.4 17.4 %copy-start.6 = (f32[4096]{0:T(1024)S(1)}, f32[4096]{0:T(1024)}, u32[]{:S(2)}) copy-start(f32[4096]{0:T(1024)} %param.9) | copy-start | bytes 49156
where the time goes:
time: 422 us; the launch traced here: 415 us
  other arithmetic  150 us (36%)
  matrix products  141 us (33%)
  local copies, waits for them, and re-layouts  83.5 us (20%)
  starting transfers between devices  24.3 us (6%)
  waiting for transfers between devices  11.8 us (3%)
    and x5, other arithmetic, intra_levels(): causal & (level == number)  59.2 us
    convert_element_type x1, other arithmetic, on_device(): mixed_in = running.astype(jnp.bfloat16)  58.4 us
    dot_general x4, matrix products, group_block(): weight = jnp.einsum('lts,lht->hts', onehot, level_part, precision=highest)  55.2 us
    dot_general x4, matrix products, group_block(): jnp.einsum('hts,shd->thd', weights, value_part, preferred_element_type=jn...  48.9 us
    another operation x1, local copies, waits for them, and re-layouts, intra_levels(): jnp.stack([(causal & (level == number)).astype(jnp.float32) for number in...  33.7 us
    dot_general x4, matrix products, on_device(): jnp.einsum('thd,hde->the', query_rows, fenwick_bf[bit_index], preferred_e...  31 us
    unnamed x17, local copies, waits for them, and re-layouts  20.7 us
    convert_element_type x1, other arithmetic, on_device(): padded = jnp.concatenate([rim_rows, projected], 1).astype(jnp.float32)  16.9 us
  transfers between devices with their start and end apart: 3, of which 1 were waited for; matrix products, arithmetic and copies ran while one was open for 56% of the time, Pallas kernels for 0%

commit v1 on v0

v1 whole, which is shorter than its diff:
```python
import functools

import jax
import jax.numpy as jnp
from jax import lax
from jax.experimental import pallas as pl
from jax.experimental.pallas import tpu as pltpu
from jax.sharding import PartitionSpec as P

NT = (((1,), (1,)), ((), ()))
ROOM = 56 * 1024 * 1024


def convolve(x_ref, rim_ref, w_ref, pad_ref, emit):
    rows, width = x_ref.shape
    taps = w_ref.shape[0]
    base = pad_ref.shape[0] - rows
    step = min(64, rows)
    pad_ref[base - (taps - 1) : base, :] = rim_ref[...].astype(jnp.float32)
    for row in range(0, rows, step):
        pad_ref[base + row : base + row + step, :] = x_ref[row : row + step, :].astype(jnp.float32)
    for col in range(0, width, 128):
        w = w_ref[:, col : col + 128]
        for row in range(0, rows, step):
            total = None
            for tap in range(taps):
                at = base - (taps - 1) + tap + row
                term = w[tap : tap + 1, :] * pad_ref[at : at + step, col : col + 128]
                total = term if total is None else total + term
            emit(row, col, total)


def kv_kernel(place, xk, xv, rk, rv, wk, wv, k_out, vt_out, s_out, padk, padv, vrow):
    rows = xk.shape[0]
    heads, dim = vt_out.shape[0], vt_out.shape[1]

    def emit_k(row, col, total):
        k_out[row : row + total.shape[0], col : col + 128] = total.astype(jnp.bfloat16)

    def emit_v(row, col, total):
        vrow[row : row + total.shape[0], col : col + 128] = total.astype(jnp.bfloat16)

    convolve(xk, rk, wk, padk, emit_k)
    convolve(xv, rv, wv, padv, emit_v)
    for head in range(heads):
        cols = slice(head * dim, (head + 1) * dim)
        vt = vrow[:, cols].T
        vt_out[head] = vt
        s_out[head] = jnp.dot(vt, k_out[:, cols], preferred_element_type=jnp.float32).astype(
            s_out.dtype
        )


def inner_weights(lam, block):
    rows = lam[0].shape[1]
    lane = lax.broadcasted_iota(jnp.int32, (8, rows), 1)
    sub = lax.broadcasted_iota(jnp.int32, (8, rows), 0)
    zero = jnp.zeros((8, rows), jnp.float32)
    near = zero
    differ = (lane & 7) ^ sub
    for level in range(1, 4):
        near = jnp.where((differ >> (level - 1)) == 1, lam[level], near)
    near = jnp.where(differ == 0, lam[0], near)
    near = jnp.where(sub <= (lane & 7), near, zero)
    group = (lane >> 3) & (block // 8 - 1)
    out = []
    for first in range(0, block // 8, 8):
        index = sub + first
        apart = index ^ group
        far = zero
        for level in range(4, block.bit_length()):
            far = jnp.where((apart >> (level - 4)) == 1, lam[level], far)
        far = jnp.where(index < group, far, zero)
        for i in range(8):
            wide = jnp.broadcast_to(far[i : i + 1, :], (8, rows))
            out.append(jnp.where(group == first + i, near, wide))
    return out


def inside_kernel(place, xq, rq, wq, k_in, vt_in, codes, q_out, in_out, padq, p_ref):
    rows = xq.shape[0]
    heads, dim = vt_in.shape[0], vt_in.shape[1]
    block = min(128, rows)
    wide = min(256, rows)
    levels = codes.shape[0]
    bits = rows.bit_length() - 1

    def emit_q(row, col, total):
        q_out[row : row + total.shape[0], col : col + 128] = total.astype(jnp.bfloat16)

    convolve(xq, rq, wq, padq, emit_q)
    for head in range(heads):
        cols = slice(head * dim, (head + 1) * dim)
        at = lax.rem(place[1] + pl.program_id(0) * heads + head, codes.shape[1])
        lam = [codes[level, pl.ds(at, 1), :].astype(jnp.float32) * 0.125 for level in range(bits + 1)]
        near = inner_weights(lam, block)
        for first in range(0, rows, wide):
            reach = first + wide
            scores = lax.dot_general(
                k_in[0:reach, cols],
                q_out[first : first + wide, cols],
                NT,
                preferred_element_type=jnp.float32,
            )
            for t0 in range(first, reach, block):
                span = slice(t0 - first, t0 - first + block)
                for s0 in range(0, reach, block):
                    if s0 > t0:
                        p_ref[head, s0 : s0 + block, t0 : t0 + block] = jnp.zeros(
                            (block, block), jnp.bfloat16
                        )
                        continue
                    if s0 == t0:
                        weight = jnp.concatenate([n[:, t0 : t0 + block] for n in near], 0)
                    else:
                        level = (s0 ^ t0).bit_length()
                        weight = lam[level][:, t0 : t0 + block]
                    part = scores[s0 : s0 + block, span] * weight
                    p_ref[head, s0 : s0 + block, t0 : t0 + block] = part.astype(jnp.bfloat16)
            in_out[head, :, first:reach] = jnp.dot(
                vt_in[head, :, 0:reach],
                p_ref[head, 0:reach, first:reach],
                preferred_element_type=jnp.float32,
            )


def across_kernel(bits, inner, place, q_in, in_in, codes, gain, *rest):
    states, out = rest[:bits], rest[-1]
    heads, dim, rows = in_in.shape
    for head in range(heads):
        cols = slice(head * dim, (head + 1) * dim)
        at = lax.rem(place[1] + pl.program_id(0) * heads + head, codes.shape[1])
        q = q_in[:, cols]
        total = in_in[head]
        for bit in range(bits):
            scale = place[3 + bit].astype(jnp.float32) * 0.125
            lam = codes[inner + bit, pl.ds(at, 1), :].astype(jnp.float32) * scale
            part = lax.dot_general(states[bit][head], q, NT, preferred_element_type=jnp.float32)
            total = total + lam * part
        mean = jnp.sum(total * total, 0, keepdims=True) * (1.0 / dim)
        normed = total * lax.rsqrt(mean + 1e-06)
        out[:, cols] = (normed.T * gain[:, cols]).astype(jnp.bfloat16)


def on_device(projected, conv_weight, level_codes, out_gain):
    taps = conv_weight.shape[1]
    rows, width = projected.shape[1:]
    levels, head_count = level_codes.shape[:2]
    dim = width // head_count
    tok_bits = rows.bit_length() - 1
    count = lax.axis_size("ctx")
    bits = count.bit_length() - 1
    index = lax.axis_index("ctx")
    core, side = index & 1, (index >> 1) & 1
    half, quarter = head_count // 2, head_count // 4
    group = 2
    code_rows = min(8, head_count)
    flags = [(index >> bit) & 1 for bit in range(bits)]
    gain = out_gain.reshape(1, width)

    def exchange(value, bit):
        return lax.ppermute(value, "ctx", [(i, i ^ (1 << bit)) for i in range(count)])

    rim = lax.ppermute(
        projected[:, rows - taps + 1 :, :], "ctx", [(i, i + 1) for i in range(count - 1)]
    )

    def place(head, local):
        return jnp.stack([head // group, head, local // group] + flags).astype(jnp.int32)

    def third(which, size):
        return pl.BlockSpec((None, size, group * dim), lambda i, p: (which, 0, p[0] + i))

    def per_head(*shape):
        return pl.BlockSpec((group, *shape), lambda i, p: (i, 0, 0))

    column = pl.BlockSpec((rows, group * dim), lambda i, p: (0, i))
    code_spec = pl.BlockSpec(
        (levels, code_rows, rows), lambda i, p: (0, (p[1] + i * group) // code_rows, 0)
    )
    params = pltpu.CompilerParams(vmem_limit_bytes=ROOM)
    pad = pltpu.VMEM((rows + 8, group * dim), jnp.float32)
    bf16, f32 = jnp.bfloat16, jnp.float32

    def key_value(head, count_heads):
        return pl.pallas_call(
            kv_kernel,
            grid_spec=pltpu.PrefetchScalarGridSpec(
                num_scalar_prefetch=1,
                grid=(count_heads // group,),
                in_specs=[
                    third(1, rows),
                    third(2, rows),
                    third(1, taps - 1),
                    third(2, taps - 1),
                    third(1, taps),
                    third(2, taps),
                ],
                out_specs=[column, per_head(dim, rows), per_head(dim, dim)],
                scratch_shapes=[pad, pad, pltpu.VMEM((rows, group * dim), bf16)],
            ),
            out_shape=[
                jax.ShapeDtypeStruct((rows, count_heads * dim), bf16),
                jax.ShapeDtypeStruct((count_heads, dim, rows), bf16),
                jax.ShapeDtypeStruct((count_heads, dim, dim), bf16),
            ],
            compiler_params=params,
            name="key_value",
        )(place(head, head * 0), projected, projected, rim, rim, conv_weight, conv_weight)

    def inside(head, keys, values):
        count_heads = values.shape[0]
        return pl.pallas_call(
            inside_kernel,
            grid_spec=pltpu.PrefetchScalarGridSpec(
                num_scalar_prefetch=1,
                grid=(count_heads // group,),
                in_specs=[
                    third(0, rows),
                    third(0, taps - 1),
                    third(0, taps),
                    column,
                    per_head(dim, rows),
                    code_spec,
                ],
                out_specs=[column, per_head(dim, rows)],
                scratch_shapes=[pad, pltpu.VMEM((group, rows, rows), bf16)],
            ),
            out_shape=[
                jax.ShapeDtypeStruct((rows, count_heads * dim), bf16),
                jax.ShapeDtypeStruct((count_heads, dim, rows), f32),
            ],
            compiler_params=params,
            name="inside",
        )(place(head, head * 0), projected, rim, conv_weight, keys, values, level_codes)

    def across(head, local, queries, inner, states, out):
        count_heads = states[0][0].shape[0] if isinstance(states[0], tuple) else states[0].shape[0]
        arrays, specs = [], []
        for state in states:
            if isinstance(state, tuple):
                arrays.append(state[0])
                specs.append(pl.BlockSpec((group, dim, dim), lambda i, p: (p[2] + i, 0, 0)))
                count_heads = quarter
            else:
                arrays.append(state)
                specs.append(pl.BlockSpec((group, dim, dim), lambda i, p: (i, 0, 0)))
        extra = [] if out is None else [out]
        return pl.pallas_call(
            functools.partial(across_kernel, bits, tok_bits + 1),
            grid_spec=pltpu.PrefetchScalarGridSpec(
                num_scalar_prefetch=1,
                grid=(quarter // group,),
                in_specs=[
                    pl.BlockSpec((rows, group * dim), lambda i, p: (0, p[2] + i)),
                    pl.BlockSpec((group, dim, rows), lambda i, p: (p[2] + i, 0, 0)),
                    code_spec,
                    pl.BlockSpec((1, group * dim), lambda i, p: (0, p[0] + i)),
                ]
                + specs
                + [pl.BlockSpec(memory_space=pl.ANY)] * len(extra),
                out_specs=pl.BlockSpec((rows, group * dim), lambda i, p: (0, p[0] + i)),
            ),
            out_shape=jax.ShapeDtypeStruct((rows, width), bf16),
            input_output_aliases={} if out is None else {5 + bits: 0},
            compiler_params=params,
            name="across",
        )(place(head, local), queries, inner, level_codes, gain, *arrays, *extra)

    other_head, own_head = (1 - core) * half, core * half
    near, far = side * quarter, (1 - side) * quarter

    def part(value, start):
        return lax.dynamic_slice_in_dim(value, start, quarter, 0)

    other_k, other_v, other_s = key_value(other_head, half)
    got0 = exchange(other_s, 0)
    own_k, own_v, own_s = key_value(own_head, half)
    total = own_s + got0
    near1 = exchange(part(total, far), 1)
    running = part(total, near) + near1
    far1 = exchange(part(total, near), 1)
    got0_other = exchange(own_s, 0)
    own_q, own_in = inside(own_head, own_k, own_v)
    other_q, other_in = inside(other_head, other_k, other_v)
    nears, fars = [near1], [far1]
    for bit in range(2, bits):
        ones = (1 << bit) - 4
        got = None
        for low in range(1 << (bit - 2)):
            pairs = [
                (i, (i & ~ones) | (low << 2) | (1 << bit))
                for i in range(count)
                if i & ones == ones and not i >> bit & 1
            ]
            piece = lax.ppermute(running, "ctx", pairs)
            got = piece if got is None else got + piece
        running = running + got
        nears.append(got)
        fars.append(exchange(got, 1))
    other_nears = [exchange(value, 0) for value in nears]
    other_fars = [exchange(value, 0) for value in fars]
    out = across(own_head + near, near, own_q, own_in, [(got0,)] + nears, None)
    out = across(other_head + near, near, other_q, other_in, [(got0_other,)] + other_nears, out)
    out = across(own_head + far, far, own_q, own_in, [(got0,)] + fars, out)
    out = across(other_head + far, far, other_q, other_in, [(got0_other,)] + other_fars, out)
    return out


def solution(mesh):
    placed = (P(None, ("groups", "ctx"), None), P(), P(None, None, ("groups", "ctx")), P())
    return jax.shard_map(
        on_device, mesh=mesh, in_specs=placed, out_specs=P(("groups", "ctx"), None), check_vma=False
    )
```

time: 422 us -> 138 us (0.33)
  the two profiles are of different devices: /device:TPU:13 before, /device:TPU:11 now
where the time goes in v1:
time: 138 us; the launch traced here: 137 us
  Pallas kernels  77.9 us (56%)
  waiting for transfers between devices  27.9 us (20%)
  starting transfers between devices  23.4 us (17%)
  local copies, waits for them, and re-layouts  6.21 us (4%)
  other arithmetic  1.56 us (1%)
    pallas_call x2, Pallas kernels, inside(): pl.pallas_call(inside_kernel, grid_spec=pltpu.PrefetchScalarGridSpec(num_...  28.7 us
    pallas_call x2, Pallas kernels, key_value(): pl.pallas_call(kv_kernel, grid_spec=pltpu.PrefetchScalarGridSpec(num_scal...  25.8 us
    pallas_call x4, Pallas kernels, across(): pl.pallas_call(functools.partial(across_kernel, bits, tok_bits + 1), grid...  23.5 us
    ppermute x12, waiting for transfers between devices, exchange(): return lax.ppermute(value, 'ctx', [(i, i ^ 1 << bit) for i in range(count)])  15.4 us
    ppermute x12, starting transfers between devices, exchange(): return lax.ppermute(value, 'ctx', [(i, i ^ 1 << bit) for i in range(count)])  12.9 us
    ppermute x3, waiting for transfers between devices, on_device(): piece = lax.ppermute(running, 'ctx', pairs)  11.5 us
    ppermute x3, starting transfers between devices, on_device(): piece = lax.ppermute(running, 'ctx', pairs)  6.83 us
    another operation x6, local copies, waits for them, and re-layouts, place(): jnp.stack([head // group, head, local // group] + flags).astype(jnp.int32)  3.77 us
  transfers between devices with their start and end apart: 16, of which 7 were waited for; matrix products, arithmetic and copies ran while one was open for 3% of the time, Pallas kernels for 43%

profile of v1, /device:TPU:11, one launch (start us, length us, event | category | flops | bytes accessed | tf_op | source)
XLA Modules:
  0.0 137.2 jit_solution(2626902246404980202)
XLA Ops:
  0.0 1.0 slice.3
  1.0 3.7 %collective-permute-start = (bf16[3,3,4096]{2,1,0:T(4,128)(2,1)S(1)}, bf16[3,3,4096]{2,1,0:T(4,128)(2,1)S(1)}, u32[]{:S(2)}, u32[]{:S(2)}) collective-permute-start(bf16[3,3,4096]{2,1,0:T(4,128)(2,1)S(1)} %slice.3), channel_id=1, source_target_pairs={{0,1},{1,2},{2,3},{3,4},{4,5},{5,6},{6,7},{7,8},{8,9},{9,10},{10,1... | collective-permute-start | bytes 221192 | tf_op jit(solution)/shard_map/ppermute | solution.py:164
  4.7 0.6 stack.58.place
  5.3 1.0 collective-permute-done.rk.rv.rq
  6.3 0.6 copy-done.1
  7.0 12.9 %key_value.2 = (bf16[512,2048]{1,0:T(8,128)(2,1)}, bf16[16,128,512]{2,1,0:T(8,128)(2,1)}, bf16[16,128,128]{2,1,0:T(8,128)(2,1)}) custom-call(s32[7]{0:T(128)} %stack.58.place, bf16[3,512,4096]{2,1,0:T(8,128)(2,1)} %xq.3, bf16[3,512,4096]{2,1,0:T(8,128)(2,1)} %xq.3, bf16[3,3,4096]{2,1,0:T(4,128)(2,1)} %copy-done.1, bf16[3,3,4096]{2,1,0:T(4,128)(2,1)} %copy-done.1, ...), custom_call_target="tpu_custom_call" | custom-call | tf_op jit(solution)/shard_map/key_value/pallas_call | solution.py:186
  19.8 2.2 %collective-permute-start.2 = (bf16[16,128,128]{2,1,0:T(8,128)(2,1)}, bf16[16,128,128]{2,1,0:T(8,128)(2,1)S(1)}, u32[]{:S(2)}, u32[]{:S(2)}) collective-permute-start(bf16[16,128,128]{2,1,0:T(8,128)(2,1)} %get-tuple-element.20), channel_id=1, source_target_pairs={{0,1},{1,0},{2,3},{3,2},{4,5},{5,4},{6,7},{7,6},{8,9},{9,8},{10,11... | collective-permute-start | bytes 1572872 | tf_op jit(solution)/shard_map/ppermute | solution.py:162
  22.1 0.6 stack.61.place
  22.7 12.9 %key_value.3 = (bf16[512,2048]{1,0:T(8,128)(2,1)}, bf16[16,128,512]{2,1,0:T(8,128)(2,1)}, bf16[16,128,128]{2,1,0:T(8,128)(2,1)}) custom-call(s32[7]{0:T(128)} %stack.61.place, bf16[3,512,4096]{2,1,0:T(8,128)(2,1)} %xq.3, bf16[3,512,4096]{2,1,0:T(8,128)(2,1)} %xq.3, bf16[3,3,4096]{2,1,0:T(4,128)(2,1)} %copy-done.1, bf16[3,3,4096]{2,1,0:T(4,128)(2,1)} %copy-done.1, ...), custom_call_target="tpu_custom_call" | custom-call | tf_op jit(solution)/shard_map/key_value/pallas_call | solution.py:186
  35.6 1.4 %add.41 = bf16[16,128,128]{2,1,0:T(8,128)(2,1)S(1)} add(bf16[16,128,128]{2,1,0:T(8,128)(2,1)} %get-tuple-element.19, bf16[16,128,128]{2,1,0:T(8,128)(2,1)S(1)} %collective-permute-done.2.rest_0_) | non-fusion elementwise | flops 262144 | bytes 1572864 | tf_op jit(solution)/shard_map/add | solution.py:279
  37.0 0.4 collective-permute-start.5
  37.4 7.6 %collective-permute-done.5.rest_1_ = bf16[8,128,128]{2,1,0:T(8,128)(2,1)S(1)} collective-permute-done((bf16[8,128,128]{2,1,0:T(8,128)(2,1)S(1)}, bf16[8,128,128]{2,1,0:T(8,128)(2,1)S(1)}, u32[]{:S(2)}, u32[]{:S(2)}) %collective-permute-start.5) | collective-permute-done | bytes 262176 | tf_op jit(solution)/shard_map/ppermute | solution.py:162
  45.0 1.3 collective-permute-start.6
  46.3 0.9 collective-permute-start.1
  47.2 6.7 %collective-permute-done.6.rest_2_ = bf16[8,128,128]{2,1,0:T(8,128)(2,1)S(1)} collective-permute-done((bf16[8,128,128]{2,1,0:T(8,128)(2,1)S(1)}, bf16[8,128,128]{2,1,0:T(8,128)(2,1)S(1)}, u32[]{:S(2)}, u32[]{:S(2)}) %collective-permute-start.6) | collective-permute-done | bytes 262176 | tf_op jit(solution)/shard_map/ppermute | solution.py:296
  53.9 0.1 add.45
  54.0 4.2 %collective-permute-start.10 = (bf16[8,128,128]{2,1,0:T(8,128)(2,1)S(1)}, bf16[8,128,128]{2,1,0:T(8,128)(2,1)S(1)}, u32[]{:S(2)}, u32[]{:S(2)}) collective-permute-start(bf16[8,128,128]{2,1,0:T(8,128)(2,1)S(1)} %add.45), channel_id=1, source_target_pairs={{4,12},{5,13},{6,14},{7,15},{20,28},{21,29},{22,30},{23,31}} | collective-permute-start | bytes 786440 | tf_op jit(solution)/shard_map/ppermute | solution.py:296
  58.2 1.3 collective-permute-start.9
  59.6 2.1 %collective-permute-start.13 = (bf16[8,128,128]{2,1,0:T(8,128)(2,1)S(1)}, bf16[8,128,128]{2,1,0:T(8,128)(2,1)S(1)}, u32[]{:S(2)}, u32[]{:S(2)}) collective-permute-start(bf16[8,128,128]{2,1,0:T(8,128)(2,1)S(1)} %collective-permute-done.5.rest_1_), channel_id=1, source_target_pairs={{0,1},{1,0},{2,3},{3,2},{4,5},{5,4},{6,7},{7,6},{8,9},{9,8},{10,11... | collective-permute-start | bytes 786440 | tf_op jit(solution)/shard_map/ppermute | solution.py:162
  61.6 0.4 collective-permute-start.3
  62.0 0.1 collective-permute-done.10
  62.1 1.0 collective-permute-start.7
  63.1 4.6 %collective-permute-done.9 = bf16[8,128,128]{2,1,0:T(8,128)(2,1)S(1)} collective-permute-done((bf16[8,128,128]{2,1,0:T(8,128)(2,1)S(1)}, bf16[8,128,128]{2,1,0:T(8,128)(2,1)S(1)}, u32[]{:S(2)}, u32[]{:S(2)}) %collective-permute-start.9) | collective-permute-done | bytes 262176 | tf_op jit(solution)/shard_map/ppermute | solution.py:296
  67.7 0.1 add.46.rest_3_
  67.8 0.4 collective-permute-start.11
  68.2 0.0 collective-permute-done.1.rest_0_
  68.2 2.9 %collective-permute-start.14 = (bf16[8,128,128]{2,1,0:T(8,128)(2,1)S(1)}, bf16[8,128,128]{2,1,0:T(8,128)(2,1)}, u32[]{:S(2)}, u32[]{:S(2)}) collective-permute-start(bf16[8,128,128]{2,1,0:T(8,128)(2,1)S(1)} %collective-permute-done.6.rest_2_), channel_id=1, source_target_pairs={{0,1},{1,0},{2,3},{3,2},{4,5},{5,4},{6,7},{7,6},{8,9},{9,8},{10,11... | collective-permute-start | bytes 786440 | tf_op jit(solution)/shard_map/ppermute | solution.py:162
  71.1 0.0 collective-permute-done.13.rest_1_
  71.1 0.1 collective-permute-start.15
  71.2 0.0 collective-permute-done.3.rest_1_
  71.2 0.4 collective-permute-start.4
  71.7 3.5 %collective-permute-done.7.rest_2_ = bf16[8,128,128]{2,1,0:T(8,128)(2,1)S(1)} collective-permute-done((bf16[8,128,128]{2,1,0:T(8,128)(2,1)S(1)}, bf16[8,128,128]{2,1,0:T(8,128)(2,1)S(1)}, u32[]{:S(2)}, u32[]{:S(2)}) %collective-permute-start.7) | collective-permute-done | bytes 262176 | tf_op jit(solution)/shard_map/ppermute | solution.py:162
  75.1 1.3 collective-permute-start.8
  76.4 4.3 %collective-permute-done.11.rest_3_ = bf16[8,128,128]{2,1,0:T(8,128)(2,1)S(1)} collective-permute-done((bf16[8,128,128]{2,1,0:T(8,128)(2,1)S(1)}, bf16[8,128,128]{2,1,0:T(8,128)(2,1)S(1)}, u32[]{:S(2)}, u32[]{:S(2)}) %collective-permute-start.11) | collective-permute-done | bytes 262176 | tf_op jit(solution)/shard_map/ppermute | solution.py:162
  80.7 0.8 collective-permute-start.12
  81.6 0.7 stack.135.place
  82.3 0.6 stack.132.place
  82.9 0.6 stack.128.place
  83.5 0.7 stack.55.place
  84.2 14.4 %inside.3 = (bf16[512,2048]{1,0:T(8,128)(2,1)}, f32[16,128,512]{2,1,0:T(8,128)}) custom-call(s32[7]{0:T(128)} %stack.61.place, bf16[3,512,4096]{2,1,0:T(8,128)(2,1)} %xq.3, bf16[3,3,4096]{2,1,0:T(4,128)(2,1)} %copy-done.1, f32[3,4,4096]{2,1,0:T(4,128)} %wq.3, bf16[512,2048]{1,0:T(8,128)(2,1)} %get-tuple-element.21.k_in, ...), custom_call_target="tpu_custom_call" | custom-call | tf_op jit(solution)/shard_map/inside/pallas_call | solution.py:213
  98.6 14.3 %inside.2 = (bf16[512,2048]{1,0:T(8,128)(2,1)}, f32[16,128,512]{2,1,0:T(8,128)}) custom-call(s32[7]{0:T(128)} %stack.58.place, bf16[3,512,4096]{2,1,0:T(8,128)(2,1)} %xq.3, bf16[3,3,4096]{2,1,0:T(4,128)(2,1)} %copy-done.1, f32[3,4,4096]{2,1,0:T(4,128)} %wq.3, bf16[512,2048]{1,0:T(8,128)(2,1)} %get-tuple-element.15.k_in, ...), custom_call_target="tpu_custom_call" | custom-call | tf_op jit(solution)/shard_map/inside/pallas_call | solution.py:213
  113.0 5.9 %across.4.rest_4_ = bf16[512,4096]{1,0:T(8,128)(2,1)} custom-call(s32[7]{0:T(128)} %stack.135.place, bf16[512,2048]{1,0:T(8,128)(2,1)} %get-tuple-element.23.q_in, f32[16,128,512]{2,1,0:T(8,128)} %get-tuple-element.24.in_in, s32[14,32,512]{2,1,0:T(8,128)} %codes.11, f32[1,4096]{1,0:T(1,128)} %bitcast.19, bf16[16,128,128]{2,1,0:T(8,128)(2,1)} %copy-done, ...), custom_call_target="tpu_custom_call" | custom-call | tf_op jit(solution)/shard_map/across/pallas_call | solution.py:249
  118.8 0.0 collective-permute-done.15.rest_3_
  118.8 5.9 %across.5.rest_4_ = bf16[512,4096]{1,0:T(8,128)(2,1)} custom-call(s32[7]{0:T(128)} %stack.132.place, bf16[512,2048]{1,0:T(8,128)(2,1)} %get-tuple-element.17.q_in, f32[16,128,512]{2,1,0:T(8,128)} %get-tuple-element.18.in_in, s32[14,32,512]{2,1,0:T(8,128)} %codes.11, f32[1,4096]{1,0:T(1,128)} %bitcast.20, ...), custom_call_target="tpu_custom_call", output_to_operand_aliasing={{}: (9, {})} | custom-call | tf_op jit(solution)/shard_map/across/pallas_call | solution.py:249
  124.7 5.9 %across.6.rest_4_ = bf16[512,4096]{1,0:T(8,128)(2,1)} custom-call(s32[7]{0:T(128)} %stack.128.place, bf16[512,2048]{1,0:T(8,128)(2,1)} %get-tuple-element.23.q_in, f32[16,128,512]{2,1,0:T(8,128)} %get-tuple-element.24.in_in, s32[14,32,512]{2,1,0:T(8,128)} %codes.11, f32[1,4096]{1,0:T(1,128)} %bitcast.21, ...), custom_call_target="tpu_custom_call", output_to_operand_aliasing={{}: (9, {})} | custom-call | tf_op jit(solution)/shard_map/across/pallas_call | solution.py:249
  130.6 0.7 copy-done.10
  131.3 0.1 copy-done.11
  131.4 5.9 %across.7 = bf16[512,4096]{1,0:T(8,128)(2,1)} custom-call(s32[7]{0:T(128)} %stack.55.place, bf16[512,2048]{1,0:T(8,128)(2,1)} %get-tuple-element.17.q_in, f32[16,128,512]{2,1,0:T(8,128)} %get-tuple-element.18.in_in, s32[14,32,512]{2,1,0:T(8,128)} %codes.11, f32[1,4096]{1,0:T(1,128)} %bitcast.22, ...), custom_call_target="tpu_custom_call", output_to_operand_aliasing={{}: (9, {})} | custom-call | tf_op jit(solution)/shard_map/across/pallas_call | solution.py:249
  (28 shorter events, 0.1 us)
Async XLA Ops:
  1.0 5.3 %collective-permute-start = (bf16[3,3,4096]{2,1,0:T(4,128)(2,1)S(1)}, bf16[3,3,4096]{2,1,0:T(4,128)(2,1)S(1)}, u32[]{:S(2)}, u32[]{:S(2)}) collective-permute-start(bf16[3,3,4096]{2,1,0:T(4,128)(2,1)S(1)} %slice.3), channel_id=1, source_target_pairs={{0,1},{1,2},{2,3},{3,4},{4,5},{5,6},{6,7},{7,8},{8,9},{9,10},{10,1... | collective-permute-start | bytes 221192 | tf_op jit(solution)/shard_map/ppermute | solution.py:164
  6.3 0.6 copy-start.1
  19.8 15.8 %collective-permute-start.2 = (bf16[16,128,128]{2,1,0:T(8,128)(2,1)}, bf16[16,128,128]{2,1,0:T(8,128)(2,1)S(1)}, u32[]{:S(2)}, u32[]{:S(2)}) collective-permute-start(bf16[16,128,128]{2,1,0:T(8,128)(2,1)} %get-tuple-element.20), channel_id=1, source_target_pairs={{0,1},{1,0},{2,3},{3,2},{4,5},{5,4},{6,7},{7,6},{8,9},{9,8},{10,11... | collective-permute-start | bytes 1572872 | tf_op jit(solution)/shard_map/ppermute | solution.py:162
  35.6 63.0 %copy-start = (bf16[16,128,128]{2,1,0:T(8,128)(2,1)}, bf16[16,128,128]{2,1,0:T(8,128)(2,1)S(1)}, u32[]{:S(2)}) copy-start(bf16[16,128,128]{2,1,0:T(8,128)(2,1)S(1)} %collective-permute-done.2.rest_0_) | copy-start | bytes 1572868
  37.0 8.0 %collective-permute-start.5 = (bf16[8,128,128]{2,1,0:T(8,128)(2,1)S(1)}, bf16[8,128,128]{2,1,0:T(8,128)(2,1)S(1)}, u32[]{:S(2)}, u32[]{:S(2)}) collective-permute-start(bf16[8,128,128]{2,1,0:T(8,128)(2,1)S(1)} %constant_dynamic-slice_fusion), channel_id=1, source_target_pairs={{0,2},{1,3},{2,0},{3,1},{4,6},{5,7},{6,4},{7,5},{8,10},{9,11},{10,... | collective-permute-start | bytes 786440 | tf_op jit(solution)/shard_map/ppermute | solution.py:162
  45.0 53.6 %copy-start.5 = (bf16[8,128,128]{2,1,0:T(8,128)(2,1)}, bf16[8,128,128]{2,1,0:T(8,128)(2,1)S(1)}, u32[]{:S(2)}) copy-start(bf16[8,128,128]{2,1,0:T(8,128)(2,1)S(1)} %collective-permute-done.5.rest_1_) | copy-start | bytes 786436
  45.0 8.9 %collective-permute-start.6 = (bf16[8,128,128]{2,1,0:T(8,128)(2,1)S(1)}, bf16[8,128,128]{2,1,0:T(8,128)(2,1)S(1)}, u32[]{:S(2)}, u32[]{:S(2)}) collective-permute-start(bf16[8,128,128]{2,1,0:T(8,128)(2,1)S(1)} %get-tuple-element.25), channel_id=1, source_target_pairs={{0,4},{1,5},{2,6},{3,7},{8,12},{9,13},{10,14},{11,15},{16,20},{17,... | collective-permute-start | bytes 786440 | tf_op jit(solution)/shard_map/ppermute | solution.py:296
  46.3 21.9 %collective-permute-start.1 = (bf16[16,128,128]{2,1,0:T(8,128)(2,1)}, bf16[16,128,128]{2,1,0:T(8,128)(2,1)S(1)}, u32[]{:S(2)}, u32[]{:S(2)}) collective-permute-start(bf16[16,128,128]{2,1,0:T(8,128)(2,1)} %get-tuple-element.19), channel_id=1, source_target_pairs={{0,1},{1,0},{2,3},{3,2},{4,5},{5,4},{6,7},{7,6},{8,9},{9,8},{10,11... | collective-permute-start | bytes 1572872 | tf_op jit(solution)/shard_map/ppermute | solution.py:162
  53.9 44.6 %copy-start.3 = (bf16[8,128,128]{2,1,0:T(8,128)(2,1)}, bf16[8,128,128]{2,1,0:T(8,128)(2,1)S(1)}, u32[]{:S(2)}) copy-start(bf16[8,128,128]{2,1,0:T(8,128)(2,1)S(1)} %collective-permute-done.6.rest_2_) | copy-start | bytes 786436
  54.0 8.1 %collective-permute-start.10 = (bf16[8,128,128]{2,1,0:T(8,128)(2,1)S(1)}, bf16[8,128,128]{2,1,0:T(8,128)(2,1)S(1)}, u32[]{:S(2)}, u32[]{:S(2)}) collective-permute-start(bf16[8,128,128]{2,1,0:T(8,128)(2,1)S(1)} %add.45), channel_id=1, source_target_pairs={{4,12},{5,13},{6,14},{7,15},{20,28},{21,29},{22,30},{23,31}} | collective-permute-start | bytes 786440 | tf_op jit(solution)/shard_map/ppermute | solution.py:296
  58.2 9.5 %collective-permute-start.9 = (bf16[8,128,128]{2,1,0:T(8,128)(2,1)S(1)}, bf16[8,128,128]{2,1,0:T(8,128)(2,1)S(1)}, u32[]{:S(2)}, u32[]{:S(2)}) collective-permute-start(bf16[8,128,128]{2,1,0:T(8,128)(2,1)S(1)} %add.45), channel_id=1, source_target_pairs={{4,8},{5,9},{6,10},{7,11},{20,24},{21,25},{22,26},{23,27}} | collective-permute-start | bytes 786440 | tf_op jit(solution)/shard_map/ppermute | solution.py:296
  59.6 11.6 %collective-permute-start.13 = (bf16[8,128,128]{2,1,0:T(8,128)(2,1)S(1)}, bf16[8,128,128]{2,1,0:T(8,128)(2,1)S(1)}, u32[]{:S(2)}, u32[]{:S(2)}) collective-permute-start(bf16[8,128,128]{2,1,0:T(8,128)(2,1)S(1)} %collective-permute-done.5.rest_1_), channel_id=1, source_target_pairs={{0,1},{1,0},{2,3},{3,2},{4,5},{5,4},{6,7},{7,6},{8,9},{9,8},{10,11... | collective-permute-start | bytes 786440 | tf_op jit(solution)/shard_map/ppermute | solution.py:162
  61.6 9.6 %collective-permute-start.3 = (bf16[8,128,128]{2,1,0:T(8,128)(2,1)S(1)}, bf16[8,128,128]{2,1,0:T(8,128)(2,1)S(1)}, u32[]{:S(2)}, u32[]{:S(2)}) collective-permute-start(bf16[8,128,128]{2,1,0:T(8,128)(2,1)S(1)} %get-tuple-element.26), channel_id=1, source_target_pairs={{0,2},{1,3},{2,0},{3,1},{4,6},{5,7},{6,4},{7,5},{8,10},{9,11},{10,... | collective-permute-start | bytes 786440 | tf_op jit(solution)/shard_map/ppermute | solution.py:162
  62.1 13.0 %collective-permute-start.7 = (bf16[8,128,128]{2,1,0:T(8,128)(2,1)S(1)}, bf16[8,128,128]{2,1,0:T(8,128)(2,1)S(1)}, u32[]{:S(2)}, u32[]{:S(2)}) collective-permute-start(bf16[8,128,128]{2,1,0:T(8,128)(2,1)S(1)} %collective-permute-done.6.rest_2_), channel_id=1, source_target_pairs={{0,2},{1,3},{2,0},{3,1},{4,6},{5,7},{6,4},{7,5},{8,10},{9,11},{10,... | collective-permute-start | bytes 786440 | tf_op jit(solution)/shard_map/ppermute | solution.py:162
  67.8 30.8 %copy-start.4 = (bf16[8,128,128]{2,1,0:T(8,128)(2,1)}, bf16[8,128,128]{2,1,0:T(8,128)(2,1)S(1)}, u32[]{:S(2)}) copy-start(bf16[8,128,128]{2,1,0:T(8,128)(2,1)S(1)} %add.46.rest_3_) | copy-start | bytes 786436
  67.8 12.9 %collective-permute-start.11 = (bf16[8,128,128]{2,1,0:T(8,128)(2,1)S(1)}, bf16[8,128,128]{2,1,0:T(8,128)(2,1)S(1)}, u32[]{:S(2)}, u32[]{:S(2)}) collective-permute-start(bf16[8,128,128]{2,1,0:T(8,128)(2,1)S(1)} %add.46.rest_3_), channel_id=1, source_target_pairs={{0,2},{1,3},{2,0},{3,1},{4,6},{5,7},{6,4},{7,5},{8,10},{9,11},{10,... | collective-permute-start | bytes 786440 | tf_op jit(solution)/shard_map/ppermute | solution.py:162
  68.2 30.4 %copy-start.2 = (bf16[16,128,128]{2,1,0:T(8,128)(2,1)}, bf16[16,128,128]{2,1,0:T(8,128)(2,1)S(1)}, u32[]{:S(2)}) copy-start(bf16[16,128,128]{2,1,0:T(8,128)(2,1)S(1)} %collective-permute-done.1.rest_0_) | copy-start | bytes 1572868
  68.2 50.6 %collective-permute-start.14 = (bf16[8,128,128]{2,1,0:T(8,128)(2,1)S(1)}, bf16[8,128,128]{2,1,0:T(8,128)(2,1)}, u32[]{:S(2)}, u32[]{:S(2)}) collective-permute-start(bf16[8,128,128]{2,1,0:T(8,128)(2,1)S(1)} %collective-permute-done.6.rest_2_), channel_id=1, source_target_pairs={{0,1},{1,0},{2,3},{3,2},{4,5},{5,4},{6,7},{7,6},{8,9},{9,8},{10,11... | collective-permute-start | bytes 786440 | tf_op jit(solution)/shard_map/ppermute | solution.py:162
  71.1 27.5 %copy-start.8 = (bf16[8,128,128]{2,1,0:T(8,128)(2,1)}, bf16[8,128,128]{2,1,0:T(8,128)(2,1)S(1)}, u32[]{:S(2)}) copy-start(bf16[8,128,128]{2,1,0:T(8,128)(2,1)S(1)} %collective-permute-done.13.rest_1_) | copy-start | bytes 786436
  71.1 47.7 %collective-permute-start.15 = (bf16[8,128,128]{2,1,0:T(8,128)(2,1)S(1)}, bf16[8,128,128]{2,1,0:T(8,128)(2,1)}, u32[]{:S(2)}, u32[]{:S(2)}) collective-permute-start(bf16[8,128,128]{2,1,0:T(8,128)(2,1)S(1)} %add.46.rest_3_), channel_id=1, source_target_pairs={{0,1},{1,0},{2,3},{3,2},{4,5},{5,4},{6,7},{7,6},{8,9},{9,8},{10,11... | collective-permute-start | bytes 786440 | tf_op jit(solution)/shard_map/ppermute | solution.py:162
  71.2 27.4 %copy-start.6 = (bf16[8,128,128]{2,1,0:T(8,128)(2,1)}, bf16[8,128,128]{2,1,0:T(8,128)(2,1)S(1)}, u32[]{:S(2)}) copy-start(bf16[8,128,128]{2,1,0:T(8,128)(2,1)S(1)} %collective-permute-done.3.rest_1_) | copy-start | bytes 786436
  71.2 59.3 %collective-permute-start.4 = (bf16[8,128,128]{2,1,0:T(8,128)(2,1)S(1)}, bf16[8,128,128]{2,1,0:T(8,128)(2,1)S(1)}, u32[]{:S(2)}, u32[]{:S(2)}) collective-permute-start(bf16[8,128,128]{2,1,0:T(8,128)(2,1)S(1)} %collective-permute-done.3.rest_1_), channel_id=1, source_target_pairs={{0,1},{1,0},{2,3},{3,2},{4,5},{5,4},{6,7},{7,6},{8,9},{9,8},{10,11... | collective-permute-start | bytes 786440 | tf_op jit(solution)/shard_map/ppermute | solution.py:162
  75.1 23.5 %copy-start.7 = (bf16[8,128,128]{2,1,0:T(8,128)(2,1)}, bf16[8,128,128]{2,1,0:T(8,128)(2,1)S(1)}, u32[]{:S(2)}) copy-start(bf16[8,128,128]{2,1,0:T(8,128)(2,1)S(1)} %collective-permute-done.7.rest_2_) | copy-start | bytes 786436
  75.1 55.5 %collective-permute-start.8 = (bf16[8,128,128]{2,1,0:T(8,128)(2,1)S(1)}, bf16[8,128,128]{2,1,0:T(8,128)(2,1)S(1)}, u32[]{:S(2)}, u32[]{:S(2)}) collective-permute-start(bf16[8,128,128]{2,1,0:T(8,128)(2,1)S(1)} %collective-permute-done.7.rest_2_), channel_id=1, source_target_pairs={{0,1},{1,0},{2,3},{3,2},{4,5},{5,4},{6,7},{7,6},{8,9},{9,8},{10,11... | collective-permute-start | bytes 786440 | tf_op jit(solution)/shard_map/ppermute | solution.py:162
  80.7 17.9 %copy-start.9 = (bf16[8,128,128]{2,1,0:T(8,128)(2,1)}, bf16[8,128,128]{2,1,0:T(8,128)(2,1)S(1)}, u32[]{:S(2)}) copy-start(bf16[8,128,128]{2,1,0:T(8,128)(2,1)S(1)} %collective-permute-done.11.rest_3_) | copy-start | bytes 786436
  80.7 49.9 %collective-permute-start.12 = (bf16[8,128,128]{2,1,0:T(8,128)(2,1)S(1)}, bf16[8,128,128]{2,1,0:T(8,128)(2,1)}, u32[]{:S(2)}, u32[]{:S(2)}) collective-permute-start(bf16[8,128,128]{2,1,0:T(8,128)(2,1)S(1)} %collective-permute-done.11.rest_3_), channel_id=1, source_target_pairs={{0,1},{1,0},{2,3},{3,2},{4,5},{5,4},{6,7},{7,6},{8,9},{9,8},{10,11... | collective-permute-start | bytes 786440 | tf_op jit(solution)/shard_map/ppermute | solution.py:162
  130.6 0.7 copy-start.10
  130.6 0.8 copy-start.11

commit v2 on v0

v2 whole, which is shorter than its diff:
```python
import functools

import jax
import jax.numpy as jnp
from jax import lax
from jax.experimental import pallas as pl
from jax.experimental.pallas import tpu as pltpu
from jax.sharding import PartitionSpec as P

NT = (((1,), (1,)), ((), ()))
ROOM = 8 * 1024 * 1024
GROUP = 8
VMEM = pltpu.VMEM


def lanes(head, dim):
    return pl.ds(pl.multiple_of(head * dim, dim), dim)


def base_of(place, where, heads):
    index = place[0]
    return (((index & 1) ^ where[0]) * 2 + (((index >> 1) & 1) ^ where[1])) * heads


def convolve(x, at, rim, w, which, head, dim, step=128):
    rows, taps = x.shape[1], w.shape[1]
    cols = lanes(head, dim)
    w_rows = [w[which, tap : tap + 1, cols] for tap in range(taps)]
    before = jnp.concatenate(
        [jnp.zeros((9 - taps, dim), jnp.float32), rim[which, :, cols].astype(jnp.float32)], 0
    )
    out = []
    for row in range(0, rows, step):
        chunk = x[at, row : row + step, cols].astype(jnp.float32)
        full = jnp.concatenate([before, chunk], 0)
        total = None
        for tap in range(taps - 2, -1, -2):
            pair = w_rows[tap + 1] * full + w_rows[tap] * pltpu.roll(full, 1, 0)
            if tap < taps - 2:
                pair = pltpu.roll(pair, taps - 2 - tap, 0)
            total = pair if total is None else total + pair
        out.append(total[8:].astype(jnp.bfloat16))
        before = chunk[step - 8 :]
    return jnp.concatenate(out, 0)


def kv_kernel(first, merge, extra, where, place, rim, w, x, *rest):
    rest, sems = rest[:-1], rest[-1]
    copies, arrivals = [], {}
    if first:
        code_home, gain_home, *rest = rest
        k_out, vt_out, s_out, x_in, xq, codes, gain, w_in = rest
        home, x, w_home, w = x, x_in, w, w_in
        heads, dim = vt_out.shape[:2]
        base = base_of(place, where, heads)
        head_count = x.shape[2] // dim
        width = GROUP * dim

        def bring(source, target):
            copy = pltpu.make_async_copy(source, target, sems.at[len(copies)])
            copy.start()
            copies.append(copy)
            return copy

        arrivals[0] = [bring(w_home, w)]
        for step in range(heads // GROUP):
            cols = pl.ds(pl.multiple_of((base + step * GROUP) * dim, width), width)
            arrivals[step] = arrivals.get(step, []) + [
                bring(home.at[which, :, cols], x.at[which - 1, :, cols]) for which in (1, 2)
            ]
        for other in range(1, head_count // heads):
            head = lax.rem(base + other * heads, head_count)
            cols = pl.ds(pl.multiple_of(head * dim, heads * dim), heads * dim)
            for which in (1, 2):
                bring(home.at[which, :, cols], x.at[which - 1, :, cols])
        bring(home.at[0], xq.at[0])
        bring(code_home, codes)
        bring(gain_home, gain)
    elif merge:
        got_home, k_out, vt_out, s_out, sum_out, got = rest
        copies.append(pltpu.make_async_copy(got_home, got, sems.at[0]))
        copies[0].start()
    else:
        k_out, vt_out, s_out = rest[extra:]
    heads, dim = vt_out.shape[:2]
    base = base_of(place, where, heads)

    for step in range(heads // GROUP):
        for copy in arrivals.get(step, []):
            copy.wait()
    if merge:
        copies[0].wait()

    @pl.loop(0, heads // GROUP)
    def _(step):
        for unit in range(GROUP):
            head = step * GROUP + unit
            keys = convolve(x, 0, rim, w, 1, base + head, dim)
            k_out[:, lanes(head, dim)] = keys
            vt = convolve(x, 1, rim, w, 2, base + head, dim).T
            vt_out[head] = vt
            state = jnp.dot(vt, keys, preferred_element_type=jnp.float32)
            s_out[head] = state.astype(jnp.bfloat16)
            if merge:
                sum_out[head] = (state + got[head].astype(jnp.float32)).astype(jnp.bfloat16)

    if first:
        for copy in copies[2 * (heads // GROUP) + 1 :]:
            copy.wait()


def merge_kernel(*refs):
    count = refs[-1].shape[0]
    out, held, sems = refs[-4], refs[-3], refs[-1]
    copies = [pltpu.make_async_copy(refs[i], held.at[i], sems.at[i]) for i in range(count)]
    for copy in copies:
        copy.start()
    for copy in copies:
        copy.wait()
    total = held[0].astype(jnp.float32)
    for i in range(1, count):
        total = total + held[i].astype(jnp.float32)
    refs[-2][...] = total.astype(refs[-2].dtype)
    last = pltpu.make_async_copy(refs[-2], out, sems.at[0])
    last.start()
    last.wait()


def inner_weights(lam, block):
    rows = lam[0].shape[1]
    lane = lax.broadcasted_iota(jnp.int32, (8, rows), 1)
    sub = lax.broadcasted_iota(jnp.int32, (8, rows), 0)
    zero = jnp.zeros((8, rows), jnp.float32)
    near = zero
    differ = (lane & 7) ^ sub
    for level in range(1, 4):
        near = jnp.where((differ >> (level - 1)) == 1, lam[level], near)
    near = jnp.where(differ == 0, lam[0], near)
    near = jnp.where(sub <= (lane & 7), near, zero)
    group = (lane >> 3) & (block // 8 - 1)
    out = []
    for first in range(0, block // 8, 8):
        index = sub + first
        apart = index ^ group
        far = zero
        for level in range(4, block.bit_length()):
            far = jnp.where((apart >> (level - 4)) == 1, lam[level], far)
        far = jnp.where(index < group, far, zero)
        for i in range(8):
            wide = jnp.broadcast_to(far[i : i + 1, :], (8, rows))
            out.append(jnp.where(group == first + i, near, wide))
    return out


def pack_kernel(count, *refs):
    out, sems = refs[-2:]
    copies = [pltpu.make_async_copy(refs[i], out.at[i], sems.at[i]) for i in range(count)]
    for copy in copies:
        copy.start()
    for copy in copies:
        copy.wait()


def inside_kernel(where, place, x, rim, w, k_in, vt_in, codes, after, q_out, in_out):
    rows = x.shape[1]
    heads, dim = vt_in.shape[:2]
    base = base_of(place, where, heads)
    block, wide = min(128, rows), min(256, rows)
    bits = rows.bit_length() - 1

    @pl.loop(0, heads // GROUP)
    def _(step):
        for unit in range(GROUP):
            head = step * GROUP + unit
            cols = lanes(head, dim)
            queries = convolve(x, 0, rim, w, 0, base + head, dim)
            q_out[:, cols] = queries
            lam = [
                codes[level, pl.ds(base + head, 1), :].astype(jnp.float32) * 0.125
                for level in range(bits + 1)
            ]
            near = inner_weights(lam, block)
            for first in range(0, rows, wide):
                reach = first + wide
                scores = lax.dot_general(
                    k_in[0:reach, cols],
                    queries[first:reach],
                    NT,
                    preferred_element_type=jnp.float32,
                )
                columns = []
                for t0 in range(first, reach, block):
                    span = slice(t0 - first, t0 - first + block)
                    parts = []
                    for s0 in range(0, reach, block):
                        if s0 > t0:
                            parts.append(jnp.zeros((block, block), jnp.bfloat16))
                            continue
                        if s0 == t0:
                            weight = jnp.concatenate([n[:, t0 : t0 + block] for n in near], 0)
                        else:
                            weight = lam[(s0 ^ t0).bit_length()][:, t0 : t0 + block]
                        parts.append((scores[s0 : s0 + block, span] * weight).astype(jnp.bfloat16))
                    columns.append(jnp.concatenate(parts, 0))
                in_out[head, :, first:reach] = jnp.dot(
                    vt_in[head, :, 0:reach],
                    jnp.concatenate(columns, 1),
                    preferred_element_type=jnp.float32,
                )


def across_kernel(bits, inner, held, where, slots, place, q_in, in_in, codes, gain, *rest):
    states, out, token = rest[:bits], rest[bits + held], rest[bits + held + 1]
    fen, mixed, sems = rest[bits + held + 2 :]
    token[...] = jnp.zeros_like(token)
    heads, dim, rows = in_in.shape
    base = base_of(place, where, heads)
    copies = [
        pltpu.make_async_copy(
            states[bit] if slots[bit] is None else states[bit].at[slots[bit]],
            fen.at[:, bit * dim : (bit + 1) * dim, :],
            sems.at[bit],
        )
        for bit in range(bits)
    ]
    for copy in copies:
        copy.start()
    for copy in copies:
        copy.wait()
    scales = [((place[0] >> bit) & 1).astype(jnp.float32) * 0.125 for bit in range(bits)]
    wide = min(256, rows)

    @pl.loop(0, heads // GROUP)
    def _(step):
        for unit in range(GROUP):
            head = step * GROUP + unit
            cols = lanes(head, dim)
            lam = [
                codes[inner + bit, pl.ds(base + head, 1), :].astype(jnp.float32) * scales[bit]
                for bit in range(bits)
            ]
            for t0 in range(0, rows, wide):
                span = slice(t0, t0 + wide)
                parts = lax.dot_general(
                    fen[head], q_in[span, cols], NT, preferred_element_type=jnp.float32
                )
                total = in_in[head, :, span]
                for bit in range(bits):
                    total = total + lam[bit][:, span] * parts[bit * dim : (bit + 1) * dim]
                mean = jnp.sum(total * total, 0, keepdims=True) * (1.0 / dim)
                normed = total * lax.rsqrt(mean + 1e-06)
                mixed[span, cols] = (normed.T * gain[:, lanes(base + head, dim)]).astype(
                    jnp.bfloat16
                )

    width = heads * dim
    home = out.at[:, pl.ds(pl.multiple_of(base * dim, width), width)]
    last = pltpu.make_async_copy(mixed, home, sems.at[bits])
    last.start()
    last.wait()


def on_device(projected, conv_weight, level_codes, out_gain):
    taps = conv_weight.shape[1]
    rows, width = projected.shape[1:]
    levels, head_count = level_codes.shape[:2]
    dim = width // head_count
    tok_bits = rows.bit_length() - 1
    count = lax.axis_size("ctx")
    bits = count.bit_length() - 1
    index = lax.axis_index("ctx")
    quarter = head_count // 4
    bf16, f32 = jnp.bfloat16, jnp.float32

    def exchange(value, bit):
        return lax.ppermute(value, "ctx", [(i, i ^ (1 << bit)) for i in range(count)])

    rim = lax.ppermute(
        projected[:, rows - taps + 1 :, :], "ctx", [(i, i + 1) for i in range(count - 1)]
    )

    def kept(value):
        return pltpu.with_memory_space_constraint(value, VMEM)

    place = index.reshape(1).astype(jnp.int32)
    params = pltpu.CompilerParams(vmem_limit_bytes=ROOM)
    whole = pl.BlockSpec(memory_space=VMEM)
    scalars = pl.BlockSpec(memory_space=pltpu.SMEM)
    anywhere = pl.BlockSpec(memory_space=pl.ANY)
    state = jax.ShapeDtypeStruct((quarter, dim, dim), bf16)

    def key_value(where, source, weight, first=False, got=None, after=None):
        merge, extra = got is not None, 0 if after is None else 1
        made = [VMEM((rows, quarter * dim), bf16), VMEM((quarter, dim, rows), bf16), state]
        scratch, operands = [], [place, rim, weight, source]
        specs = [scalars, whole] + [anywhere if first else whole] * 2
        if first:
            gain = out_gain.reshape(1, width)
            operands[-2:] = [
                pltpu.with_memory_space_constraint(a, pltpu.HBM)
                for a in (weight, source, level_codes, gain)
            ]
            specs += [anywhere] * 2
            made += [VMEM((2, rows, width), bf16), VMEM((1, rows, width), bf16)]
            made += [VMEM(a.shape, a.dtype) for a in (level_codes, gain, weight)]
        if merge:
            operands.append(got)
            specs.append(anywhere)
            made.append(state)
            scratch.append(VMEM(state.shape, bf16))
        if extra:
            operands.append(after)
            specs.append(anywhere)
        return pl.pallas_call(
            functools.partial(kv_kernel, first, merge, extra, where),
            in_specs=specs,
            out_specs=[whole] * len(made),
            out_shape=made,
            scratch_shapes=scratch + [pltpu.SemaphoreType.DMA((2 * quarter // GROUP + 10,))],
            compiler_params=params,
            name="key_value",
        )(*operands)

    def merged(values, after):
        return pl.pallas_call(
            merge_kernel,
            in_specs=[anywhere] * (len(values) + len(after)),
            out_specs=anywhere,
            out_shape=state,
            scratch_shapes=[
                VMEM((len(values), *state.shape), bf16),
                VMEM(state.shape, bf16),
                pltpu.SemaphoreType.DMA((len(values),)),
            ],
            compiler_params=params,
            name="merge",
        )(*values, *after)

    def packed(values, after):
        shape = (len(values), *state.shape)
        return pl.pallas_call(
            functools.partial(pack_kernel, len(values)),
            in_specs=[anywhere] * (len(values) + len(after)),
            out_specs=anywhere,
            out_shape=jax.ShapeDtypeStruct(shape, bf16),
            scratch_shapes=[pltpu.SemaphoreType.DMA((len(values),))],
            compiler_params=params,
            name="pack",
        )(*values, *after)

    def inside(where, after):
        return pl.pallas_call(
            functools.partial(inside_kernel, where),
            in_specs=[scalars] + [whole] * 6 + [anywhere],
            out_specs=[whole] * 2,
            out_shape=[VMEM((rows, quarter * dim), bf16), VMEM((quarter, dim, rows), f32)],
            compiler_params=params,
            name="inside",
        )(
            place, raw, rim, weight, kept(keys[where]), kept(values[where]), codes, after
        )

    def across(where, local, states, out):
        held = [] if out is None else [out]
        queries, inner = local
        states, slots = zip(*(a if isinstance(a, tuple) else (a, None) for a in states))
        return pl.pallas_call(
            functools.partial(across_kernel, bits, tok_bits + 1, len(held), where, slots),
            in_specs=[scalars] + [whole] * 4 + [anywhere] * (bits + len(held)),
            out_specs=[anywhere, whole],
            out_shape=[jax.ShapeDtypeStruct((rows, width), bf16), VMEM((8, 128), f32)],
            input_output_aliases={5 + bits: 0} if held else {},
            scratch_shapes=[
                VMEM((quarter, bits * dim, dim), bf16),
                VMEM((rows, quarter * dim), bf16),
                pltpu.SemaphoreType.DMA((bits + 1,)),
            ],
            compiler_params=params,
            name="across",
        )(place, kept(queries), kept(inner), codes, gain, *states, *held)

    near, far, other_near, other_far = (0, 0), (0, 1), (1, 0), (1, 1)
    keys, values, local = {}, {}, {}
    keys[other_far], values[other_far], sent, source, raw, codes, gain, weight = key_value(
        other_far, projected, conv_weight, first=True
    )
    source, raw, codes, gain, weight = map(kept, (source, raw, codes, gain, weight))
    got_far = exchange(sent, 0)
    keys[far], values[far], state_far, total_far = key_value(far, source, weight, got=got_far)
    near1 = exchange(total_far, 1)
    keys[other_near], values[other_near], sent = key_value(
        other_near, source, weight, after=total_far
    )
    got_near = exchange(sent, 0)
    keys[near], values[near], state_near, total_near = key_value(
        near, source, weight, got=got_near
    )
    far1 = exchange(total_near, 1)
    nears, fars = [got_near, near1], [got_far, far1]
    running = merged([total_near, near1], [])
    waiting = [near, far, other_near, other_far]

    def work(where, after):
        waiting.remove(where)
        local[where] = inside(where, after)
        return local[where][1]

    for bit in range(2, bits):
        ones = (1 << bit) - 4
        pieces = []
        for low in reversed(range(1 << (bit - 2))):
            pairs = [
                (i, (i & ~ones) | (low << 2) | (1 << bit))
                for i in range(count)
                if i & ones == ones and not i >> bit & 1
            ]
            pieces.append(lax.ppermute(running, "ctx", pairs))
        after = []
        for _ in range(bit - 1):
            if len(waiting) > 1:
                after.append(work(waiting[0], after[-1] if after else running))
        got = merged(pieces, after) if len(pieces) > 1 else pieces[0]
        if bit + 1 < bits:
            running = merged([running, got], after)
        nears.append(got)
        fars.append(exchange(got, 1))
        if bit == 2:
            early = exchange(packed([state_near, near1, state_far, far1], [running]), 0)
    late = exchange(packed(nears[2:] + fars[2:-1], []), 0)
    after = [work(where, nears[-1]) for where in list(waiting)]
    out, token = across(near, local[near], nears, None)
    last = merged(fars[-1:], after + [token])
    later = bits - 2
    other_nears = [(early, 0), (early, 1)] + [(late, i) for i in range(later)]
    other_fars = [(early, 2), (early, 3)] + [(late, later + i) for i in range(later - 1)]
    other_fars.append(exchange(last, 0))
    out, _ = across(other_near, local[other_near], other_nears, out)
    out, _ = across(far, local[far], fars[:-1] + [last], out)
    return across(other_far, local[other_far], other_fars, out)[0]


def solution(mesh):
    placed = (P(None, ("groups", "ctx"), None), P(), P(None, None, ("groups", "ctx")), P())
    return jax.shard_map(
        on_device, mesh=mesh, in_specs=placed, out_specs=P(("groups", "ctx"), None), check_vma=False
    )
```

time: 422 us -> 71.7 us (0.17)
  the two profiles are of different devices: /device:TPU:13 before, /device:TPU:27 now
where the time goes in v2:
time: 71.7 us; the launch traced here: 71.5 us
  Pallas kernels  38.8 us (54%)
  starting transfers between devices  17.4 us (24%)
  waiting for transfers between devices  14 us (20%)
  local copies, waits for them, and re-layouts  0.98 us (1%)
    pallas_call x4, Pallas kernels, inside(): pl.pallas_call(functools.partial(inside_kernel, where), in_specs=[scalars...  13.2 us
    pallas_call x4, Pallas kernels, across(): pl.pallas_call(functools.partial(across_kernel, bits, tok_bits + 1, len(h...  12.7 us
    pallas_call x4, Pallas kernels, key_value(): pl.pallas_call(functools.partial(kv_kernel, first, merge, extra, where),...  12.2 us
    ppermute x9, starting transfers between devices, exchange(): return lax.ppermute(value, 'ctx', [(i, i ^ 1 << bit) for i in range(count)])  10.2 us
    ppermute x9, waiting for transfers between devices, exchange(): return lax.ppermute(value, 'ctx', [(i, i ^ 1 << bit) for i in range(count)])  7.74 us
    ppermute x3, waiting for transfers between devices, on_device(): pieces.append(lax.ppermute(running, 'ctx', pairs))  4.66 us
    ppermute x1, starting transfers between devices, on_device(): lax.ppermute(projected[:, rows - taps + 1:, :], 'ctx', [(i, i + 1) for i...  3.71 us
    ppermute x3, starting transfers between devices, on_device(): pieces.append(lax.ppermute(running, 'ctx', pairs))  3.44 us
  transfers between devices with their start and end apart: 13, of which 7 were waited for; matrix products, arithmetic and copies ran while one was open for 0% of the time, Pallas kernels for 36%

profile of v2, /device:TPU:27, one launch (start us, length us, event | category | flops | bytes accessed | tf_op | source)
XLA Modules:
  0.0 71.5 jit_solution(14830625528374977529)
XLA Ops:
  0.0 1.0 %slice.3 = bf16[3,3,4096]{2,1,0:T(4,128)(2,1)S(1)} slice(bf16[3,512,4096]{2,1,0:T(8,128)(2,1)} %x.1), slice={[0:3], [509:512], [0:4096]} | slice | bytes 147456 | tf_op jit(solution)/shard_map/slice | solution.py:279
  1.0 3.7 %collective-permute-start = (bf16[3,3,4096]{2,1,0:T(4,128)(2,1)S(1)}, bf16[3,3,4096]{2,1,0:T(4,128)(2,1)S(1)}, u32[]{:S(2)}, u32[]{:S(2)}) collective-permute-start(bf16[3,3,4096]{2,1,0:T(4,128)(2,1)S(1)} %slice.3), channel_id=1, source_target_pairs={{0,1},{1,2},{2,3},{3,4},{4,5},{5,6},{6,7},{7,8},{8,9},{9,10},{10,1... | collective-permute-start | bytes 221192 | tf_op jit(solution)/shard_map/ppermute | solution.py:278
  4.7 1.6 %collective-permute-done.rim = bf16[3,3,4096]{2,1,0:T(4,128)(2,1)S(1)} collective-permute-done((bf16[3,3,4096]{2,1,0:T(4,128)(2,1)S(1)}, bf16[3,3,4096]{2,1,0:T(4,128)(2,1)S(1)}, u32[]{:S(2)}, u32[]{:S(2)}) %collective-permute-start) | collective-permute-done | bytes 73760 | tf_op jit(solution)/shard_map/ppermute | solution.py:278
  6.3 5.1 %key_value.4 = (bf16[512,1024]{1,0:T(8,128)(2,1)S(1)}, bf16[8,128,512]{2,1,0:T(8,128)(2,1)S(1)}, bf16[8,128,128]{2,1,0:T(8,128)(2,1)S(1)}, bf16[2,512,4096]{2,1,...) custom-call(s32[1]{0:T(128)} %bitcast.place, ...), custom_call_target="tpu_custom_call" | custom-call | tf_op jit(solution)/shard_map/key_value/pallas_call | solution.py:314
  11.4 2.2 %collective-permute-start.1 = (bf16[8,128,128]{2,1,0:T(8,128)(2,1)S(1)}, bf16[8,128,128]{2,1,0:T(8,128)(2,1)S(1)}, u32[]{:S(2)}, u32[]{:S(2)}) collective-permute-start(bf16[8,128,128]{2,1,0:T(8,128)(2,1)S(1)} %get-tuple-element.43), channel_id=1, source_target_pairs={{0,1},{1,0},{2,3},{3,2},{4,5},{5,4},{6,7},{7,6},{8,9},{9,8},{10,11... | collective-permute-start | bytes 786440 | tf_op jit(solution)/shard_map/ppermute | solution.py:276
  13.7 1.2 %collective-permute-done.1.rest_0_ = bf16[8,128,128]{2,1,0:T(8,128)(2,1)S(1)} collective-permute-done((bf16[8,128,128]{2,1,0:T(8,128)(2,1)S(1)}, bf16[8,128,128]{2,1,0:T(8,128)(2,1)S(1)}, u32[]{:S(2)}, u32[]{:S(2)}) %collective-permute-start.1) | collective-permute-done | bytes 262176 | tf_op jit(solution)/shard_map/ppermute | solution.py:276
  14.8 2.4 %key_value.5 = (bf16[512,1024]{1,0:T(8,128)(2,1)S(1)}, bf16[8,128,512]{2,1,0:T(8,128)(2,1)S(1)}, bf16[8,128,128]{2,1,0:T(8,128)(2,1)S(1)}, bf16[8,128,128]{2,1,0:T(8,128)(2,1)S(1)}) custom-call(s32[1]{0:T(128)} %bitcast.place, bf16[3,3,4096]{2,1,0:T(4,128)(2,1)S(1)} %collective-permute-done.rim, f32[3,4,4096]{2,1,0:T(4,128)S(1)} %get-tuple-element.38.w, ...), custom_call_target="tpu_custom_call" | custom-call | tf_op jit(solution)/shard_map/key_value/pallas_call | solution.py:314
  17.2 2.3 %key_value.6 = (bf16[512,1024]{1,0:T(8,128)(2,1)S(1)}, bf16[8,128,512]{2,1,0:T(8,128)(2,1)S(1)}, bf16[8,128,128]{2,1,0:T(8,128)(2,1)S(1)}) custom-call(s32[1]{0:T(128)} %bitcast.place, bf16[3,3,4096]{2,1,0:T(4,128)(2,1)S(1)} %collective-permute-done.rim, f32[3,4,4096]{2,1,0:T(4,128)S(1)} %get-tuple-element.38.w, ...), custom_call_target="tpu_custom_call" | custom-call | tf_op jit(solution)/shard_map/key_value/pallas_call | solution.py:314
  19.6 0.4 collective-permute-start.2
  20.0 0.3 collective-permute-start.3
  20.3 0.8 %collective-permute-done.2.rest_0_ = bf16[8,128,128]{2,1,0:T(8,128)(2,1)S(1)} collective-permute-done((bf16[8,128,128]{2,1,0:T(8,128)(2,1)S(1)}, bf16[8,128,128]{2,1,0:T(8,128)(2,1)S(1)}, u32[]{:S(2)}, u32[]{:S(2)}) %collective-permute-start.2) | collective-permute-done | bytes 262176 | tf_op jit(solution)/shard_map/ppermute | solution.py:276
  21.2 2.4 %key_value.7 = (bf16[512,1024]{1,0:T(8,128)(2,1)S(1)}, bf16[8,128,512]{2,1,0:T(8,128)(2,1)S(1)}, bf16[8,128,128]{2,1,0:T(8,128)(2,1)S(1)}, bf16[8,128,128]{2,1,0:T(8,128)(2,1)S(1)}) custom-call(s32[1]{0:T(128)} %bitcast.place, bf16[3,3,4096]{2,1,0:T(4,128)(2,1)S(1)} %collective-permute-done.rim, f32[3,4,4096]{2,1,0:T(4,128)S(1)} %get-tuple-element.38.w, ...), custom_call_target="tpu_custom_call" | custom-call | tf_op jit(solution)/shard_map/key_value/pallas_call | solution.py:314
  23.6 4.2 %collective-permute-done.3.refs_1_.rest_1_ = bf16[8,128,128]{2,1,0:T(8,128)(2,1)S(1)} collective-permute-done((bf16[8,128,128]{2,1,0:T(8,128)(2,1)S(1)}, bf16[8,128,128]{2,1,0:T(8,128)(2,1)S(1)}, u32[]{:S(2)}, u32[]{:S(2)}) %collective-permute-start.3) | collective-permute-done | bytes 262176 | tf_op jit(solution)/shard_map/ppermute | solution.py:276
  27.8 0.1 merge.4.after.refs_0_
  27.9 1.5 %collective-permute-start.4 = (bf16[8,128,128]{2,1,0:T(8,128)(2,1)S(1)}, bf16[8,128,128]{2,1,0:T(8,128)(2,1)S(1)}, u32[]{:S(2)}, u32[]{:S(2)}) collective-permute-start(bf16[8,128,128]{2,1,0:T(8,128)(2,1)S(1)} %merge.4.after.refs_0_), channel_id=1, source_target_pairs={{0,4},{1,5},{2,6},{3,7},{8,12},{9,13},{10,14},{11,15},{16,20},{17,... | collective-permute-start | bytes 786440 | tf_op jit(solution)/shard_map/ppermute | solution.py:417
  29.4 0.4 collective-permute-start.7
  29.8 3.3 %inside.4 = (bf16[512,1024]{1,0:T(8,128)(2,1)S(1)}, f32[8,128,512]{2,1,0:T(8,128)S(1)}) custom-call(s32[1]{0:T(128)} %bitcast.place, bf16[1,512,4096]{2,1,0:T(8,128)(2,1)S(1)} %get-tuple-element.37.x, bf16[3,3,4096]{2,1,0:T(4,128)(2,1)S(1)} %collective-permute-done.rim, f32[3,4,4096]{2,1,0:T(4,128)S(1)} %get-tuple-element.38.w, ...), custom_call_target="tpu_custom_call" | custom-call | tf_op jit(solution)/shard_map/inside/pallas_call | solution.py:352
  33.1 3.6 %collective-permute-done.4.refs_1_.refs_0_.rest_2_ = bf16[8,128,128]{2,1,0:T(8,128)(2,1)S(1)} collective-permute-done((bf16[8,128,128]{2,1,0:T(8,128)(2,1)S(1)}, bf16[8,128,128]{2,1,0:T(8,128)(2,1)S(1)}, u32[]{:S(2)}, u32[]{:S(2)}) %collective-permute-start.4) | collective-permute-done | bytes 262176 | tf_op jit(solution)/shard_map/ppermute | solution.py:417
  36.7 0.1 merge.5.after.refs_4_
  36.8 0.7 collective-permute-start.6
  37.5 1.3 %collective-permute-start.5 = (bf16[8,128,128]{2,1,0:T(8,128)(2,1)S(1)}, bf16[8,128,128]{2,1,0:T(8,128)(2,1)S(1)}, u32[]{:S(2)}, u32[]{:S(2)}) collective-permute-start(bf16[8,128,128]{2,1,0:T(8,128)(2,1)S(1)} %merge.5.after.refs_4_), channel_id=1, source_target_pairs={{4,12},{5,13},{6,14},{7,15},{20,28},{21,29},{22,30},{23,31}} | collective-permute-start | bytes 786440 | tf_op jit(solution)/shard_map/ppermute | solution.py:417
  38.8 0.4 collective-permute-start.9
  39.2 0.0 collective-permute-done.7.refs_3_.rest_1_
  39.2 0.1 pack.2
  39.3 2.2 %collective-permute-start.8 = (bf16[4,8,128,128]{3,2,1,0:T(8,128)(2,1)S(1)}, bf16[4,8,128,128]{3,2,1,0:T(8,128)(2,1)S(1)}, u32[]{:S(2)}, u32[]{:S(2)}) collective-permute-start(bf16[4,8,128,128]{3,2,1,0:T(8,128)(2,1)S(1)} %pack.2), channel_id=1, source_target_pairs={{0,1},{1,0},{2,3},{3,2},{4,5},{5,4},{6,7},{7,6},{8,9},{9,8},{10,11... | collective-permute-start | bytes 3145736 | tf_op jit(solution)/shard_map/ppermute | solution.py:276
  41.5 3.3 %inside.5 = (bf16[512,1024]{1,0:T(8,128)(2,1)S(1)}, f32[8,128,512]{2,1,0:T(8,128)S(1)}) custom-call(s32[1]{0:T(128)} %bitcast.place, bf16[1,512,4096]{2,1,0:T(8,128)(2,1)S(1)} %get-tuple-element.37.x, bf16[3,3,4096]{2,1,0:T(4,128)(2,1)S(1)} %collective-permute-done.rim, f32[3,4,4096]{2,1,0:T(4,128)S(1)} %get-tuple-element.38.w, ...), custom_call_target="tpu_custom_call" | custom-call | tf_op jit(solution)/shard_map/inside/pallas_call | solution.py:352
  44.9 3.3 %inside.6 = (bf16[512,1024]{1,0:T(8,128)(2,1)S(1)}, f32[8,128,512]{2,1,0:T(8,128)S(1)}) custom-call(s32[1]{0:T(128)} %bitcast.place, bf16[1,512,4096]{2,1,0:T(8,128)(2,1)S(1)} %get-tuple-element.37.x, bf16[3,3,4096]{2,1,0:T(4,128)(2,1)S(1)} %collective-permute-done.rim, f32[3,4,4096]{2,1,0:T(4,128)S(1)} %get-tuple-element.38.w, ...), custom_call_target="tpu_custom_call" | custom-call | tf_op jit(solution)/shard_map/inside/pallas_call | solution.py:352
  48.2 0.0 collective-permute-done.6.refs_1_
  48.2 1.1 %collective-permute-done.5.refs_0_ = bf16[8,128,128]{2,1,0:T(8,128)(2,1)S(1)} collective-permute-done((bf16[8,128,128]{2,1,0:T(8,128)(2,1)S(1)}, bf16[8,128,128]{2,1,0:T(8,128)(2,1)S(1)}, u32[]{:S(2)}, u32[]{:S(2)}) %collective-permute-start.5) | collective-permute-done | bytes 262176 | tf_op jit(solution)/shard_map/ppermute | solution.py:417
  49.3 0.1 merge.6.after.refs_1_.rest_3_
  49.4 0.0 collective-permute-done.9.refs_2_.rest_2_
  49.4 0.1 pack.3
  49.5 2.8 %collective-permute-start.10 = (bf16[3,8,128,128]{3,2,1,0:T(8,128)(2,1)S(1)}, bf16[3,8,128,128]{3,2,1,0:T(8,128)(2,1)S(1)}, u32[]{:S(2)}, u32[]{:S(2)}) collective-permute-start(bf16[3,8,128,128]{3,2,1,0:T(8,128)(2,1)S(1)} %pack.3), channel_id=1, source_target_pairs={{0,1},{1,0},{2,3},{3,2},{4,5},{5,4},{6,7},{7,6},{8,9},{9,8},{10,11... | collective-permute-start | bytes 2359304 | tf_op jit(solution)/shard_map/ppermute | solution.py:276
  52.4 0.4 collective-permute-start.11
  52.8 3.3 %inside.7 = (bf16[512,1024]{1,0:T(8,128)(2,1)S(1)}, f32[8,128,512]{2,1,0:T(8,128)S(1)}) custom-call(s32[1]{0:T(128)} %bitcast.place, bf16[1,512,4096]{2,1,0:T(8,128)(2,1)S(1)} %get-tuple-element.37.x, bf16[3,3,4096]{2,1,0:T(4,128)(2,1)S(1)} %collective-permute-done.rim, f32[3,4,4096]{2,1,0:T(4,128)S(1)} %get-tuple-element.38.w, ...), custom_call_target="tpu_custom_call" | custom-call | tf_op jit(solution)/shard_map/inside/pallas_call | solution.py:352
  56.1 2.6 %across.4 = (bf16[512,4096]{1,0:T(8,128)(2,1)}, f32[8,128]{1,0:T(8,128)S(1)}) custom-call(s32[1]{0:T(128)} %bitcast.place, bf16[512,1024]{1,0:T(8,128)(2,1)S(1)} %get-tuple-element.61.q_in, f32[8,128,512]{2,1,0:T(8,128)S(1)} %get-tuple-element.49.refs_2_.in_in, s32[14,32,512]{2,1,0:T(8,128)S(1)} %get-tuple-element.41.codes, ...), custom_call_target="tpu_custom_call" | custom-call | tf_op jit(solution)/shard_map/across/pallas_call | solution.py:367
  58.7 1.5 %collective-permute-done.11.refs_0_ = bf16[8,128,128]{2,1,0:T(8,128)(2,1)S(1)} collective-permute-done((bf16[8,128,128]{2,1,0:T(8,128)(2,1)S(1)}, bf16[8,128,128]{2,1,0:T(8,128)(2,1)S(1)}, u32[]{:S(2)}, u32[]{:S(2)}) %collective-permute-start.11) | collective-permute-done | bytes 262176 | tf_op jit(solution)/shard_map/ppermute | solution.py:276
  60.2 0.1 merge.7.rest_3_
  60.4 0.9 %collective-permute-start.12 = (bf16[8,128,128]{2,1,0:T(8,128)(2,1)S(1)}, bf16[8,128,128]{2,1,0:T(8,128)(2,1)S(1)}, u32[]{:S(2)}, u32[]{:S(2)}) collective-permute-start(bf16[8,128,128]{2,1,0:T(8,128)(2,1)S(1)} %merge.7.rest_3_), channel_id=1, source_target_pairs={{0,1},{1,0},{2,3},{3,2},{4,5},{5,4},{6,7},{7,6},{8,9},{9,8},{10,11... | collective-permute-start | bytes 786440 | tf_op jit(solution)/shard_map/ppermute | solution.py:276
  61.3 0.0 collective-permute-done.10.rest_2_.rest_3_
  61.3 0.0 collective-permute-done.8.rest_0_.rest_1_
  61.3 3.5 %across.5 = (bf16[512,4096]{1,0:T(8,128)(2,1)}, f32[8,128]{1,0:T(8,128)}) custom-call(s32[1]{0:T(128)} %bitcast.place, bf16[512,1024]{1,0:T(8,128)(2,1)S(1)} %get-tuple-element.64.q_in, f32[8,128,512]{2,1,0:T(8,128)S(1)} %get-tuple-element.55.refs_3_.in_in, s32[14,32,512]{2,1,0:T(8,128)S(1)} %get-tuple-element.41.codes, ...), custom_call_target="tpu_custom_call", output_to_operand_aliasing={{0}: (9, {})} | custom-call | tf_op jit(solution)/shard_map/across/pallas_call | solution.py:367
  64.8 3.3 %across.6 = (bf16[512,4096]{1,0:T(8,128)(2,1)}, f32[8,128]{1,0:T(8,128)}) custom-call(s32[1]{0:T(128)} %bitcast.place, bf16[512,1024]{1,0:T(8,128)(2,1)S(1)} %get-tuple-element.63.q_in, f32[8,128,512]{2,1,0:T(8,128)S(1)} %get-tuple-element.52.after.refs_2_.in_in, s32[14,32,512]{2,1,0:T(8,128)S(1)} %get-tuple-element.41.codes, ...), custom_call_target="tpu_custom_call", output_to_operand_aliasing={{0}: (9, {})} | custom-call | tf_op jit(solution)/shard_map/across/pallas_call | solution.py:367
  68.1 0.0 collective-permute-done.12.rest_3_
  68.1 3.3 %across.7 = (bf16[512,4096]{1,0:T(8,128)(2,1)}, f32[8,128]{1,0:T(8,128)}) custom-call(s32[1]{0:T(128)} %bitcast.place, bf16[512,1024]{1,0:T(8,128)(2,1)S(1)} %get-tuple-element.56.q_in, f32[8,128,512]{2,1,0:T(8,128)S(1)} %get-tuple-element.57.refs_1_.in_in, s32[14,32,512]{2,1,0:T(8,128)S(1)} %get-tuple-element.41.codes, ...), custom_call_target="tpu_custom_call", output_to_operand_aliasing={{0}: (9, {})} | custom-call | tf_op jit(solution)/shard_map/across/pallas_call | solution.py:367
Async XLA Ops:
  1.0 5.3 %collective-permute-start = (bf16[3,3,4096]{2,1,0:T(4,128)(2,1)S(1)}, bf16[3,3,4096]{2,1,0:T(4,128)(2,1)S(1)}, u32[]{:S(2)}, u32[]{:S(2)}) collective-permute-start(bf16[3,3,4096]{2,1,0:T(4,128)(2,1)S(1)} %slice.3), channel_id=1, source_target_pairs={{0,1},{1,2},{2,3},{3,4},{4,5},{5,6},{6,7},{7,8},{8,9},{9,10},{10,1... | collective-permute-start | bytes 221192 | tf_op jit(solution)/shard_map/ppermute | solution.py:278
  11.4 3.4 %collective-permute-start.1 = (bf16[8,128,128]{2,1,0:T(8,128)(2,1)S(1)}, bf16[8,128,128]{2,1,0:T(8,128)(2,1)S(1)}, u32[]{:S(2)}, u32[]{:S(2)}) collective-permute-start(bf16[8,128,128]{2,1,0:T(8,128)(2,1)S(1)} %get-tuple-element.43), channel_id=1, source_target_pairs={{0,1},{1,0},{2,3},{3,2},{4,5},{5,4},{6,7},{7,6},{8,9},{9,8},{10,11... | collective-permute-start | bytes 786440 | tf_op jit(solution)/shard_map/ppermute | solution.py:276
  19.6 1.6 %collective-permute-start.2 = (bf16[8,128,128]{2,1,0:T(8,128)(2,1)S(1)}, bf16[8,128,128]{2,1,0:T(8,128)(2,1)S(1)}, u32[]{:S(2)}, u32[]{:S(2)}) collective-permute-start(bf16[8,128,128]{2,1,0:T(8,128)(2,1)S(1)} %get-tuple-element.45), channel_id=1, source_target_pairs={{0,1},{1,0},{2,3},{3,2},{4,5},{5,4},{6,7},{7,6},{8,9},{9,8},{10,11... | collective-permute-start | bytes 786440 | tf_op jit(solution)/shard_map/ppermute | solution.py:276
  20.0 7.8 %collective-permute-start.3 = (bf16[8,128,128]{2,1,0:T(8,128)(2,1)S(1)}, bf16[8,128,128]{2,1,0:T(8,128)(2,1)S(1)}, u32[]{:S(2)}, u32[]{:S(2)}) collective-permute-start(bf16[8,128,128]{2,1,0:T(8,128)(2,1)S(1)} %get-tuple-element.44.rest_0_), channel_id=1, source_target_pairs={{0,2},{1,3},{2,0},{3,1},{4,6},{5,7},{6,4},{7,5},{8,10},{9,11},{10,... | collective-permute-start | bytes 786440 | tf_op jit(solution)/shard_map/ppermute | solution.py:276
  27.9 8.8 %collective-permute-start.4 = (bf16[8,128,128]{2,1,0:T(8,128)(2,1)S(1)}, bf16[8,128,128]{2,1,0:T(8,128)(2,1)S(1)}, u32[]{:S(2)}, u32[]{:S(2)}) collective-permute-start(bf16[8,128,128]{2,1,0:T(8,128)(2,1)S(1)} %merge.4.after.refs_0_), channel_id=1, source_target_pairs={{0,4},{1,5},{2,6},{3,7},{8,12},{9,13},{10,14},{11,15},{16,20},{17,... | collective-permute-start | bytes 786440 | tf_op jit(solution)/shard_map/ppermute | solution.py:417
  29.4 9.8 %collective-permute-start.7 = (bf16[8,128,128]{2,1,0:T(8,128)(2,1)S(1)}, bf16[8,128,128]{2,1,0:T(8,128)(2,1)S(1)}, u32[]{:S(2)}, u32[]{:S(2)}) collective-permute-start(bf16[8,128,128]{2,1,0:T(8,128)(2,1)S(1)} %get-tuple-element.46.refs_0_), channel_id=1, source_target_pairs={{0,2},{1,3},{2,0},{3,1},{4,6},{5,7},{6,4},{7,5},{8,10},{9,11},{10,... | collective-permute-start | bytes 786440 | tf_op jit(solution)/shard_map/ppermute | solution.py:276
  36.8 11.3 %collective-permute-start.6 = (bf16[8,128,128]{2,1,0:T(8,128)(2,1)S(1)}, bf16[8,128,128]{2,1,0:T(8,128)(2,1)S(1)}, u32[]{:S(2)}, u32[]{:S(2)}) collective-permute-start(bf16[8,128,128]{2,1,0:T(8,128)(2,1)S(1)} %merge.5.after.refs_4_), channel_id=1, source_target_pairs={{4,8},{5,9},{6,10},{7,11},{20,24},{21,25},{22,26},{23,27}} | collective-permute-start | bytes 786440 | tf_op jit(solution)/shard_map/ppermute | solution.py:417
  37.5 11.7 %collective-permute-start.5 = (bf16[8,128,128]{2,1,0:T(8,128)(2,1)S(1)}, bf16[8,128,128]{2,1,0:T(8,128)(2,1)S(1)}, u32[]{:S(2)}, u32[]{:S(2)}) collective-permute-start(bf16[8,128,128]{2,1,0:T(8,128)(2,1)S(1)} %merge.5.after.refs_4_), channel_id=1, source_target_pairs={{4,12},{5,13},{6,14},{7,15},{20,28},{21,29},{22,30},{23,31}} | collective-permute-start | bytes 786440 | tf_op jit(solution)/shard_map/ppermute | solution.py:417
  38.8 10.6 %collective-permute-start.9 = (bf16[8,128,128]{2,1,0:T(8,128)(2,1)S(1)}, bf16[8,128,128]{2,1,0:T(8,128)(2,1)S(1)}, u32[]{:S(2)}, u32[]{:S(2)}) collective-permute-start(bf16[8,128,128]{2,1,0:T(8,128)(2,1)S(1)} %collective-permute-done.4.refs_1_.refs_0_.rest_2_), channel_id=1, source_target_pairs={{0,2},{1,3},{2,0},{3,1},{4,6},{5,7},{6,4},{7,5},{8,10},{9,11},{10,... | collective-permute-start | bytes 786440 | tf_op jit(solution)/shard_map/ppermute | solution.py:276
  39.3 21.9 %collective-permute-start.8 = (bf16[4,8,128,128]{3,2,1,0:T(8,128)(2,1)S(1)}, bf16[4,8,128,128]{3,2,1,0:T(8,128)(2,1)S(1)}, u32[]{:S(2)}, u32[]{:S(2)}) collective-permute-start(bf16[4,8,128,128]{3,2,1,0:T(8,128)(2,1)S(1)} %pack.2), channel_id=1, source_target_pairs={{0,1},{1,0},{2,3},{3,2},{4,5},{5,4},{6,7},{7,6},{8,9},{9,8},{10,11... | collective-permute-start | bytes 3145736 | tf_op jit(solution)/shard_map/ppermute | solution.py:276
  49.5 11.8 %collective-permute-start.10 = (bf16[3,8,128,128]{3,2,1,0:T(8,128)(2,1)S(1)}, bf16[3,8,128,128]{3,2,1,0:T(8,128)(2,1)S(1)}, u32[]{:S(2)}, u32[]{:S(2)}) collective-permute-start(bf16[3,8,128,128]{3,2,1,0:T(8,128)(2,1)S(1)} %pack.3), channel_id=1, source_target_pairs={{0,1},{1,0},{2,3},{3,2},{4,5},{5,4},{6,7},{7,6},{8,9},{9,8},{10,11... | collective-permute-start | bytes 2359304 | tf_op jit(solution)/shard_map/ppermute | solution.py:276
  52.4 7.9 %collective-permute-start.11 = (bf16[8,128,128]{2,1,0:T(8,128)(2,1)S(1)}, bf16[8,128,128]{2,1,0:T(8,128)(2,1)S(1)}, u32[]{:S(2)}, u32[]{:S(2)}) collective-permute-start(bf16[8,128,128]{2,1,0:T(8,128)(2,1)S(1)} %merge.6.after.refs_1_.rest_3_), channel_id=1, source_target_pairs={{0,2},{1,3},{2,0},{3,1},{4,6},{5,7},{6,4},{7,5},{8,10},{9,11},{10,... | collective-permute-start | bytes 786440 | tf_op jit(solution)/shard_map/ppermute | solution.py:276
  60.4 7.7 %collective-permute-start.12 = (bf16[8,128,128]{2,1,0:T(8,128)(2,1)S(1)}, bf16[8,128,128]{2,1,0:T(8,128)(2,1)S(1)}, u32[]{:S(2)}, u32[]{:S(2)}) collective-permute-start(bf16[8,128,128]{2,1,0:T(8,128)(2,1)S(1)} %merge.7.rest_3_), channel_id=1, source_target_pairs={{0,1},{1,0},{2,3},{3,2},{4,5},{5,4},{6,7},{7,6},{8,9},{9,8},{10,11... | collective-permute-start | bytes 786440 | tf_op jit(solution)/shard_map/ppermute | solution.py:276

commit v3 on v2

--- a/solution.py
+++ b/solution.py
@@ -22,12 +22,18 @@
     return (((index & 1) ^ where[0]) * 2 + (((index >> 1) & 1) ^ where[1])) * heads
 
 
-def convolve(x, at, rim, w, which, head, dim, step=128):
+def before_span(place, even, odd, which, cols):
+    index = place[0]
+    rows = jnp.where((index & 1) == 1, odd[which, :, cols], even[which, :, cols])
+    return jnp.where(index == 0, 0.0, rows.astype(jnp.float32))
+
+
+def convolve(x, at, place, even, odd, w, which, head, dim, step=128):
     rows, taps = x.shape[1], w.shape[1]
     cols = lanes(head, dim)
     w_rows = [w[which, tap : tap + 1, cols] for tap in range(taps)]
     before = jnp.concatenate(
-        [jnp.zeros((9 - taps, dim), jnp.float32), rim[which, :, cols].astype(jnp.float32)], 0
+        [jnp.zeros((9 - taps, dim), jnp.float32), before_span(place, even, odd, which, cols)], 0
     )
     out = []
     for row in range(0, rows, step):
@@ -44,69 +50,47 @@
     return jnp.concatenate(out, 0)
 
 
-def kv_kernel(first, merge, extra, where, place, rim, w, x, *rest):
-    rest, sems = rest[:-1], rest[-1]
-    copies, arrivals = [], {}
-    if first:
-        code_home, gain_home, *rest = rest
-        k_out, vt_out, s_out, x_in, xq, codes, gain, w_in = rest
-        home, x, w_home, w = x, x_in, w, w_in
-        heads, dim = vt_out.shape[:2]
-        base = base_of(place, where, heads)
-        head_count = x.shape[2] // dim
-        width = GROUP * dim
-
-        def bring(source, target):
-            copy = pltpu.make_async_copy(source, target, sems.at[len(copies)])
-            copy.start()
-            copies.append(copy)
-            return copy
-
-        arrivals[0] = [bring(w_home, w)]
-        for step in range(heads // GROUP):
-            cols = pl.ds(pl.multiple_of((base + step * GROUP) * dim, width), width)
-            arrivals[step] = arrivals.get(step, []) + [
-                bring(home.at[which, :, cols], x.at[which - 1, :, cols]) for which in (1, 2)
-            ]
-        for other in range(1, head_count // heads):
-            head = lax.rem(base + other * heads, head_count)
-            cols = pl.ds(pl.multiple_of(head * dim, heads * dim), heads * dim)
-            for which in (1, 2):
-                bring(home.at[which, :, cols], x.at[which - 1, :, cols])
-        bring(home.at[0], xq.at[0])
-        bring(code_home, codes)
-        bring(gain_home, gain)
-    elif merge:
-        got_home, k_out, vt_out, s_out, sum_out, got = rest
-        copies.append(pltpu.make_async_copy(got_home, got, sems.at[0]))
-        copies[0].start()
-    else:
-        k_out, vt_out, s_out = rest[extra:]
+def stage_kernel(count, first, *refs):
+    outs, sems = refs[-1 - count : -1], refs[-1]
+    copies = [
+        pltpu.make_async_copy(home, out, sems.at[i])
+        for i, (home, out) in enumerate(zip(refs, outs))
+        if home.shape == out.shape
+    ]
+    if refs[0].shape != outs[0].shape:
+        part = refs[0].at[first : first + outs[0].shape[0]]
+        copies.append(pltpu.make_async_copy(part, outs[0], sems.at[0]))
+    for copy in copies:
+        copy.start()
+    for copy in copies:
+        copy.wait()
+
+
+def kv_kernel(merge, extra, where, place, even, odd, w, x, *rest):
+    if merge:
+        got_home, rest, got, sems = rest[0], rest[1:-2], rest[-2], rest[-1]
+        copy = pltpu.make_async_copy(got_home, got, sems.at[0])
+        copy.start()
+    rest = rest[extra:]
+    k_out, vt_out, s_out = rest[:3]
     heads, dim = vt_out.shape[:2]
     base = base_of(place, where, heads)
-
-    for step in range(heads // GROUP):
-        for copy in arrivals.get(step, []):
-            copy.wait()
     if merge:
-        copies[0].wait()
+        sum_out = rest[3]
+        copy.wait()
 
     @pl.loop(0, heads // GROUP)
     def _(step):
         for unit in range(GROUP):
             head = step * GROUP + unit
-            keys = convolve(x, 0, rim, w, 1, base + head, dim)
+            keys = convolve(x, 0, place, even, odd, w, 1, base + head, dim)
             k_out[:, lanes(head, dim)] = keys
-            vt = convolve(x, 1, rim, w, 2, base + head, dim).T
+            vt = convolve(x, 1, place, even, odd, w, 2, base + head, dim).T
             vt_out[head] = vt
             state = jnp.dot(vt, keys, preferred_element_type=jnp.float32)
             s_out[head] = state.astype(jnp.bfloat16)
             if merge:
                 sum_out[head] = (state + got[head].astype(jnp.float32)).astype(jnp.bfloat16)
-
-    if first:
-        for copy in copies[2 * (heads // GROUP) + 1 :]:
-            copy.wait()
 
 
 def merge_kernel(*refs):
@@ -152,6 +136,18 @@
     return out
 
 
+def choose_kernel(count, place, *refs):
+    out, sem = refs[-2:]
+    mine = (place[0] >> 2) & (count - 1)
+    for low in range(count):
+
+        @pl.when(mine == low)
+        def _(low=low):
+            copy = pltpu.make_async_copy(refs[low], out, sem)
+            copy.start()
+            copy.wait()
+
+
 def pack_kernel(count, *refs):
     out, sems = refs[-2:]
     copies = [pltpu.make_async_copy(refs[i], out.at[i], sems.at[i]) for i in range(count)]
@@ -161,7 +157,7 @@
         copy.wait()
 
 
-def inside_kernel(where, place, x, rim, w, k_in, vt_in, codes, after, q_out, in_out):
+def inside_kernel(where, place, x, even, odd, w, k_in, vt_in, codes, after, q_out, in_out):
     rows = x.shape[1]
     heads, dim = vt_in.shape[:2]
     base = base_of(place, where, heads)
@@ -173,7 +169,7 @@
         for unit in range(GROUP):
             head = step * GROUP + unit
             cols = lanes(head, dim)
-            queries = convolve(x, 0, rim, w, 0, base + head, dim)
+            queries = convolve(x, 0, place, even, odd, w, 0, base + head, dim)
             q_out[:, cols] = queries
             lam = [
                 codes[level, pl.ds(base + head, 1), :].astype(jnp.float32) * 0.125
@@ -260,6 +256,16 @@
     last.wait()
 
 
+def spread(wanted, count):
+    pairs, free = dict(wanted), [i for i in range(count) if i not in wanted.values()]
+    for i in range(count):
+        if i not in pairs:
+            good = [k for k in (i + 1, i - 1) if k in free] + [k for k in free if k != i] + free
+            pairs[i] = good[0]
+            free.remove(good[0])
+    return sorted(pairs.items())
+
+
 def on_device(projected, conv_weight, level_codes, out_gain):
     taps = conv_weight.shape[1]
     rows, width = projected.shape[1:]
@@ -275,9 +281,11 @@
     def exchange(value, bit):
         return lax.ppermute(value, "ctx", [(i, i ^ (1 << bit)) for i in range(count)])
 
-    rim = lax.ppermute(
-        projected[:, rows - taps + 1 :, :], "ctx", [(i, i + 1) for i in range(count - 1)]
-    )
+    edge = projected[:, rows - taps + 1 :, :]
+    steps = {i: i + 1 for i in range(1, count - 2, 2)} | {i: i - 1 for i in range(4, count - 2, 2)}
+    steps |= {0: 1, 2: 0, count - 2: count - 1, count - 1: count - 3}
+    rim_even = lax.ppermute(edge, "ctx", sorted(steps.items()))
+    rim_odd = exchange(edge, 0)
 
     def kept(value):
         return pltpu.with_memory_space_constraint(value, VMEM)
@@ -289,34 +297,38 @@
     anywhere = pl.BlockSpec(memory_space=pl.ANY)
     state = jax.ShapeDtypeStruct((quarter, dim, dim), bf16)
 
-    def key_value(where, source, weight, first=False, got=None, after=None):
+    def staged(first, shape, arrays, after):
+        shapes = [shape] + [a.shape for a in arrays[1:]]
+        homes = [pltpu.with_memory_space_constraint(a, pltpu.HBM) for a in arrays]
+        brought = pl.pallas_call(
+            functools.partial(stage_kernel, len(homes), first),
+            in_specs=[anywhere] * (len(homes) + 1),
+            out_specs=[whole] * len(homes),
+            out_shape=[VMEM(size, a.dtype) for size, a in zip(shapes, arrays)],
+            scratch_shapes=[pltpu.SemaphoreType.DMA((len(homes),))],
+            compiler_params=params,
+            name="stage",
+        )(*homes, after)
+        return map(kept, brought)
+
+    def key_value(where, got=None, after=None):
         merge, extra = got is not None, 0 if after is None else 1
+        operands = [place, rim_even, rim_odd, weight, source]
+        specs = [scalars] + [whole] * 4
         made = [VMEM((rows, quarter * dim), bf16), VMEM((quarter, dim, rows), bf16), state]
-        scratch, operands = [], [place, rim, weight, source]
-        specs = [scalars, whole] + [anywhere if first else whole] * 2
-        if first:
-            gain = out_gain.reshape(1, width)
-            operands[-2:] = [
-                pltpu.with_memory_space_constraint(a, pltpu.HBM)
-                for a in (weight, source, level_codes, gain)
-            ]
-            specs += [anywhere] * 2
-            made += [VMEM((2, rows, width), bf16), VMEM((1, rows, width), bf16)]
-            made += [VMEM(a.shape, a.dtype) for a in (level_codes, gain, weight)]
+        scratch = []
         if merge:
             operands.append(got)
-            specs.append(anywhere)
             made.append(state)
-            scratch.append(VMEM(state.shape, bf16))
+            scratch = [VMEM(state.shape, bf16), pltpu.SemaphoreType.DMA((1,))]
         if extra:
             operands.append(after)
-            specs.append(anywhere)
-        return pl.pallas_call(
-            functools.partial(kv_kernel, first, merge, extra, where),
-            in_specs=specs,
+        return pl.pallas_call(
+            functools.partial(kv_kernel, merge, extra, where),
+            in_specs=specs + [anywhere] * (len(operands) - len(specs)),
             out_specs=[whole] * len(made),
             out_shape=made,
-            scratch_shapes=scratch + [pltpu.SemaphoreType.DMA((2 * quarter // GROUP + 10,))],
+            scratch_shapes=scratch,
             compiler_params=params,
             name="key_value",
         )(*operands)
@@ -336,6 +348,17 @@
             name="merge",
         )(*values, *after)
 
+    def chosen(values, after):
+        return pl.pallas_call(
+            functools.partial(choose_kernel, len(values)),
+            in_specs=[scalars] + [anywhere] * (len(values) + len(after)),
+            out_specs=anywhere,
+            out_shape=state,
+            scratch_shapes=[pltpu.SemaphoreType.DMA],
+            compiler_params=params,
+            name="choose",
+        )(place, *values, *after)
+
     def packed(values, after):
         shape = (len(values), *state.shape)
         return pl.pallas_call(
@@ -351,13 +374,13 @@
     def inside(where, after):
         return pl.pallas_call(
             functools.partial(inside_kernel, where),
-            in_specs=[scalars] + [whole] * 6 + [anywhere],
+            in_specs=[scalars] + [whole] * 7 + [anywhere],
             out_specs=[whole] * 2,
             out_shape=[VMEM((rows, quarter * dim), bf16), VMEM((quarter, dim, rows), f32)],
             compiler_params=params,
             name="inside",
         )(
-            place, raw, rim, weight, kept(keys[where]), kept(values[where]), codes, after
+            place, raw, rim_even, rim_odd, weight, kept(keys[where]), kept(values[where]), codes, after
         )
 
     def across(where, local, states, out):
@@ -381,23 +404,18 @@
 
     near, far, other_near, other_far = (0, 0), (0, 1), (1, 0), (1, 1)
     keys, values, local = {}, {}, {}
-    keys[other_far], values[other_far], sent, source, raw, codes, gain, weight = key_value(
-        other_far, projected, conv_weight, first=True
-    )
-    source, raw, codes, gain, weight = map(kept, (source, raw, codes, gain, weight))
+    source, weight = staged(1, (2, rows, width), (projected, conv_weight), edge)
+    keys[other_far], values[other_far], sent = key_value(other_far)
     got_far = exchange(sent, 0)
-    keys[far], values[far], state_far, total_far = key_value(far, source, weight, got=got_far)
+    keys[other_near], values[other_near], sent = key_value(other_near, after=sent)
+    got_near = exchange(sent, 0)
+    keys[far], values[far], state_far, total_far = key_value(far, got_far, after=sent)
     near1 = exchange(total_far, 1)
-    keys[other_near], values[other_near], sent = key_value(
-        other_near, source, weight, after=total_far
-    )
-    got_near = exchange(sent, 0)
-    keys[near], values[near], state_near, total_near = key_value(
-        near, source, weight, got=got_near
-    )
+    keys[near], values[near], state_near, total_near = key_value(near, got_near, after=total_far)
     far1 = exchange(total_near, 1)
+    rest = (projected, level_codes, out_gain.reshape(1, width))
+    raw, codes, gain = staged(0, (1, rows, width), rest, total_near)
     nears, fars = [got_near, near1], [got_far, far1]
-    running = merged([total_near, near1], [])
     waiting = [near, far, other_near, other_far]
 
     def work(where, after):
@@ -405,21 +423,25 @@
         local[where] = inside(where, after)
         return local[where][1]
 
+    running = merged([total_near, near1], [work(near, total_near)])
     for bit in range(2, bits):
         ones = (1 << bit) - 4
-        pieces = []
-        for low in reversed(range(1 << (bit - 2))):
-            pairs = [
-                (i, (i & ~ones) | (low << 2) | (1 << bit))
-                for i in range(count)
-                if i & ones == ones and not i >> bit & 1
-            ]
-            pieces.append(lax.ppermute(running, "ctx", pairs))
+        if bit == 2:
+            pieces = [exchange(running, bit)]
+        else:
+            pieces = []
+            for low in reversed(range(1 << (bit - 2))):
+                holders = [
+                    i for i in range(count // 4) if i << 2 & ones == ones and not i << 2 >> bit & 1
+                ]
+                wanted = {i: (i & ~(ones >> 2)) | low | (1 << (bit - 2)) for i in holders}
+                pairs = [(i * 4 + j, k * 4 + j) for i, k in spread(wanted, count // 4) for j in range(4)]
+                pieces.append(lax.ppermute(running, "ctx", pairs))
         after = []
         for _ in range(bit - 1):
-            if len(waiting) > 1:
+            if waiting:
                 after.append(work(waiting[0], after[-1] if after else running))
-        got = merged(pieces, after) if len(pieces) > 1 else pieces[0]
+        got = chosen(pieces[::-1], after) if len(pieces) > 1 else pieces[0]
         if bit + 1 < bits:
             running = merged([running, got], after)
         nears.append(got)
@@ -427,14 +449,14 @@
         if bit == 2:
             early = exchange(packed([state_near, near1, state_far, far1], [running]), 0)
     late = exchange(packed(nears[2:] + fars[2:-1], []), 0)
+    later = bits - 2
+    other_nears = [(early, 0), (early, 1)] + [(late, i) for i in range(later)]
     after = [work(where, nears[-1]) for where in list(waiting)]
     out, token = across(near, local[near], nears, None)
+    out, token = across(other_near, local[other_near], other_nears, out)
     last = merged(fars[-1:], after + [token])
-    later = bits - 2
-    other_nears = [(early, 0), (early, 1)] + [(late, i) for i in range(later)]
     other_fars = [(early, 2), (early, 3)] + [(late, later + i) for i in range(later - 1)]
     other_fars.append(exchange(last, 0))
-    out, _ = across(other_near, local[other_near], other_nears, out)
     out, _ = across(far, local[far], fars[:-1] + [last], out)
     return across(other_far, local[other_far], other_fars, out)[0]
 

time: 71.7 us -> 64.5 us (0.90)
  the two profiles are of different devices: /device:TPU:27 before, /device:TPU:1 now
where the time goes in v3:
time: 64.5 us; the launch traced here: 64.3 us
  Pallas kernels  41.9 us (65%)
  starting transfers between devices  13.2 us (20%)
  waiting for transfers between devices  7.79 us (12%)
  local copies, waits for them, and re-layouts  0.98 us (2%)
    pallas_call x4, Pallas kernels, inside(): pl.pallas_call(functools.partial(inside_kernel, where), in_specs=[scalars...  13.2 us
    pallas_call x4, Pallas kernels, across(): pl.pallas_call(functools.partial(across_kernel, bits, tok_bits + 1, len(h...  12.5 us
    pallas_call x4, Pallas kernels, key_value(): pl.pallas_call(functools.partial(kv_kernel, merge, extra, where), in_spec...  9.21 us
    ppermute x11, starting transfers between devices, exchange(): return lax.ppermute(value, 'ctx', [(i, i ^ 1 << bit) for i in range(count)])  7.88 us
    pallas_call x2, Pallas kernels, staged(): pl.pallas_call(functools.partial(stage_kernel, len(homes), first), in_spe...  6.03 us
    ppermute x11, waiting for transfers between devices, exchange(): return lax.ppermute(value, 'ctx', [(i, i ^ 1 << bit) for i in range(count)])  4.08 us
    ppermute x2, waiting for transfers between devices, on_device(): pieces.append(lax.ppermute(running, 'ctx', pairs))  3.71 us
    ppermute x1, starting transfers between devices, on_device(): rim_even = lax.ppermute(edge, 'ctx', sorted(steps.items()))  2.68 us
  transfers between devices with their start and end apart: 14, of which 3 were waited for; matrix products, arithmetic and copies ran while one was open for 0% of the time, Pallas kernels for 56%

profile of v3, /device:TPU:1, one launch (start us, length us, event | category | flops | bytes accessed | tf_op | source)
XLA Modules:
  0.0 64.3 jit_solution(11679056188842954254)
XLA Ops:
  0.0 1.0 %slice.3.refs_2_ = bf16[3,3,4096]{2,1,0:T(4,128)(2,1)S(1)} slice(bf16[3,512,4096]{2,1,0:T(8,128)(2,1)} %refs_0_.3), slice={[0:3], [509:512], [0:4096]} | slice | bytes 147456 | tf_op jit(solution)/shard_map/slice | solution.py:284
  1.0 2.7 %collective-permute-start = (bf16[3,3,4096]{2,1,0:T(4,128)(2,1)S(1)}, bf16[3,3,4096]{2,1,0:T(4,128)(2,1)S(1)}, u32[]{:S(2)}, u32[]{:S(2)}) collective-permute-start(bf16[3,3,4096]{2,1,0:T(4,128)(2,1)S(1)} %slice.3.refs_2_), channel_id=1, source_target_pairs={{0,1},{1,2},{2,0},{3,4},{4,3},{5,6},{6,5},{7,8},{8,7},{9,10},{10,9... | collective-permute-start | bytes 221192 | tf_op jit(solution)/shard_map/ppermute | solution.py:287
  3.7 0.0 collective-permute-start.1
  3.7 3.5 %stage.2 = (bf16[2,512,4096]{2,1,0:T(8,128)(2,1)S(1)}, f32[3,4,4096]{2,1,0:T(4,128)S(1)}) custom-call(bf16[3,512,4096]{2,1,0:T(8,128)(2,1)} %refs_0_.3, f32[3,4,4096]{2,1,0:T(4,128)} %refs_1_.2, bf16[3,3,4096]{2,1,0:T(4,128)(2,1)S(1)} %slice.3.refs_2_), custom_call_target="tpu_custom_call" | custom-call | tf_op jit(solution)/shard_map/stage/pallas_call | solution.py:303
  7.2 0.0 collective-permute-done.even
  7.2 0.0 collective-permute-done.1.odd
  7.2 2.2 %key_value.4 = (bf16[512,1024]{1,0:T(8,128)(2,1)S(1)}, bf16[8,128,512]{2,1,0:T(8,128)(2,1)S(1)}, bf16[8,128,128]{2,1,0:T(8,128)(2,1)S(1)}) custom-call(s32[1]{0:T(128)} %bitcast.place, bf16[3,3,4096]{2,1,0:T(4,128)(2,1)S(1)} %collective-permute-done.even, bf16[3,3,4096]{2,1,0:T(4,128)(2,1)S(1)} %collective-permute-done.1.odd, ...), custom_call_target="tpu_custom_call" | custom-call | tf_op jit(solution)/shard_map/key_value/pallas_call | solution.py:326
  9.5 0.6 collective-permute-start.3
  10.0 2.2 %key_value.5 = (bf16[512,1024]{1,0:T(8,128)(2,1)S(1)}, bf16[8,128,512]{2,1,0:T(8,128)(2,1)S(1)}, bf16[8,128,128]{2,1,0:T(8,128)(2,1)S(1)}) custom-call(s32[1]{0:T(128)} %bitcast.place, bf16[3,3,4096]{2,1,0:T(4,128)(2,1)S(1)} %collective-permute-done.even, bf16[3,3,4096]{2,1,0:T(4,128)(2,1)S(1)} %collective-permute-done.1.odd, ...), custom_call_target="tpu_custom_call" | custom-call | tf_op jit(solution)/shard_map/key_value/pallas_call | solution.py:326
  12.3 0.1 collective-permute-start.2
  12.3 0.0 collective-permute-done.3.rest_0_
  12.4 2.5 %key_value.6 = (bf16[512,1024]{1,0:T(8,128)(2,1)S(1)}, bf16[8,128,512]{2,1,0:T(8,128)(2,1)S(1)}, bf16[8,128,128]{2,1,0:T(8,128)(2,1)S(1)}, bf16[8,128,128]{2,1,0:T(8,128)(2,1)S(1)}) custom-call(s32[1]{0:T(128)} %bitcast.place, bf16[3,3,4096]{2,1,0:T(4,128)(2,1)S(1)} %collective-permute-done.even, bf16[3,3,4096]{2,1,0:T(4,128)(2,1)S(1)} %collective-permute-done.1.odd, ...), custom_call_target="tpu_custom_call" | custom-call | tf_op jit(solution)/shard_map/key_value/pallas_call | solution.py:326
  14.8 1.3 %collective-permute-start.4 = (bf16[8,128,128]{2,1,0:T(8,128)(2,1)S(1)}, bf16[8,128,128]{2,1,0:T(8,128)(2,1)S(1)}, u32[]{:S(2)}, u32[]{:S(2)}) collective-permute-start(bf16[8,128,128]{2,1,0:T(8,128)(2,1)S(1)} %get-tuple-element.41.rest_1_), channel_id=1, source_target_pairs={{0,2},{1,3},{2,0},{3,1},{4,6},{5,7},{6,4},{7,5},{8,10},{9,11},{10,... | collective-permute-start | bytes 786440 | tf_op jit(solution)/shard_map/ppermute | solution.py:282
  16.1 0.0 collective-permute-done.2.rest_0_
  16.1 2.3 %key_value.7 = (bf16[512,1024]{1,0:T(8,128)(2,1)S(1)}, bf16[8,128,512]{2,1,0:T(8,128)(2,1)S(1)}, bf16[8,128,128]{2,1,0:T(8,128)(2,1)S(1)}, bf16[8,128,128]{2,1,0:T(8,128)(2,1)S(1)}) custom-call(s32[1]{0:T(128)} %bitcast.place, bf16[3,3,4096]{2,1,0:T(4,128)(2,1)S(1)} %collective-permute-done.even, bf16[3,3,4096]{2,1,0:T(4,128)(2,1)S(1)} %collective-permute-done.1.odd, ...), custom_call_target="tpu_custom_call" | custom-call | tf_op jit(solution)/shard_map/key_value/pallas_call | solution.py:326
  18.4 2.5 %stage.3 = (bf16[1,512,4096]{2,1,0:T(8,128)(2,1)S(1)}, s32[14,32,512]{2,1,0:T(8,128)S(1)}, f32[1,4096]{1,0:T(1,128)S(1)}) custom-call(bf16[3,512,4096]{2,1,0:T(8,128)(2,1)} %refs_0_.3, s32[14,32,512]{2,1,0:T(8,128)} %refs_1_.3, f32[1,4096]{1,0:T(1,128)} %bitcast.2, bf16[8,128,128]{2,1,0:T(8,128)(2,1)S(1)} %get-tuple-element.42.refs_3_.after.refs_0_), custom_call_target="tpu_custom_call" | custom-call | tf_op jit(solution)/shard_map/stage/pallas_call | solution.py:303
  21.0 3.3 %inside.4 = (bf16[512,1024]{1,0:T(8,128)(2,1)S(1)}, f32[8,128,512]{2,1,0:T(8,128)S(1)}) custom-call(s32[1]{0:T(128)} %bitcast.place, bf16[1,512,4096]{2,1,0:T(8,128)(2,1)S(1)} %get-tuple-element.43.x, bf16[3,3,4096]{2,1,0:T(4,128)(2,1)S(1)} %collective-permute-done.even, bf16[3,3,4096]{2,1,0:T(4,128)(2,1)S(1)} %collective-permute-done.1.odd, ...), custom_call_target="tpu_custom_call" | custom-call | tf_op jit(solution)/shard_map/inside/pallas_call | solution.py:375
  24.3 0.0 collective-permute-done.4.refs_1_.rest_1_
  24.3 0.1 merge.3.after.refs_0_
  24.4 1.4 %collective-permute-start.5 = (bf16[8,128,128]{2,1,0:T(8,128)(2,1)S(1)}, bf16[8,128,128]{2,1,0:T(8,128)(2,1)S(1)}, u32[]{:S(2)}, u32[]{:S(2)}) collective-permute-start(bf16[8,128,128]{2,1,0:T(8,128)(2,1)S(1)} %merge.3.after.refs_0_), channel_id=1, source_target_pairs={{0,4},{1,5},{2,6},{3,7},{4,0},{5,1},{6,2},{7,3},{8,12},{9,13},{10,... | collective-permute-start | bytes 786440 | tf_op jit(solution)/shard_map/ppermute | solution.py:282
  25.8 0.2 collective-permute-start.6
  26.0 3.3 %inside.5 = (bf16[512,1024]{1,0:T(8,128)(2,1)S(1)}, f32[8,128,512]{2,1,0:T(8,128)S(1)}) custom-call(s32[1]{0:T(128)} %bitcast.place, bf16[1,512,4096]{2,1,0:T(8,128)(2,1)S(1)} %get-tuple-element.43.x, bf16[3,3,4096]{2,1,0:T(4,128)(2,1)S(1)} %collective-permute-done.even, bf16[3,3,4096]{2,1,0:T(4,128)(2,1)S(1)} %collective-permute-done.1.odd, ...), custom_call_target="tpu_custom_call" | custom-call | tf_op jit(solution)/shard_map/inside/pallas_call | solution.py:375
  29.3 2.5 %collective-permute-done.5.refs_1_.refs_0_.rest_2_ = bf16[8,128,128]{2,1,0:T(8,128)(2,1)S(1)} collective-permute-done((bf16[8,128,128]{2,1,0:T(8,128)(2,1)S(1)}, bf16[8,128,128]{2,1,0:T(8,128)(2,1)S(1)}, u32[]{:S(2)}, u32[]{:S(2)}) %collective-permute-start.5) | collective-permute-done | bytes 262176 | tf_op jit(solution)/shard_map/ppermute | solution.py:282
  31.8 0.1 merge.4.after.refs_4_
  31.9 1.3 %collective-permute-start.8 = (bf16[8,128,128]{2,1,0:T(8,128)(2,1)S(1)}, bf16[8,128,128]{2,1,0:T(8,128)(2,1)S(1)}, u32[]{:S(2)}, u32[]{:S(2)}) collective-permute-start(bf16[8,128,128]{2,1,0:T(8,128)(2,1)S(1)} %merge.4.after.refs_4_), channel_id=1, source_target_pairs={{0,4},{1,5},{2,6},{3,7},{4,8},{5,9},{6,10},{7,11},{8,12},{9,13},{1... | collective-permute-start | bytes 786440 | tf_op jit(solution)/shard_map/ppermute | solution.py:439
  33.3 1.3 %collective-permute-start.9 = (bf16[8,128,128]{2,1,0:T(8,128)(2,1)S(1)}, bf16[8,128,128]{2,1,0:T(8,128)(2,1)S(1)}, u32[]{:S(2)}, u32[]{:S(2)}) collective-permute-start(bf16[8,128,128]{2,1,0:T(8,128)(2,1)S(1)} %merge.4.after.refs_4_), channel_id=1, source_target_pairs={{0,4},{1,5},{2,6},{3,7},{4,12},{5,13},{6,14},{7,15},{8,0},{9,1},{1... | collective-permute-start | bytes 786440 | tf_op jit(solution)/shard_map/ppermute | solution.py:439
  34.6 0.2 collective-permute-start.10
  34.8 0.0 collective-permute-done.6.refs_3_.rest_1_
  34.8 0.1 pack.2
  34.9 2.3 %collective-permute-start.7 = (bf16[4,8,128,128]{3,2,1,0:T(8,128)(2,1)S(1)}, bf16[4,8,128,128]{3,2,1,0:T(8,128)(2,1)S(1)}, u32[]{:S(2)}, u32[]{:S(2)}) collective-permute-start(bf16[4,8,128,128]{3,2,1,0:T(8,128)(2,1)S(1)} %pack.2), channel_id=1, source_target_pairs={{0,1},{1,0},{2,3},{3,2},{4,5},{5,4},{6,7},{7,6},{8,9},{9,8},{10,11... | collective-permute-start | bytes 3145736 | tf_op jit(solution)/shard_map/ppermute | solution.py:282
  37.3 3.3 %inside.6 = (bf16[512,1024]{1,0:T(8,128)(2,1)S(1)}, f32[8,128,512]{2,1,0:T(8,128)S(1)}) custom-call(s32[1]{0:T(128)} %bitcast.place, bf16[1,512,4096]{2,1,0:T(8,128)(2,1)S(1)} %get-tuple-element.43.x, bf16[3,3,4096]{2,1,0:T(4,128)(2,1)S(1)} %collective-permute-done.even, bf16[3,3,4096]{2,1,0:T(4,128)(2,1)S(1)} %collective-permute-done.1.odd, ...), custom_call_target="tpu_custom_call" | custom-call | tf_op jit(solution)/shard_map/inside/pallas_call | solution.py:375
  40.6 3.3 %inside.7 = (bf16[512,1024]{1,0:T(8,128)(2,1)S(1)}, f32[8,128,512]{2,1,0:T(8,128)S(1)}) custom-call(s32[1]{0:T(128)} %bitcast.place, bf16[1,512,4096]{2,1,0:T(8,128)(2,1)S(1)} %get-tuple-element.43.x, bf16[3,3,4096]{2,1,0:T(4,128)(2,1)S(1)} %collective-permute-done.even, bf16[3,3,4096]{2,1,0:T(4,128)(2,1)S(1)} %collective-permute-done.1.odd, ...), custom_call_target="tpu_custom_call" | custom-call | tf_op jit(solution)/shard_map/inside/pallas_call | solution.py:375
  43.9 0.0 collective-permute-done.8.refs_0_
  43.9 3.7 %collective-permute-done.9.refs_1_ = bf16[8,128,128]{2,1,0:T(8,128)(2,1)S(1)} collective-permute-done((bf16[8,128,128]{2,1,0:T(8,128)(2,1)S(1)}, bf16[8,128,128]{2,1,0:T(8,128)(2,1)S(1)}, u32[]{:S(2)}, u32[]{:S(2)}) %collective-permute-start.9) | collective-permute-done | bytes 262176 | tf_op jit(solution)/shard_map/ppermute | solution.py:439
  47.7 0.0 collective-permute-done.10.refs_2_.rest_2_
  47.7 0.3 pack.3
  48.0 0.6 collective-permute-start.11
  48.6 0.3 collective-permute-start.12
  48.9 3.3 %across.4 = (bf16[512,4096]{1,0:T(8,128)(2,1)}, f32[8,128]{1,0:T(8,128)}) custom-call(s32[1]{0:T(128)} %bitcast.place, bf16[512,1024]{1,0:T(8,128)(2,1)S(1)} %get-tuple-element.62.q_in, f32[8,128,512]{2,1,0:T(8,128)S(1)} %get-tuple-element.51.refs_2_.in_in, s32[14,32,512]{2,1,0:T(8,128)S(1)} %get-tuple-element.46.codes, ...), custom_call_target="tpu_custom_call" | custom-call | tf_op jit(solution)/shard_map/across/pallas_call | solution.py:390
  52.2 0.0 collective-permute-done.11.rest_2_.rest_3_
  52.2 0.0 collective-permute-done.7.rest_0_.rest_1_
  52.2 2.7 %across.5 = (bf16[512,4096]{1,0:T(8,128)(2,1)}, f32[8,128]{1,0:T(8,128)S(1)}) custom-call(s32[1]{0:T(128)} %bitcast.place, bf16[512,1024]{1,0:T(8,128)(2,1)S(1)} %get-tuple-element.61.q_in, f32[8,128,512]{2,1,0:T(8,128)S(1)} %get-tuple-element.55.after.refs_2_.in_in, s32[14,32,512]{2,1,0:T(8,128)S(1)} %get-tuple-element.46.codes, ...), custom_call_target="tpu_custom_call", output_to_operand_aliasing={{0}: (9, {})} | custom-call | tf_op jit(solution)/shard_map/across/pallas_call | solution.py:390
  54.9 1.6 %collective-permute-done.12.refs_0_ = bf16[8,128,128]{2,1,0:T(8,128)(2,1)S(1)} collective-permute-done((bf16[8,128,128]{2,1,0:T(8,128)(2,1)S(1)}, bf16[8,128,128]{2,1,0:T(8,128)(2,1)S(1)}, u32[]{:S(2)}, u32[]{:S(2)}) %collective-permute-start.12) | collective-permute-done | bytes 262176 | tf_op jit(solution)/shard_map/ppermute | solution.py:282
  56.5 0.1 merge.5.rest_3_
  56.6 0.9 %collective-permute-start.13 = (bf16[8,128,128]{2,1,0:T(8,128)(2,1)S(1)}, bf16[8,128,128]{2,1,0:T(8,128)(2,1)S(1)}, u32[]{:S(2)}, u32[]{:S(2)}) collective-permute-start(bf16[8,128,128]{2,1,0:T(8,128)(2,1)S(1)} %merge.5.rest_3_), channel_id=1, source_target_pairs={{0,1},{1,0},{2,3},{3,2},{4,5},{5,4},{6,7},{7,6},{8,9},{9,8},{10,11... | collective-permute-start | bytes 786440 | tf_op jit(solution)/shard_map/ppermute | solution.py:282
  57.5 3.3 %across.6 = (bf16[512,4096]{1,0:T(8,128)(2,1)}, f32[8,128]{1,0:T(8,128)}) custom-call(s32[1]{0:T(128)} %bitcast.place, bf16[512,1024]{1,0:T(8,128)(2,1)S(1)} %get-tuple-element.65.q_in, f32[8,128,512]{2,1,0:T(8,128)S(1)} %get-tuple-element.54.refs_2_.in_in, s32[14,32,512]{2,1,0:T(8,128)S(1)} %get-tuple-element.46.codes, ...), custom_call_target="tpu_custom_call", output_to_operand_aliasing={{0}: (9, {})} | custom-call | tf_op jit(solution)/shard_map/across/pallas_call | solution.py:390
  60.8 0.0 collective-permute-done.13.rest_3_
  60.8 3.3 %across.7 = (bf16[512,4096]{1,0:T(8,128)(2,1)}, f32[8,128]{1,0:T(8,128)}) custom-call(s32[1]{0:T(128)} %bitcast.place, bf16[512,1024]{1,0:T(8,128)(2,1)S(1)} %get-tuple-element.56.q_in, f32[8,128,512]{2,1,0:T(8,128)S(1)} %get-tuple-element.57.refs_3_.in_in, s32[14,32,512]{2,1,0:T(8,128)S(1)} %get-tuple-element.46.codes, ...), custom_call_target="tpu_custom_call", output_to_operand_aliasing={{0}: (9, {})} | custom-call | tf_op jit(solution)/shard_map/across/pallas_call | solution.py:390
  (1 shorter events, 0.0 us)
Async XLA Ops:
  1.0 6.2 %collective-permute-start = (bf16[3,3,4096]{2,1,0:T(4,128)(2,1)S(1)}, bf16[3,3,4096]{2,1,0:T(4,128)(2,1)S(1)}, u32[]{:S(2)}, u32[]{:S(2)}) collective-permute-start(bf16[3,3,4096]{2,1,0:T(4,128)(2,1)S(1)} %slice.3.refs_2_), channel_id=1, source_target_pairs={{0,1},{1,2},{2,0},{3,4},{4,3},{5,6},{6,5},{7,8},{8,7},{9,10},{10,9... | collective-permute-start | bytes 221192 | tf_op jit(solution)/shard_map/ppermute | solution.py:287
  3.7 3.5 %collective-permute-start.1 = (bf16[3,3,4096]{2,1,0:T(4,128)(2,1)S(1)}, bf16[3,3,4096]{2,1,0:T(4,128)(2,1)S(1)}, u32[]{:S(2)}, u32[]{:S(2)}) collective-permute-start(bf16[3,3,4096]{2,1,0:T(4,128)(2,1)S(1)} %slice.3.refs_2_), channel_id=1, source_target_pairs={{0,1},{1,0},{2,3},{3,2},{4,5},{5,4},{6,7},{7,6},{8,9},{9,8},{10,11... | collective-permute-start | bytes 221192 | tf_op jit(solution)/shard_map/ppermute | solution.py:282
  9.5 2.9 %collective-permute-start.3 = (bf16[8,128,128]{2,1,0:T(8,128)(2,1)S(1)}, bf16[8,128,128]{2,1,0:T(8,128)(2,1)S(1)}, u32[]{:S(2)}, u32[]{:S(2)}) collective-permute-start(bf16[8,128,128]{2,1,0:T(8,128)(2,1)S(1)} %get-tuple-element.39.rest_0_), channel_id=1, source_target_pairs={{0,1},{1,0},{2,3},{3,2},{4,5},{5,4},{6,7},{7,6},{8,9},{9,8},{10,11... | collective-permute-start | bytes 786440 | tf_op jit(solution)/shard_map/ppermute | solution.py:282
  12.3 3.9 %collective-permute-start.2 = (bf16[8,128,128]{2,1,0:T(8,128)(2,1)S(1)}, bf16[8,128,128]{2,1,0:T(8,128)(2,1)S(1)}, u32[]{:S(2)}, u32[]{:S(2)}) collective-permute-start(bf16[8,128,128]{2,1,0:T(8,128)(2,1)S(1)} %get-tuple-element.40.rest_1_), channel_id=1, source_target_pairs={{0,1},{1,0},{2,3},{3,2},{4,5},{5,4},{6,7},{7,6},{8,9},{9,8},{10,11... | collective-permute-start | bytes 786440 | tf_op jit(solution)/shard_map/ppermute | solution.py:282
  14.8 9.4 %collective-permute-start.4 = (bf16[8,128,128]{2,1,0:T(8,128)(2,1)S(1)}, bf16[8,128,128]{2,1,0:T(8,128)(2,1)S(1)}, u32[]{:S(2)}, u32[]{:S(2)}) collective-permute-start(bf16[8,128,128]{2,1,0:T(8,128)(2,1)S(1)} %get-tuple-element.41.rest_1_), channel_id=1, source_target_pairs={{0,2},{1,3},{2,0},{3,1},{4,6},{5,7},{6,4},{7,5},{8,10},{9,11},{10,... | collective-permute-start | bytes 786440 | tf_op jit(solution)/shard_map/ppermute | solution.py:282
  24.4 7.3 %collective-permute-start.5 = (bf16[8,128,128]{2,1,0:T(8,128)(2,1)S(1)}, bf16[8,128,128]{2,1,0:T(8,128)(2,1)S(1)}, u32[]{:S(2)}, u32[]{:S(2)}) collective-permute-start(bf16[8,128,128]{2,1,0:T(8,128)(2,1)S(1)} %merge.3.after.refs_0_), channel_id=1, source_target_pairs={{0,4},{1,5},{2,6},{3,7},{4,0},{5,1},{6,2},{7,3},{8,12},{9,13},{10,... | collective-permute-start | bytes 786440 | tf_op jit(solution)/shard_map/ppermute | solution.py:282
  25.8 9.0 %collective-permute-start.6 = (bf16[8,128,128]{2,1,0:T(8,128)(2,1)S(1)}, bf16[8,128,128]{2,1,0:T(8,128)(2,1)S(1)}, u32[]{:S(2)}, u32[]{:S(2)}) collective-permute-start(bf16[8,128,128]{2,1,0:T(8,128)(2,1)S(1)} %get-tuple-element.42.refs_3_.after.refs_0_), channel_id=1, source_target_pairs={{0,2},{1,3},{2,0},{3,1},{4,6},{5,7},{6,4},{7,5},{8,10},{9,11},{10,... | collective-permute-start | bytes 786440 | tf_op jit(solution)/shard_map/ppermute | solution.py:282
  31.9 12.0 %collective-permute-start.8 = (bf16[8,128,128]{2,1,0:T(8,128)(2,1)S(1)}, bf16[8,128,128]{2,1,0:T(8,128)(2,1)S(1)}, u32[]{:S(2)}, u32[]{:S(2)}) collective-permute-start(bf16[8,128,128]{2,1,0:T(8,128)(2,1)S(1)} %merge.4.after.refs_4_), channel_id=1, source_target_pairs={{0,4},{1,5},{2,6},{3,7},{4,8},{5,9},{6,10},{7,11},{8,12},{9,13},{1... | collective-permute-start | bytes 786440 | tf_op jit(solution)/shard_map/ppermute | solution.py:439
  33.3 14.3 %collective-permute-start.9 = (bf16[8,128,128]{2,1,0:T(8,128)(2,1)S(1)}, bf16[8,128,128]{2,1,0:T(8,128)(2,1)S(1)}, u32[]{:S(2)}, u32[]{:S(2)}) collective-permute-start(bf16[8,128,128]{2,1,0:T(8,128)(2,1)S(1)} %merge.4.after.refs_4_), channel_id=1, source_target_pairs={{0,4},{1,5},{2,6},{3,7},{4,12},{5,13},{6,14},{7,15},{8,0},{9,1},{1... | collective-permute-start | bytes 786440 | tf_op jit(solution)/shard_map/ppermute | solution.py:439
  34.6 13.1 %collective-permute-start.10 = (bf16[8,128,128]{2,1,0:T(8,128)(2,1)S(1)}, bf16[8,128,128]{2,1,0:T(8,128)(2,1)S(1)}, u32[]{:S(2)}, u32[]{:S(2)}) collective-permute-start(bf16[8,128,128]{2,1,0:T(8,128)(2,1)S(1)} %collective-permute-done.5.refs_1_.refs_0_.rest_2_), channel_id=1, source_target_pairs={{0,2},{1,3},{2,0},{3,1},{4,6},{5,7},{6,4},{7,5},{8,10},{9,11},{10,... | collective-permute-start | bytes 786440 | tf_op jit(solution)/shard_map/ppermute | solution.py:282
  34.9 17.3 %collective-permute-start.7 = (bf16[4,8,128,128]{3,2,1,0:T(8,128)(2,1)S(1)}, bf16[4,8,128,128]{3,2,1,0:T(8,128)(2,1)S(1)}, u32[]{:S(2)}, u32[]{:S(2)}) collective-permute-start(bf16[4,8,128,128]{3,2,1,0:T(8,128)(2,1)S(1)} %pack.2), channel_id=1, source_target_pairs={{0,1},{1,0},{2,3},{3,2},{4,5},{5,4},{6,7},{7,6},{8,9},{9,8},{10,11... | collective-permute-start | bytes 3145736 | tf_op jit(solution)/shard_map/ppermute | solution.py:282
  48.0 4.1 %collective-permute-start.11 = (bf16[3,8,128,128]{3,2,1,0:T(8,128)(2,1)S(1)}, bf16[3,8,128,128]{3,2,1,0:T(8,128)(2,1)S(1)}, u32[]{:S(2)}, u32[]{:S(2)}) collective-permute-start(bf16[3,8,128,128]{3,2,1,0:T(8,128)(2,1)S(1)} %pack.3), channel_id=1, source_target_pairs={{0,1},{1,0},{2,3},{3,2},{4,5},{5,4},{6,7},{7,6},{8,9},{9,8},{10,11... | collective-permute-start | bytes 2359304 | tf_op jit(solution)/shard_map/ppermute | solution.py:282
  48.6 7.9 %collective-permute-start.12 = (bf16[8,128,128]{2,1,0:T(8,128)(2,1)S(1)}, bf16[8,128,128]{2,1,0:T(8,128)(2,1)S(1)}, u32[]{:S(2)}, u32[]{:S(2)}) collective-permute-start(bf16[8,128,128]{2,1,0:T(8,128)(2,1)S(1)} %choose.1.refs_1_.rest_3_), channel_id=1, source_target_pairs={{0,2},{1,3},{2,0},{3,1},{4,6},{5,7},{6,4},{7,5},{8,10},{9,11},{10,... | collective-permute-start | bytes 786440 | tf_op jit(solution)/shard_map/ppermute | solution.py:282
  56.6 4.2 %collective-permute-start.13 = (bf16[8,128,128]{2,1,0:T(8,128)(2,1)S(1)}, bf16[8,128,128]{2,1,0:T(8,128)(2,1)S(1)}, u32[]{:S(2)}, u32[]{:S(2)}) collective-permute-start(bf16[8,128,128]{2,1,0:T(8,128)(2,1)S(1)} %merge.5.rest_3_), channel_id=1, source_target_pairs={{0,1},{1,0},{2,3},{3,2},{4,5},{5,4},{6,7},{7,6},{8,9},{9,8},{10,11... | collective-permute-start | bytes 786440 | tf_op jit(solution)/shard_map/ppermute | solution.py:282

commit v4 on v3

--- a/solution.py
+++ b/solution.py
@@ -10,6 +10,7 @@
 NT = (((1,), (1,)), ((), ()))
 ROOM = 8 * 1024 * 1024
 GROUP = 8
+CHUNK = 4
 VMEM = pltpu.VMEM
 
 
@@ -207,22 +208,17 @@
 
 def across_kernel(bits, inner, held, where, slots, place, q_in, in_in, codes, gain, *rest):
     states, out, token = rest[:bits], rest[bits + held], rest[bits + held + 1]
-    fen, mixed, sems = rest[bits + held + 2 :]
+    mixed, sems = rest[bits + held + 2 :]
     token[...] = jnp.zeros_like(token)
     heads, dim, rows = in_in.shape
     base = base_of(place, where, heads)
-    copies = [
-        pltpu.make_async_copy(
-            states[bit] if slots[bit] is None else states[bit].at[slots[bit]],
-            fen.at[:, bit * dim : (bit + 1) * dim, :],
-            sems.at[bit],
-        )
-        for bit in range(bits)
-    ]
-    for copy in copies:
-        copy.start()
-    for copy in copies:
-        copy.wait()
+    width = CHUNK * dim
+
+    def ship(chunk):
+        source = mixed.at[:, pl.ds(pl.multiple_of(chunk * width, width), width)]
+        home = out.at[:, pl.ds(pl.multiple_of(base * dim + chunk * width, width), width)]
+        return pltpu.make_async_copy(source, home, sems.at[chunk])
+
     scales = [((place[0] >> bit) & 1).astype(jnp.float32) * 0.125 for bit in range(bits)]
     wide = min(256, rows)
 
@@ -235,10 +231,17 @@
                 codes[inner + bit, pl.ds(base + head, 1), :].astype(jnp.float32) * scales[bit]
                 for bit in range(bits)
             ]
+            fenwick = jnp.concatenate(
+                [
+                    state[head] if slot is None else state[slot, head]
+                    for state, slot in zip(states, slots)
+                ],
+                0,
+            )
             for t0 in range(0, rows, wide):
                 span = slice(t0, t0 + wide)
                 parts = lax.dot_general(
-                    fen[head], q_in[span, cols], NT, preferred_element_type=jnp.float32
+                    fenwick, q_in[span, cols], NT, preferred_element_type=jnp.float32
                 )
                 total = in_in[head, :, span]
                 for bit in range(bits):
@@ -249,11 +252,11 @@
                     jnp.bfloat16
                 )
 
-    width = heads * dim
-    home = out.at[:, pl.ds(pl.multiple_of(base * dim, width), width)]
-    last = pltpu.make_async_copy(mixed, home, sems.at[bits])
-    last.start()
-    last.wait()
+            if (unit + 1) % CHUNK == 0:
+                ship(step * (GROUP // CHUNK) + unit // CHUNK).start()
+
+    for chunk in range(heads // CHUNK):
+        ship(chunk).wait()
 
 
 def spread(wanted, count):
@@ -389,18 +392,17 @@
         states, slots = zip(*(a if isinstance(a, tuple) else (a, None) for a in states))
         return pl.pallas_call(
             functools.partial(across_kernel, bits, tok_bits + 1, len(held), where, slots),
-            in_specs=[scalars] + [whole] * 4 + [anywhere] * (bits + len(held)),
+            in_specs=[scalars] + [whole] * (4 + bits) + [anywhere] * len(held),
             out_specs=[anywhere, whole],
             out_shape=[jax.ShapeDtypeStruct((rows, width), bf16), VMEM((8, 128), f32)],
             input_output_aliases={5 + bits: 0} if held else {},
             scratch_shapes=[
-                VMEM((quarter, bits * dim, dim), bf16),
                 VMEM((rows, quarter * dim), bf16),
-                pltpu.SemaphoreType.DMA((bits + 1,)),
+                pltpu.SemaphoreType.DMA((quarter // CHUNK,)),
             ],
             compiler_params=params,
             name="across",
-        )(place, kept(queries), kept(inner), codes, gain, *states, *held)
+        )(place, kept(queries), kept(inner), codes, gain, *map(kept, states), *held)
 
     near, far, other_near, other_far = (0, 0), (0, 1), (1, 0), (1, 1)
     keys, values, local = {}, {}, {}
@@ -423,7 +425,8 @@
         local[where] = inside(where, after)
         return local[where][1]
 
-    running = merged([total_near, near1], [work(near, total_near)])
+    early = exchange(packed([state_near, state_far], [total_near]), 0)
+    running = merged([total_near, near1], [raw])
     for bit in range(2, bits):
         ones = (1 << bit) - 4
         if bit == 2:
@@ -438,24 +441,22 @@
                 pairs = [(i * 4 + j, k * 4 + j) for i, k in spread(wanted, count // 4) for j in range(4)]
                 pieces.append(lax.ppermute(running, "ctx", pairs))
         after = []
-        for _ in range(bit - 1):
+        for _ in range(2):
             if waiting:
                 after.append(work(waiting[0], after[-1] if after else running))
         got = chosen(pieces[::-1], after) if len(pieces) > 1 else pieces[0]
         if bit + 1 < bits:
-            running = merged([running, got], after)
+            running = merged([running, got], after + [early, far1])
         nears.append(got)
         fars.append(exchange(got, 1))
-        if bit == 2:
-            early = exchange(packed([state_near, near1, state_far, far1], [running]), 0)
-    late = exchange(packed(nears[2:] + fars[2:-1], []), 0)
-    later = bits - 2
-    other_nears = [(early, 0), (early, 1)] + [(late, i) for i in range(later)]
+    late = exchange(packed(nears[1:] + fars[1:-1], []), 0)
+    later = bits - 1
+    other_nears = [(early, 0)] + [(late, i) for i in range(later)]
     after = [work(where, nears[-1]) for where in list(waiting)]
     out, token = across(near, local[near], nears, None)
     out, token = across(other_near, local[other_near], other_nears, out)
     last = merged(fars[-1:], after + [token])
-    other_fars = [(early, 2), (early, 3)] + [(late, later + i) for i in range(later - 1)]
+    other_fars = [(early, 1)] + [(late, later + i) for i in range(later - 1)]
     other_fars.append(exchange(last, 0))
     out, _ = across(far, local[far], fars[:-1] + [last], out)
     return across(other_far, local[other_far], other_fars, out)[0]

time: 64.5 us -> 61.9 us (0.960)
  Pallas kernels: 41.9 us -> 40.4 us
  waiting for transfers between devices: 7.79 us -> 6.86 us
    ppermute x11, waiting for transfers between devices: 4.08 us -> 1.83 us  [exchange(): return lax.ppermute(value, 'ctx', [(i, i ^ 1 << bit) for i in range(count)])]
    ppermute x2, waiting for transfers between devices: 3.71 us -> 5.02 us  [on_device(): pieces.append(lax.ppermute(running, 'ctx', pairs))]
    pallas_call x4, Pallas kernels: 12.5 us -> 11.3 us  [across(): pl.pallas_call(functools.partial(across_kernel, bits, tok_bits + 1, len(h...]
where the time goes in v4:
time: 61.9 us; the launch traced here: 61.7 us
  Pallas kernels  40.4 us (65%)
  starting transfers between devices  13 us (21%)
  waiting for transfers between devices  6.86 us (11%)
  local copies, waits for them, and re-layouts  0.98 us (2%)
    pallas_call x4, Pallas kernels, inside(): pl.pallas_call(functools.partial(inside_kernel, where), in_specs=[scalars...  13.2 us
    pallas_call x4, Pallas kernels, across(): pl.pallas_call(functools.partial(across_kernel, bits, tok_bits + 1, len(h...  11.3 us
    pallas_call x4, Pallas kernels, key_value(): pl.pallas_call(functools.partial(kv_kernel, merge, extra, where), in_spec...  9.21 us
    ppermute x11, starting transfers between devices, exchange(): return lax.ppermute(value, 'ctx', [(i, i ^ 1 << bit) for i in range(count)])  7.72 us
    pallas_call x2, Pallas kernels, staged(): pl.pallas_call(functools.partial(stage_kernel, len(homes), first), in_spe...  6.03 us
    ppermute x2, waiting for transfers between devices, on_device(): pieces.append(lax.ppermute(running, 'ctx', pairs))  5.02 us
    ppermute x1, starting transfers between devices, on_device(): rim_even = lax.ppermute(edge, 'ctx', sorted(steps.items()))  2.68 us
    ppermute x2, starting transfers between devices, on_device(): pieces.append(lax.ppermute(running, 'ctx', pairs))  2.65 us
  transfers between devices with their start and end apart: 14, of which 3 were waited for; matrix products, arithmetic and copies ran while one was open for 0% of the time, Pallas kernels for 56%

profile of v4, /device:TPU:1, one launch (start us, length us, event | category | flops | bytes accessed | tf_op | source)
XLA Modules:
  0.0 61.7 jit_solution(6920806174730865813)
XLA Ops:
  0.0 1.0 %slice.3.refs_2_ = bf16[3,3,4096]{2,1,0:T(4,128)(2,1)S(1)} slice(bf16[3,512,4096]{2,1,0:T(8,128)(2,1)} %refs_0_.3), slice={[0:3], [509:512], [0:4096]} | slice | bytes 147456 | tf_op jit(solution)/shard_map/slice | solution.py:287
  1.0 2.7 %collective-permute-start = (bf16[3,3,4096]{2,1,0:T(4,128)(2,1)S(1)}, bf16[3,3,4096]{2,1,0:T(4,128)(2,1)S(1)}, u32[]{:S(2)}, u32[]{:S(2)}) collective-permute-start(bf16[3,3,4096]{2,1,0:T(4,128)(2,1)S(1)} %slice.3.refs_2_), channel_id=1, source_target_pairs={{0,1},{1,2},{2,0},{3,4},{4,3},{5,6},{6,5},{7,8},{8,7},{9,10},{10,9... | collective-permute-start | bytes 221192 | tf_op jit(solution)/shard_map/ppermute | solution.py:290
  3.7 0.0 collective-permute-start.1
  3.7 3.5 %stage.2 = (bf16[2,512,4096]{2,1,0:T(8,128)(2,1)S(1)}, f32[3,4,4096]{2,1,0:T(4,128)S(1)}) custom-call(bf16[3,512,4096]{2,1,0:T(8,128)(2,1)} %refs_0_.3, f32[3,4,4096]{2,1,0:T(4,128)} %refs_1_.2, bf16[3,3,4096]{2,1,0:T(4,128)(2,1)S(1)} %slice.3.refs_2_), custom_call_target="tpu_custom_call" | custom-call | tf_op jit(solution)/shard_map/stage/pallas_call | solution.py:306
  7.2 0.0 collective-permute-done.even
  7.2 0.0 collective-permute-done.1.odd
  7.2 2.2 %key_value.4 = (bf16[512,1024]{1,0:T(8,128)(2,1)S(1)}, bf16[8,128,512]{2,1,0:T(8,128)(2,1)S(1)}, bf16[8,128,128]{2,1,0:T(8,128)(2,1)S(1)}) custom-call(s32[1]{0:T(128)} %bitcast.place, bf16[3,3,4096]{2,1,0:T(4,128)(2,1)S(1)} %collective-permute-done.even, bf16[3,3,4096]{2,1,0:T(4,128)(2,1)S(1)} %collective-permute-done.1.odd, ...), custom_call_target="tpu_custom_call" | custom-call | tf_op jit(solution)/shard_map/key_value/pallas_call | solution.py:329
  9.5 0.6 collective-permute-start.3
  10.0 2.2 %key_value.5 = (bf16[512,1024]{1,0:T(8,128)(2,1)S(1)}, bf16[8,128,512]{2,1,0:T(8,128)(2,1)S(1)}, bf16[8,128,128]{2,1,0:T(8,128)(2,1)S(1)}) custom-call(s32[1]{0:T(128)} %bitcast.place, bf16[3,3,4096]{2,1,0:T(4,128)(2,1)S(1)} %collective-permute-done.even, bf16[3,3,4096]{2,1,0:T(4,128)(2,1)S(1)} %collective-permute-done.1.odd, ...), custom_call_target="tpu_custom_call" | custom-call | tf_op jit(solution)/shard_map/key_value/pallas_call | solution.py:329
  12.3 0.1 collective-permute-start.2
  12.3 0.0 collective-permute-done.3.rest_0_
  12.4 2.5 %key_value.6 = (bf16[512,1024]{1,0:T(8,128)(2,1)S(1)}, bf16[8,128,512]{2,1,0:T(8,128)(2,1)S(1)}, bf16[8,128,128]{2,1,0:T(8,128)(2,1)S(1)}, bf16[8,128,128]{2,1,0:T(8,128)(2,1)S(1)}) custom-call(s32[1]{0:T(128)} %bitcast.place, bf16[3,3,4096]{2,1,0:T(4,128)(2,1)S(1)} %collective-permute-done.even, bf16[3,3,4096]{2,1,0:T(4,128)(2,1)S(1)} %collective-permute-done.1.odd, ...), custom_call_target="tpu_custom_call" | custom-call | tf_op jit(solution)/shard_map/key_value/pallas_call | solution.py:329
  14.8 1.3 %collective-permute-start.4 = (bf16[8,128,128]{2,1,0:T(8,128)(2,1)S(1)}, bf16[8,128,128]{2,1,0:T(8,128)(2,1)S(1)}, u32[]{:S(2)}, u32[]{:S(2)}) collective-permute-start(bf16[8,128,128]{2,1,0:T(8,128)(2,1)S(1)} %get-tuple-element.41.rest_1_), channel_id=1, source_target_pairs={{0,2},{1,3},{2,0},{3,1},{4,6},{5,7},{6,4},{7,5},{8,10},{9,11},{10,... | collective-permute-start | bytes 786440 | tf_op jit(solution)/shard_map/ppermute | solution.py:285
  16.1 0.0 collective-permute-done.2.rest_0_
  16.1 2.3 %key_value.7 = (bf16[512,1024]{1,0:T(8,128)(2,1)S(1)}, bf16[8,128,512]{2,1,0:T(8,128)(2,1)S(1)}, bf16[8,128,128]{2,1,0:T(8,128)(2,1)S(1)}, bf16[8,128,128]{2,1,0:T(8,128)(2,1)S(1)}) custom-call(s32[1]{0:T(128)} %bitcast.place, bf16[3,3,4096]{2,1,0:T(4,128)(2,1)S(1)} %collective-permute-done.even, bf16[3,3,4096]{2,1,0:T(4,128)(2,1)S(1)} %collective-permute-done.1.odd, ...), custom_call_target="tpu_custom_call" | custom-call | tf_op jit(solution)/shard_map/key_value/pallas_call | solution.py:329
  18.4 0.1 pack.2
  18.5 0.6 %collective-permute-start.6 = (bf16[2,8,128,128]{3,2,1,0:T(8,128)(2,1)S(1)}, bf16[2,8,128,128]{3,2,1,0:T(8,128)(2,1)S(1)}, u32[]{:S(2)}, u32[]{:S(2)}) collective-permute-start(bf16[2,8,128,128]{3,2,1,0:T(8,128)(2,1)S(1)} %pack.2), channel_id=1, source_target_pairs={{0,1},{1,0},{2,3},{3,2},{4,5},{5,4},{6,7},{7,6},{8,9},{9,8},{10,11... | collective-permute-start | bytes 1572872 | tf_op jit(solution)/shard_map/ppermute | solution.py:285
  19.1 0.2 collective-permute-start.7
  19.4 2.5 %stage.3 = (bf16[1,512,4096]{2,1,0:T(8,128)(2,1)S(1)}, s32[14,32,512]{2,1,0:T(8,128)S(1)}, f32[1,4096]{1,0:T(1,128)S(1)}) custom-call(bf16[3,512,4096]{2,1,0:T(8,128)(2,1)} %refs_0_.3, s32[14,32,512]{2,1,0:T(8,128)} %refs_1_.3, f32[1,4096]{1,0:T(1,128)} %bitcast.2, bf16[8,128,128]{2,1,0:T(8,128)(2,1)S(1)} %get-tuple-element.42.refs_3_.refs_0_.refs_2_), custom_call_target="tpu_custom_call" | custom-call | tf_op jit(solution)/shard_map/stage/pallas_call | solution.py:306
  21.9 0.6 collective-permute-done.4.refs_1_.refs_0_.rest_1_
  22.5 0.1 merge.3.after.refs_0_
  22.6 1.4 %collective-permute-start.5 = (bf16[8,128,128]{2,1,0:T(8,128)(2,1)S(1)}, bf16[8,128,128]{2,1,0:T(8,128)(2,1)S(1)}, u32[]{:S(2)}, u32[]{:S(2)}) collective-permute-start(bf16[8,128,128]{2,1,0:T(8,128)(2,1)S(1)} %merge.3.after.refs_0_), channel_id=1, source_target_pairs={{0,4},{1,5},{2,6},{3,7},{4,0},{5,1},{6,2},{7,3},{8,12},{9,13},{10,... | collective-permute-start | bytes 786440 | tf_op jit(solution)/shard_map/ppermute | solution.py:285
  24.0 3.3 %inside.4 = (bf16[512,1024]{1,0:T(8,128)(2,1)S(1)}, f32[8,128,512]{2,1,0:T(8,128)S(1)}) custom-call(s32[1]{0:T(128)} %bitcast.place, bf16[1,512,4096]{2,1,0:T(8,128)(2,1)S(1)} %get-tuple-element.43.refs_2_.x, bf16[3,3,4096]{2,1,0:T(4,128)(2,1)S(1)} %collective-permute-done.even, bf16[3,3,4096]{2,1,0:T(4,128)(2,1)S(1)} %collective-permute-done.1.odd, ...), custom_call_target="tpu_custom_call" | custom-call | tf_op jit(solution)/shard_map/inside/pallas_call | solution.py:378
  27.3 3.3 %inside.5 = (bf16[512,1024]{1,0:T(8,128)(2,1)S(1)}, f32[8,128,512]{2,1,0:T(8,128)S(1)}) custom-call(s32[1]{0:T(128)} %bitcast.place, bf16[1,512,4096]{2,1,0:T(8,128)(2,1)S(1)} %get-tuple-element.43.refs_2_.x, bf16[3,3,4096]{2,1,0:T(4,128)(2,1)S(1)} %collective-permute-done.even, bf16[3,3,4096]{2,1,0:T(4,128)(2,1)S(1)} %collective-permute-done.1.odd, ...), custom_call_target="tpu_custom_call" | custom-call | tf_op jit(solution)/shard_map/inside/pallas_call | solution.py:378
  30.6 0.0 collective-permute-done.7.refs_5_.refs_3_.rest_1_
  30.6 0.0 collective-permute-done.6.refs_4_.rest_0_
  30.7 0.0 collective-permute-done.5.refs_1_.rest_2_
  30.7 0.1 merge.4.after
  30.8 0.2 collective-permute-start.8
  31.1 2.4 %collective-permute-start.9 = (bf16[8,128,128]{2,1,0:T(8,128)(2,1)S(1)}, bf16[8,128,128]{2,1,0:T(8,128)(2,1)S(1)}, u32[]{:S(2)}, u32[]{:S(2)}) collective-permute-start(bf16[8,128,128]{2,1,0:T(8,128)(2,1)S(1)} %merge.4.after), channel_id=1, source_target_pairs={{0,4},{1,5},{2,6},{3,7},{4,12},{5,13},{6,14},{7,15},{8,0},{9,1},{1... | collective-permute-start | bytes 786440 | tf_op jit(solution)/shard_map/ppermute | solution.py:442
  33.5 0.1 collective-permute-start.10
  33.6 3.3 %inside.6 = (bf16[512,1024]{1,0:T(8,128)(2,1)S(1)}, f32[8,128,512]{2,1,0:T(8,128)S(1)}) custom-call(s32[1]{0:T(128)} %bitcast.place, bf16[1,512,4096]{2,1,0:T(8,128)(2,1)S(1)} %get-tuple-element.43.refs_2_.x, bf16[3,3,4096]{2,1,0:T(4,128)(2,1)S(1)} %collective-permute-done.even, bf16[3,3,4096]{2,1,0:T(4,128)(2,1)S(1)} %collective-permute-done.1.odd, ...), custom_call_target="tpu_custom_call" | custom-call | tf_op jit(solution)/shard_map/inside/pallas_call | solution.py:378
  36.9 3.3 %inside.7 = (bf16[512,1024]{1,0:T(8,128)(2,1)S(1)}, f32[8,128,512]{2,1,0:T(8,128)S(1)}) custom-call(s32[1]{0:T(128)} %bitcast.place, bf16[1,512,4096]{2,1,0:T(8,128)(2,1)S(1)} %get-tuple-element.43.refs_2_.x, bf16[3,3,4096]{2,1,0:T(4,128)(2,1)S(1)} %collective-permute-done.even, bf16[3,3,4096]{2,1,0:T(4,128)(2,1)S(1)} %collective-permute-done.1.odd, ...), custom_call_target="tpu_custom_call" | custom-call | tf_op jit(solution)/shard_map/inside/pallas_call | solution.py:378
  40.2 0.0 collective-permute-done.8.refs_0_
  40.2 5.0 %collective-permute-done.9.refs_1_ = bf16[8,128,128]{2,1,0:T(8,128)(2,1)S(1)} collective-permute-done((bf16[8,128,128]{2,1,0:T(8,128)(2,1)S(1)}, bf16[8,128,128]{2,1,0:T(8,128)(2,1)S(1)}, u32[]{:S(2)}, u32[]{:S(2)}) %collective-permute-start.9) | collective-permute-done | bytes 262176 | tf_op jit(solution)/shard_map/ppermute | solution.py:442
  45.3 0.0 collective-permute-done.10.refs_4_.rest_2_
  45.3 0.1 pack.3
  45.4 1.2 %collective-permute-start.11 = (bf16[5,8,128,128]{3,2,1,0:T(8,128)(2,1)S(1)}, bf16[5,8,128,128]{3,2,1,0:T(8,128)(2,1)S(1)}, u32[]{:S(2)}, u32[]{:S(2)}) collective-permute-start(bf16[5,8,128,128]{3,2,1,0:T(8,128)(2,1)S(1)} %pack.3), channel_id=1, source_target_pairs={{0,1},{1,0},{2,3},{3,2},{4,5},{5,4},{6,7},{7,6},{8,9},{9,8},{10,11... | collective-permute-start | bytes 3932168 | tf_op jit(solution)/shard_map/ppermute | solution.py:285
  46.7 1.3 %collective-permute-start.12 = (bf16[8,128,128]{2,1,0:T(8,128)(2,1)S(1)}, bf16[8,128,128]{2,1,0:T(8,128)(2,1)S(1)}, u32[]{:S(2)}, u32[]{:S(2)}) collective-permute-start(bf16[8,128,128]{2,1,0:T(8,128)(2,1)S(1)} %choose.1.refs_2_.rest_3_), channel_id=1, source_target_pairs={{0,2},{1,3},{2,0},{3,1},{4,6},{5,7},{6,4},{7,5},{8,10},{9,11},{10,... | collective-permute-start | bytes 786440 | tf_op jit(solution)/shard_map/ppermute | solution.py:285
  47.9 3.0 %across.4 = (bf16[512,4096]{1,0:T(8,128)(2,1)}, f32[8,128]{1,0:T(8,128)}) custom-call(s32[1]{0:T(128)} %bitcast.place, bf16[512,1024]{1,0:T(8,128)(2,1)S(1)} %get-tuple-element.62.q_in, f32[8,128,512]{2,1,0:T(8,128)S(1)} %get-tuple-element.51.after.refs_2_.in_in, s32[14,32,512]{2,1,0:T(8,128)S(1)} %get-tuple-element.46.codes, ...), custom_call_target="tpu_custom_call" | custom-call | tf_op jit(solution)/shard_map/across/pallas_call | solution.py:393
  50.9 0.0 collective-permute-done.11.rest_1_.rest_2_.rest_3_
  50.9 2.4 %across.5 = (bf16[512,4096]{1,0:T(8,128)(2,1)}, f32[8,128]{1,0:T(8,128)S(1)}) custom-call(s32[1]{0:T(128)} %bitcast.place, bf16[512,1024]{1,0:T(8,128)(2,1)S(1)} %get-tuple-element.61.q_in, f32[8,128,512]{2,1,0:T(8,128)S(1)} %get-tuple-element.57.after.refs_2_.in_in, s32[14,32,512]{2,1,0:T(8,128)S(1)} %get-tuple-element.46.codes, ...), custom_call_target="tpu_custom_call", output_to_operand_aliasing={{0}: (9, {})} | custom-call | tf_op jit(solution)/shard_map/across/pallas_call | solution.py:393
  53.3 1.2 %collective-permute-done.12.refs_0_ = bf16[8,128,128]{2,1,0:T(8,128)(2,1)S(1)} collective-permute-done((bf16[8,128,128]{2,1,0:T(8,128)(2,1)S(1)}, bf16[8,128,128]{2,1,0:T(8,128)(2,1)S(1)}, u32[]{:S(2)}, u32[]{:S(2)}) %collective-permute-start.12) | collective-permute-done | bytes 262176 | tf_op jit(solution)/shard_map/ppermute | solution.py:285
  54.6 0.1 merge.5.rest_3_
  54.7 0.9 %collective-permute-start.13 = (bf16[8,128,128]{2,1,0:T(8,128)(2,1)S(1)}, bf16[8,128,128]{2,1,0:T(8,128)(2,1)S(1)}, u32[]{:S(2)}, u32[]{:S(2)}) collective-permute-start(bf16[8,128,128]{2,1,0:T(8,128)(2,1)S(1)} %merge.5.rest_3_), channel_id=1, source_target_pairs={{0,1},{1,0},{2,3},{3,2},{4,5},{5,4},{6,7},{7,6},{8,9},{9,8},{10,11... | collective-permute-start | bytes 786440 | tf_op jit(solution)/shard_map/ppermute | solution.py:285
  55.6 3.0 %across.6 = (bf16[512,4096]{1,0:T(8,128)(2,1)}, f32[8,128]{1,0:T(8,128)}) custom-call(s32[1]{0:T(128)} %bitcast.place, bf16[512,1024]{1,0:T(8,128)(2,1)S(1)} %get-tuple-element.65.q_in, f32[8,128,512]{2,1,0:T(8,128)S(1)} %get-tuple-element.54.refs_3_.in_in, s32[14,32,512]{2,1,0:T(8,128)S(1)} %get-tuple-element.46.codes, ...), custom_call_target="tpu_custom_call", output_to_operand_aliasing={{0}: (9, {})} | custom-call | tf_op jit(solution)/shard_map/across/pallas_call | solution.py:393
  58.5 0.0 collective-permute-done.13.rest_3_
  58.6 3.0 %across.7 = (bf16[512,4096]{1,0:T(8,128)(2,1)}, f32[8,128]{1,0:T(8,128)}) custom-call(s32[1]{0:T(128)} %bitcast.place, bf16[512,1024]{1,0:T(8,128)(2,1)S(1)} %get-tuple-element.58.q_in, f32[8,128,512]{2,1,0:T(8,128)S(1)} %get-tuple-element.59.refs_3_.in_in, s32[14,32,512]{2,1,0:T(8,128)S(1)} %get-tuple-element.46.codes, ...), custom_call_target="tpu_custom_call", output_to_operand_aliasing={{0}: (9, {})} | custom-call | tf_op jit(solution)/shard_map/across/pallas_call | solution.py:393
  (1 shorter events, 0.0 us)
Async XLA Ops:
  1.0 6.2 %collective-permute-start = (bf16[3,3,4096]{2,1,0:T(4,128)(2,1)S(1)}, bf16[3,3,4096]{2,1,0:T(4,128)(2,1)S(1)}, u32[]{:S(2)}, u32[]{:S(2)}) collective-permute-start(bf16[3,3,4096]{2,1,0:T(4,128)(2,1)S(1)} %slice.3.refs_2_), channel_id=1, source_target_pairs={{0,1},{1,2},{2,0},{3,4},{4,3},{5,6},{6,5},{7,8},{8,7},{9,10},{10,9... | collective-permute-start | bytes 221192 | tf_op jit(solution)/shard_map/ppermute | solution.py:290
  3.7 3.5 %collective-permute-start.1 = (bf16[3,3,4096]{2,1,0:T(4,128)(2,1)S(1)}, bf16[3,3,4096]{2,1,0:T(4,128)(2,1)S(1)}, u32[]{:S(2)}, u32[]{:S(2)}) collective-permute-start(bf16[3,3,4096]{2,1,0:T(4,128)(2,1)S(1)} %slice.3.refs_2_), channel_id=1, source_target_pairs={{0,1},{1,0},{2,3},{3,2},{4,5},{5,4},{6,7},{7,6},{8,9},{9,8},{10,11... | collective-permute-start | bytes 221192 | tf_op jit(solution)/shard_map/ppermute | solution.py:285
  9.5 2.9 %collective-permute-start.3 = (bf16[8,128,128]{2,1,0:T(8,128)(2,1)S(1)}, bf16[8,128,128]{2,1,0:T(8,128)(2,1)S(1)}, u32[]{:S(2)}, u32[]{:S(2)}) collective-permute-start(bf16[8,128,128]{2,1,0:T(8,128)(2,1)S(1)} %get-tuple-element.39.rest_0_), channel_id=1, source_target_pairs={{0,1},{1,0},{2,3},{3,2},{4,5},{5,4},{6,7},{7,6},{8,9},{9,8},{10,11... | collective-permute-start | bytes 786440 | tf_op jit(solution)/shard_map/ppermute | solution.py:285
  12.3 3.9 %collective-permute-start.2 = (bf16[8,128,128]{2,1,0:T(8,128)(2,1)S(1)}, bf16[8,128,128]{2,1,0:T(8,128)(2,1)S(1)}, u32[]{:S(2)}, u32[]{:S(2)}) collective-permute-start(bf16[8,128,128]{2,1,0:T(8,128)(2,1)S(1)} %get-tuple-element.40.rest_1_), channel_id=1, source_target_pairs={{0,1},{1,0},{2,3},{3,2},{4,5},{5,4},{6,7},{7,6},{8,9},{9,8},{10,11... | collective-permute-start | bytes 786440 | tf_op jit(solution)/shard_map/ppermute | solution.py:285
  14.8 7.7 %collective-permute-start.4 = (bf16[8,128,128]{2,1,0:T(8,128)(2,1)S(1)}, bf16[8,128,128]{2,1,0:T(8,128)(2,1)S(1)}, u32[]{:S(2)}, u32[]{:S(2)}) collective-permute-start(bf16[8,128,128]{2,1,0:T(8,128)(2,1)S(1)} %get-tuple-element.41.rest_1_), channel_id=1, source_target_pairs={{0,2},{1,3},{2,0},{3,1},{4,6},{5,7},{6,4},{7,5},{8,10},{9,11},{10,... | collective-permute-start | bytes 786440 | tf_op jit(solution)/shard_map/ppermute | solution.py:285
  18.5 12.2 %collective-permute-start.6 = (bf16[2,8,128,128]{3,2,1,0:T(8,128)(2,1)S(1)}, bf16[2,8,128,128]{3,2,1,0:T(8,128)(2,1)S(1)}, u32[]{:S(2)}, u32[]{:S(2)}) collective-permute-start(bf16[2,8,128,128]{3,2,1,0:T(8,128)(2,1)S(1)} %pack.2), channel_id=1, source_target_pairs={{0,1},{1,0},{2,3},{3,2},{4,5},{5,4},{6,7},{7,6},{8,9},{9,8},{10,11... | collective-permute-start | bytes 1572872 | tf_op jit(solution)/shard_map/ppermute | solution.py:285
  19.1 11.5 %collective-permute-start.7 = (bf16[8,128,128]{2,1,0:T(8,128)(2,1)S(1)}, bf16[8,128,128]{2,1,0:T(8,128)(2,1)S(1)}, u32[]{:S(2)}, u32[]{:S(2)}) collective-permute-start(bf16[8,128,128]{2,1,0:T(8,128)(2,1)S(1)} %get-tuple-element.42.refs_3_.refs_0_.refs_2_), channel_id=1, source_target_pairs={{0,2},{1,3},{2,0},{3,1},{4,6},{5,7},{6,4},{7,5},{8,10},{9,11},{10,... | collective-permute-start | bytes 786440 | tf_op jit(solution)/shard_map/ppermute | solution.py:285
  22.6 8.0 %collective-permute-start.5 = (bf16[8,128,128]{2,1,0:T(8,128)(2,1)S(1)}, bf16[8,128,128]{2,1,0:T(8,128)(2,1)S(1)}, u32[]{:S(2)}, u32[]{:S(2)}) collective-permute-start(bf16[8,128,128]{2,1,0:T(8,128)(2,1)S(1)} %merge.3.after.refs_0_), channel_id=1, source_target_pairs={{0,4},{1,5},{2,6},{3,7},{4,0},{5,1},{6,2},{7,3},{8,12},{9,13},{10,... | collective-permute-start | bytes 786440 | tf_op jit(solution)/shard_map/ppermute | solution.py:285
  30.8 9.4 %collective-permute-start.8 = (bf16[8,128,128]{2,1,0:T(8,128)(2,1)S(1)}, bf16[8,128,128]{2,1,0:T(8,128)(2,1)S(1)}, u32[]{:S(2)}, u32[]{:S(2)}) collective-permute-start(bf16[8,128,128]{2,1,0:T(8,128)(2,1)S(1)} %merge.4.after), channel_id=1, source_target_pairs={{0,4},{1,5},{2,6},{3,7},{4,8},{5,9},{6,10},{7,11},{8,12},{9,13},{1... | collective-permute-start | bytes 786440 | tf_op jit(solution)/shard_map/ppermute | solution.py:442
  31.1 14.2 %collective-permute-start.9 = (bf16[8,128,128]{2,1,0:T(8,128)(2,1)S(1)}, bf16[8,128,128]{2,1,0:T(8,128)(2,1)S(1)}, u32[]{:S(2)}, u32[]{:S(2)}) collective-permute-start(bf16[8,128,128]{2,1,0:T(8,128)(2,1)S(1)} %merge.4.after), channel_id=1, source_target_pairs={{0,4},{1,5},{2,6},{3,7},{4,12},{5,13},{6,14},{7,15},{8,0},{9,1},{1... | collective-permute-start | bytes 786440 | tf_op jit(solution)/shard_map/ppermute | solution.py:442
  33.5 11.8 %collective-permute-start.10 = (bf16[8,128,128]{2,1,0:T(8,128)(2,1)S(1)}, bf16[8,128,128]{2,1,0:T(8,128)(2,1)S(1)}, u32[]{:S(2)}, u32[]{:S(2)}) collective-permute-start(bf16[8,128,128]{2,1,0:T(8,128)(2,1)S(1)} %collective-permute-done.5.refs_1_.rest_2_), channel_id=1, source_target_pairs={{0,2},{1,3},{2,0},{3,1},{4,6},{5,7},{6,4},{7,5},{8,10},{9,11},{10,... | collective-permute-start | bytes 786440 | tf_op jit(solution)/shard_map/ppermute | solution.py:285
  45.4 5.5 %collective-permute-start.11 = (bf16[5,8,128,128]{3,2,1,0:T(8,128)(2,1)S(1)}, bf16[5,8,128,128]{3,2,1,0:T(8,128)(2,1)S(1)}, u32[]{:S(2)}, u32[]{:S(2)}) collective-permute-start(bf16[5,8,128,128]{3,2,1,0:T(8,128)(2,1)S(1)} %pack.3), channel_id=1, source_target_pairs={{0,1},{1,0},{2,3},{3,2},{4,5},{5,4},{6,7},{7,6},{8,9},{9,8},{10,11... | collective-permute-start | bytes 3932168 | tf_op jit(solution)/shard_map/ppermute | solution.py:285
  46.7 7.9 %collective-permute-start.12 = (bf16[8,128,128]{2,1,0:T(8,128)(2,1)S(1)}, bf16[8,128,128]{2,1,0:T(8,128)(2,1)S(1)}, u32[]{:S(2)}, u32[]{:S(2)}) collective-permute-start(bf16[8,128,128]{2,1,0:T(8,128)(2,1)S(1)} %choose.1.refs_2_.rest_3_), channel_id=1, source_target_pairs={{0,2},{1,3},{2,0},{3,1},{4,6},{5,7},{6,4},{7,5},{8,10},{9,11},{10,... | collective-permute-start | bytes 786440 | tf_op jit(solution)/shard_map/ppermute | solution.py:285
  54.7 3.9 %collective-permute-start.13 = (bf16[8,128,128]{2,1,0:T(8,128)(2,1)S(1)}, bf16[8,128,128]{2,1,0:T(8,128)(2,1)S(1)}, u32[]{:S(2)}, u32[]{:S(2)}) collective-permute-start(bf16[8,128,128]{2,1,0:T(8,128)(2,1)S(1)} %merge.5.rest_3_), channel_id=1, source_target_pairs={{0,1},{1,0},{2,3},{3,2},{4,5},{5,4},{6,7},{7,6},{8,9},{9,8},{10,11... | collective-permute-start | bytes 786440 | tf_op jit(solution)/shard_map/ppermute | solution.py:285

commit v5 on v4

--- a/solution.py
+++ b/solution.py
@@ -10,7 +10,8 @@
 NT = (((1,), (1,)), ((), ()))
 ROOM = 8 * 1024 * 1024
 GROUP = 8
-CHUNK = 4
+WIDE = 8
+CHUNK = 2
 VMEM = pltpu.VMEM
 
 
@@ -222,38 +223,43 @@
     scales = [((place[0] >> bit) & 1).astype(jnp.float32) * 0.125 for bit in range(bits)]
     wide = min(256, rows)
 
-    @pl.loop(0, heads // GROUP)
-    def _(step):
-        for unit in range(GROUP):
-            head = step * GROUP + unit
-            cols = lanes(head, dim)
-            lam = [
-                codes[inner + bit, pl.ds(base + head, 1), :].astype(jnp.float32) * scales[bit]
-                for bit in range(bits)
-            ]
-            fenwick = jnp.concatenate(
-                [
-                    state[head] if slot is None else state[slot, head]
-                    for state, slot in zip(states, slots)
-                ],
-                0,
-            )
-            for t0 in range(0, rows, wide):
-                span = slice(t0, t0 + wide)
-                parts = lax.dot_general(
-                    fenwick, q_in[span, cols], NT, preferred_element_type=jnp.float32
+    def work(used):
+        @pl.loop(0, heads // WIDE)
+        def _(step):
+            for unit in range(WIDE):
+                head = step * WIDE + unit
+                cols = lanes(head, dim)
+                lam = [
+                    codes[inner + bit, pl.ds(base + head, 1), :].astype(jnp.float32) * scales[bit]
+                    for bit in range(used)
+                ]
+                fenwick = jnp.concatenate(
+                    [
+                        state[head] if slot is None else state[slot, head]
+                        for state, slot in zip(states[:used], slots)
+                    ],
+                    0,
                 )
-                total = in_in[head, :, span]
-                for bit in range(bits):
-                    total = total + lam[bit][:, span] * parts[bit * dim : (bit + 1) * dim]
-                mean = jnp.sum(total * total, 0, keepdims=True) * (1.0 / dim)
-                normed = total * lax.rsqrt(mean + 1e-06)
-                mixed[span, cols] = (normed.T * gain[:, lanes(base + head, dim)]).astype(
-                    jnp.bfloat16
-                )
-
-            if (unit + 1) % CHUNK == 0:
-                ship(step * (GROUP // CHUNK) + unit // CHUNK).start()
+                for t0 in range(0, rows, wide):
+                    span = slice(t0, t0 + wide)
+                    parts = lax.dot_general(
+                        fenwick, q_in[span, cols], NT, preferred_element_type=jnp.float32
+                    )
+                    total = in_in[head, :, span]
+                    for bit in range(used):
+                        total = total + lam[bit][:, span] * parts[bit * dim : (bit + 1) * dim]
+                    mean = jnp.sum(total * total, 0, keepdims=True) * (1.0 / dim)
+                    normed = total * lax.rsqrt(mean + 1e-06)
+                    mixed[span, cols] = (normed.T * gain[:, lanes(base + head, dim)]).astype(
+                        jnp.bfloat16
+                    )
+
+                if (unit + 1) % CHUNK == 0:
+                    ship(step * (WIDE // CHUNK) + unit // CHUNK).start()
+
+    few = min(2, bits)
+    pl.when(place[0] < 1 << few)(functools.partial(work, few))
+    pl.when(place[0] >= 1 << few)(functools.partial(work, bits))
 
     for chunk in range(heads // CHUNK):
         ship(chunk).wait()

time: 61.9 us -> 61.2 us (0.989)
  Pallas kernels: 40.4 us -> 38.6 us
  waiting for transfers between devices: 6.86 us -> 7.77 us
    pallas_call x4, Pallas kernels: 11.3 us -> 9.53 us  [across(): pl.pallas_call(functools.partial(across_kernel, bits, tok_bits + 1, len(h...]
    ppermute x11, waiting for transfers between devices: 1.83 us -> 2.75 us  [exchange(): return lax.ppermute(value, 'ctx', [(i, i ^ 1 << bit) for i in range(count)])]
  transfers between devices with their start and end apart: 14 -> 14, of which waited for: 3 -> 3; matrix products, arithmetic and copies ran while one was open for 0% -> 0% of each run, Pallas kernels for 56% -> 55%
where the time goes in v5:
time: 61.2 us; the launch traced here: 60.8 us
  Pallas kernels  38.6 us (63%)
  starting transfers between devices  13 us (21%)
  waiting for transfers between devices  7.77 us (13%)
  local copies, waits for them, and re-layouts  0.98 us (2%)
    pallas_call x4, Pallas kernels, inside(): pl.pallas_call(functools.partial(inside_kernel, where), in_specs=[scalars...  13.2 us
    pallas_call x4, Pallas kernels, across(): pl.pallas_call(functools.partial(across_kernel, bits, tok_bits + 1, len(h...  9.53 us
    pallas_call x4, Pallas kernels, key_value(): pl.pallas_call(functools.partial(kv_kernel, merge, extra, where), in_spec...  9.21 us
    ppermute x11, starting transfers between devices, exchange(): return lax.ppermute(value, 'ctx', [(i, i ^ 1 << bit) for i in range(count)])  7.72 us
    pallas_call x2, Pallas kernels, staged(): pl.pallas_call(functools.partial(stage_kernel, len(homes), first), in_spe...  6.03 us
    ppermute x2, waiting for transfers between devices, on_device(): pieces.append(lax.ppermute(running, 'ctx', pairs))  5.02 us
    ppermute x11, waiting for transfers between devices, exchange(): return lax.ppermute(value, 'ctx', [(i, i ^ 1 << bit) for i in range(count)])  2.75 us
    ppermute x1, starting transfers between devices, on_device(): rim_even = lax.ppermute(edge, 'ctx', sorted(steps.items()))  2.68 us
  transfers between devices with their start and end apart: 14, of which 3 were waited for; matrix products, arithmetic and copies ran while one was open for 0% of the time, Pallas kernels for 55%

profile of v5, /device:TPU:1, one launch (start us, length us, event | category | flops | bytes accessed | tf_op | source)
XLA Modules:
  0.0 60.8 jit_solution(845098060451792445)
XLA Ops:
  0.0 1.0 %slice.3.refs_2_ = bf16[3,3,4096]{2,1,0:T(4,128)(2,1)S(1)} slice(bf16[3,512,4096]{2,1,0:T(8,128)(2,1)} %refs_0_.3), slice={[0:3], [509:512], [0:4096]} | slice | bytes 147456 | tf_op jit(solution)/shard_map/slice | solution.py:293
  1.0 2.7 %collective-permute-start = (bf16[3,3,4096]{2,1,0:T(4,128)(2,1)S(1)}, bf16[3,3,4096]{2,1,0:T(4,128)(2,1)S(1)}, u32[]{:S(2)}, u32[]{:S(2)}) collective-permute-start(bf16[3,3,4096]{2,1,0:T(4,128)(2,1)S(1)} %slice.3.refs_2_), channel_id=1, source_target_pairs={{0,1},{1,2},{2,0},{3,4},{4,3},{5,6},{6,5},{7,8},{8,7},{9,10},{10,9... | collective-permute-start | bytes 221192 | tf_op jit(solution)/shard_map/ppermute | solution.py:296
  3.7 0.0 collective-permute-start.1
  3.7 3.5 %stage.2 = (bf16[2,512,4096]{2,1,0:T(8,128)(2,1)S(1)}, f32[3,4,4096]{2,1,0:T(4,128)S(1)}) custom-call(bf16[3,512,4096]{2,1,0:T(8,128)(2,1)} %refs_0_.3, f32[3,4,4096]{2,1,0:T(4,128)} %refs_1_.2, bf16[3,3,4096]{2,1,0:T(4,128)(2,1)S(1)} %slice.3.refs_2_), custom_call_target="tpu_custom_call" | custom-call | tf_op jit(solution)/shard_map/stage/pallas_call | solution.py:312
  7.2 0.0 collective-permute-done.even
  7.2 0.0 collective-permute-done.1.odd
  7.2 2.2 %key_value.4 = (bf16[512,1024]{1,0:T(8,128)(2,1)S(1)}, bf16[8,128,512]{2,1,0:T(8,128)(2,1)S(1)}, bf16[8,128,128]{2,1,0:T(8,128)(2,1)S(1)}) custom-call(s32[1]{0:T(128)} %bitcast.place, bf16[3,3,4096]{2,1,0:T(4,128)(2,1)S(1)} %collective-permute-done.even, bf16[3,3,4096]{2,1,0:T(4,128)(2,1)S(1)} %collective-permute-done.1.odd, ...), custom_call_target="tpu_custom_call" | custom-call | tf_op jit(solution)/shard_map/key_value/pallas_call | solution.py:335
  9.5 0.6 collective-permute-start.3
  10.0 2.2 %key_value.5 = (bf16[512,1024]{1,0:T(8,128)(2,1)S(1)}, bf16[8,128,512]{2,1,0:T(8,128)(2,1)S(1)}, bf16[8,128,128]{2,1,0:T(8,128)(2,1)S(1)}) custom-call(s32[1]{0:T(128)} %bitcast.place, bf16[3,3,4096]{2,1,0:T(4,128)(2,1)S(1)} %collective-permute-done.even, bf16[3,3,4096]{2,1,0:T(4,128)(2,1)S(1)} %collective-permute-done.1.odd, ...), custom_call_target="tpu_custom_call" | custom-call | tf_op jit(solution)/shard_map/key_value/pallas_call | solution.py:335
  12.3 0.1 collective-permute-start.2
  12.3 0.0 collective-permute-done.3.rest_0_
  12.4 2.5 %key_value.6 = (bf16[512,1024]{1,0:T(8,128)(2,1)S(1)}, bf16[8,128,512]{2,1,0:T(8,128)(2,1)S(1)}, bf16[8,128,128]{2,1,0:T(8,128)(2,1)S(1)}, bf16[8,128,128]{2,1,0:T(8,128)(2,1)S(1)}) custom-call(s32[1]{0:T(128)} %bitcast.place, bf16[3,3,4096]{2,1,0:T(4,128)(2,1)S(1)} %collective-permute-done.even, bf16[3,3,4096]{2,1,0:T(4,128)(2,1)S(1)} %collective-permute-done.1.odd, ...), custom_call_target="tpu_custom_call" | custom-call | tf_op jit(solution)/shard_map/key_value/pallas_call | solution.py:335
  14.8 1.3 %collective-permute-start.4 = (bf16[8,128,128]{2,1,0:T(8,128)(2,1)S(1)}, bf16[8,128,128]{2,1,0:T(8,128)(2,1)S(1)}, u32[]{:S(2)}, u32[]{:S(2)}) collective-permute-start(bf16[8,128,128]{2,1,0:T(8,128)(2,1)S(1)} %get-tuple-element.41.rest_1_), channel_id=1, source_target_pairs={{0,2},{1,3},{2,0},{3,1},{4,6},{5,7},{6,4},{7,5},{8,10},{9,11},{10,... | collective-permute-start | bytes 786440 | tf_op jit(solution)/shard_map/ppermute | solution.py:291
  16.1 0.0 collective-permute-done.2.rest_0_
  16.1 2.3 %key_value.7 = (bf16[512,1024]{1,0:T(8,128)(2,1)S(1)}, bf16[8,128,512]{2,1,0:T(8,128)(2,1)S(1)}, bf16[8,128,128]{2,1,0:T(8,128)(2,1)S(1)}, bf16[8,128,128]{2,1,0:T(8,128)(2,1)S(1)}) custom-call(s32[1]{0:T(128)} %bitcast.place, bf16[3,3,4096]{2,1,0:T(4,128)(2,1)S(1)} %collective-permute-done.even, bf16[3,3,4096]{2,1,0:T(4,128)(2,1)S(1)} %collective-permute-done.1.odd, ...), custom_call_target="tpu_custom_call" | custom-call | tf_op jit(solution)/shard_map/key_value/pallas_call | solution.py:335
  18.4 0.1 pack.2
  18.5 0.6 %collective-permute-start.6 = (bf16[2,8,128,128]{3,2,1,0:T(8,128)(2,1)S(1)}, bf16[2,8,128,128]{3,2,1,0:T(8,128)(2,1)S(1)}, u32[]{:S(2)}, u32[]{:S(2)}) collective-permute-start(bf16[2,8,128,128]{3,2,1,0:T(8,128)(2,1)S(1)} %pack.2), channel_id=1, source_target_pairs={{0,1},{1,0},{2,3},{3,2},{4,5},{5,4},{6,7},{7,6},{8,9},{9,8},{10,11... | collective-permute-start | bytes 1572872 | tf_op jit(solution)/shard_map/ppermute | solution.py:291
  19.1 0.2 collective-permute-start.7
  19.4 2.5 %stage.3 = (bf16[1,512,4096]{2,1,0:T(8,128)(2,1)S(1)}, s32[14,32,512]{2,1,0:T(8,128)S(1)}, f32[1,4096]{1,0:T(1,128)S(1)}) custom-call(bf16[3,512,4096]{2,1,0:T(8,128)(2,1)} %refs_0_.3, s32[14,32,512]{2,1,0:T(8,128)} %refs_1_.3, f32[1,4096]{1,0:T(1,128)} %bitcast.2, bf16[8,128,128]{2,1,0:T(8,128)(2,1)S(1)} %get-tuple-element.42.refs_3_.refs_0_.refs_2_), custom_call_target="tpu_custom_call" | custom-call | tf_op jit(solution)/shard_map/stage/pallas_call | solution.py:312
  21.9 0.6 collective-permute-done.4.refs_1_.refs_0_.rest_1_
  22.5 0.1 merge.3.after.refs_0_
  22.6 1.4 %collective-permute-start.5 = (bf16[8,128,128]{2,1,0:T(8,128)(2,1)S(1)}, bf16[8,128,128]{2,1,0:T(8,128)(2,1)S(1)}, u32[]{:S(2)}, u32[]{:S(2)}) collective-permute-start(bf16[8,128,128]{2,1,0:T(8,128)(2,1)S(1)} %merge.3.after.refs_0_), channel_id=1, source_target_pairs={{0,4},{1,5},{2,6},{3,7},{4,0},{5,1},{6,2},{7,3},{8,12},{9,13},{10,... | collective-permute-start | bytes 786440 | tf_op jit(solution)/shard_map/ppermute | solution.py:291
  24.0 3.3 %inside.4 = (bf16[512,1024]{1,0:T(8,128)(2,1)S(1)}, f32[8,128,512]{2,1,0:T(8,128)S(1)}) custom-call(s32[1]{0:T(128)} %bitcast.place, bf16[1,512,4096]{2,1,0:T(8,128)(2,1)S(1)} %get-tuple-element.43.refs_2_.x, bf16[3,3,4096]{2,1,0:T(4,128)(2,1)S(1)} %collective-permute-done.even, bf16[3,3,4096]{2,1,0:T(4,128)(2,1)S(1)} %collective-permute-done.1.odd, ...), custom_call_target="tpu_custom_call" | custom-call | tf_op jit(solution)/shard_map/inside/pallas_call | solution.py:384
  27.3 3.3 %inside.5 = (bf16[512,1024]{1,0:T(8,128)(2,1)S(1)}, f32[8,128,512]{2,1,0:T(8,128)S(1)}) custom-call(s32[1]{0:T(128)} %bitcast.place, bf16[1,512,4096]{2,1,0:T(8,128)(2,1)S(1)} %get-tuple-element.43.refs_2_.x, bf16[3,3,4096]{2,1,0:T(4,128)(2,1)S(1)} %collective-permute-done.even, bf16[3,3,4096]{2,1,0:T(4,128)(2,1)S(1)} %collective-permute-done.1.odd, ...), custom_call_target="tpu_custom_call" | custom-call | tf_op jit(solution)/shard_map/inside/pallas_call | solution.py:384
  30.6 0.0 collective-permute-done.7.refs_5_.refs_3_.rest_1_
  30.6 0.0 collective-permute-done.6.refs_4_.rest_0_
  30.7 0.0 collective-permute-done.5.refs_1_.rest_2_
  30.7 0.1 merge.4.after
  30.8 0.2 collective-permute-start.8
  31.1 2.4 %collective-permute-start.9 = (bf16[8,128,128]{2,1,0:T(8,128)(2,1)S(1)}, bf16[8,128,128]{2,1,0:T(8,128)(2,1)S(1)}, u32[]{:S(2)}, u32[]{:S(2)}) collective-permute-start(bf16[8,128,128]{2,1,0:T(8,128)(2,1)S(1)} %merge.4.after), channel_id=1, source_target_pairs={{0,4},{1,5},{2,6},{3,7},{4,12},{5,13},{6,14},{7,15},{8,0},{9,1},{1... | collective-permute-start | bytes 786440 | tf_op jit(solution)/shard_map/ppermute | solution.py:448
  33.5 0.1 collective-permute-start.10
  33.6 3.3 %inside.6 = (bf16[512,1024]{1,0:T(8,128)(2,1)S(1)}, f32[8,128,512]{2,1,0:T(8,128)S(1)}) custom-call(s32[1]{0:T(128)} %bitcast.place, bf16[1,512,4096]{2,1,0:T(8,128)(2,1)S(1)} %get-tuple-element.43.refs_2_.x, bf16[3,3,4096]{2,1,0:T(4,128)(2,1)S(1)} %collective-permute-done.even, bf16[3,3,4096]{2,1,0:T(4,128)(2,1)S(1)} %collective-permute-done.1.odd, ...), custom_call_target="tpu_custom_call" | custom-call | tf_op jit(solution)/shard_map/inside/pallas_call | solution.py:384
  36.9 3.3 %inside.7 = (bf16[512,1024]{1,0:T(8,128)(2,1)S(1)}, f32[8,128,512]{2,1,0:T(8,128)S(1)}) custom-call(s32[1]{0:T(128)} %bitcast.place, bf16[1,512,4096]{2,1,0:T(8,128)(2,1)S(1)} %get-tuple-element.43.refs_2_.x, bf16[3,3,4096]{2,1,0:T(4,128)(2,1)S(1)} %collective-permute-done.even, bf16[3,3,4096]{2,1,0:T(4,128)(2,1)S(1)} %collective-permute-done.1.odd, ...), custom_call_target="tpu_custom_call" | custom-call | tf_op jit(solution)/shard_map/inside/pallas_call | solution.py:384
  40.2 0.0 collective-permute-done.8.refs_0_
  40.2 5.0 %collective-permute-done.9.refs_1_ = bf16[8,128,128]{2,1,0:T(8,128)(2,1)S(1)} collective-permute-done((bf16[8,128,128]{2,1,0:T(8,128)(2,1)S(1)}, bf16[8,128,128]{2,1,0:T(8,128)(2,1)S(1)}, u32[]{:S(2)}, u32[]{:S(2)}) %collective-permute-start.9) | collective-permute-done | bytes 262176 | tf_op jit(solution)/shard_map/ppermute | solution.py:448
  45.3 0.0 collective-permute-done.10.refs_4_.rest_2_
  45.3 0.1 pack.3
  45.4 1.2 %collective-permute-start.11 = (bf16[5,8,128,128]{3,2,1,0:T(8,128)(2,1)S(1)}, bf16[5,8,128,128]{3,2,1,0:T(8,128)(2,1)S(1)}, u32[]{:S(2)}, u32[]{:S(2)}) collective-permute-start(bf16[5,8,128,128]{3,2,1,0:T(8,128)(2,1)S(1)} %pack.3), channel_id=1, source_target_pairs={{0,1},{1,0},{2,3},{3,2},{4,5},{5,4},{6,7},{7,6},{8,9},{9,8},{10,11... | collective-permute-start | bytes 3932168 | tf_op jit(solution)/shard_map/ppermute | solution.py:291
  46.7 1.3 %collective-permute-start.12 = (bf16[8,128,128]{2,1,0:T(8,128)(2,1)S(1)}, bf16[8,128,128]{2,1,0:T(8,128)(2,1)S(1)}, u32[]{:S(2)}, u32[]{:S(2)}) collective-permute-start(bf16[8,128,128]{2,1,0:T(8,128)(2,1)S(1)} %choose.1.refs_2_.rest_3_), channel_id=1, source_target_pairs={{0,2},{1,3},{2,0},{3,1},{4,6},{5,7},{6,4},{7,5},{8,10},{9,11},{10,... | collective-permute-start | bytes 786440 | tf_op jit(solution)/shard_map/ppermute | solution.py:291
  47.9 2.5 %across.4 = (bf16[512,4096]{1,0:T(8,128)(2,1)}, f32[8,128]{1,0:T(8,128)}) custom-call(s32[1]{0:T(128)} %bitcast.place, bf16[512,1024]{1,0:T(8,128)(2,1)S(1)} %get-tuple-element.62.q_in, f32[8,128,512]{2,1,0:T(8,128)S(1)} %get-tuple-element.51.after.refs_2_.in_in, s32[14,32,512]{2,1,0:T(8,128)S(1)} %get-tuple-element.46.codes, ...), custom_call_target="tpu_custom_call" | custom-call | tf_op jit(solution)/shard_map/across/pallas_call | solution.py:399
  50.4 0.0 collective-permute-done.11.rest_1_.rest_2_.rest_3_
  50.5 2.0 %across.5 = (bf16[512,4096]{1,0:T(8,128)(2,1)}, f32[8,128]{1,0:T(8,128)S(1)}) custom-call(s32[1]{0:T(128)} %bitcast.place, bf16[512,1024]{1,0:T(8,128)(2,1)S(1)} %get-tuple-element.61.q_in, f32[8,128,512]{2,1,0:T(8,128)S(1)} %get-tuple-element.57.after.refs_2_.in_in, s32[14,32,512]{2,1,0:T(8,128)S(1)} %get-tuple-element.46.codes, ...), custom_call_target="tpu_custom_call", output_to_operand_aliasing={{0}: (9, {})} | custom-call | tf_op jit(solution)/shard_map/across/pallas_call | solution.py:399
  52.4 2.1 %collective-permute-done.12.refs_0_ = bf16[8,128,128]{2,1,0:T(8,128)(2,1)S(1)} collective-permute-done((bf16[8,128,128]{2,1,0:T(8,128)(2,1)S(1)}, bf16[8,128,128]{2,1,0:T(8,128)(2,1)S(1)}, u32[]{:S(2)}, u32[]{:S(2)}) %collective-permute-start.12) | collective-permute-done | bytes 262176 | tf_op jit(solution)/shard_map/ppermute | solution.py:291
  54.6 0.1 merge.5.rest_3_
  54.7 0.9 %collective-permute-start.13 = (bf16[8,128,128]{2,1,0:T(8,128)(2,1)S(1)}, bf16[8,128,128]{2,1,0:T(8,128)(2,1)S(1)}, u32[]{:S(2)}, u32[]{:S(2)}) collective-permute-start(bf16[8,128,128]{2,1,0:T(8,128)(2,1)S(1)} %merge.5.rest_3_), channel_id=1, source_target_pairs={{0,1},{1,0},{2,3},{3,2},{4,5},{5,4},{6,7},{7,6},{8,9},{9,8},{10,11... | collective-permute-start | bytes 786440 | tf_op jit(solution)/shard_map/ppermute | solution.py:291
  55.6 2.5 %across.6 = (bf16[512,4096]{1,0:T(8,128)(2,1)}, f32[8,128]{1,0:T(8,128)}) custom-call(s32[1]{0:T(128)} %bitcast.place, bf16[512,1024]{1,0:T(8,128)(2,1)S(1)} %get-tuple-element.65.q_in, f32[8,128,512]{2,1,0:T(8,128)S(1)} %get-tuple-element.54.refs_3_.in_in, s32[14,32,512]{2,1,0:T(8,128)S(1)} %get-tuple-element.46.codes, ...), custom_call_target="tpu_custom_call", output_to_operand_aliasing={{0}: (9, {})} | custom-call | tf_op jit(solution)/shard_map/across/pallas_call | solution.py:399
  58.1 0.0 collective-permute-done.13.rest_3_
  58.1 2.5 %across.7 = (bf16[512,4096]{1,0:T(8,128)(2,1)}, f32[8,128]{1,0:T(8,128)}) custom-call(s32[1]{0:T(128)} %bitcast.place, bf16[512,1024]{1,0:T(8,128)(2,1)S(1)} %get-tuple-element.58.q_in, f32[8,128,512]{2,1,0:T(8,128)S(1)} %get-tuple-element.59.refs_3_.in_in, s32[14,32,512]{2,1,0:T(8,128)S(1)} %get-tuple-element.46.codes, ...), custom_call_target="tpu_custom_call", output_to_operand_aliasing={{0}: (9, {})} | custom-call | tf_op jit(solution)/shard_map/across/pallas_call | solution.py:399
  (1 shorter events, 0.0 us)
Async XLA Ops:
  1.0 6.2 %collective-permute-start = (bf16[3,3,4096]{2,1,0:T(4,128)(2,1)S(1)}, bf16[3,3,4096]{2,1,0:T(4,128)(2,1)S(1)}, u32[]{:S(2)}, u32[]{:S(2)}) collective-permute-start(bf16[3,3,4096]{2,1,0:T(4,128)(2,1)S(1)} %slice.3.refs_2_), channel_id=1, source_target_pairs={{0,1},{1,2},{2,0},{3,4},{4,3},{5,6},{6,5},{7,8},{8,7},{9,10},{10,9... | collective-permute-start | bytes 221192 | tf_op jit(solution)/shard_map/ppermute | solution.py:296
  3.7 3.5 %collective-permute-start.1 = (bf16[3,3,4096]{2,1,0:T(4,128)(2,1)S(1)}, bf16[3,3,4096]{2,1,0:T(4,128)(2,1)S(1)}, u32[]{:S(2)}, u32[]{:S(2)}) collective-permute-start(bf16[3,3,4096]{2,1,0:T(4,128)(2,1)S(1)} %slice.3.refs_2_), channel_id=1, source_target_pairs={{0,1},{1,0},{2,3},{3,2},{4,5},{5,4},{6,7},{7,6},{8,9},{9,8},{10,11... | collective-permute-start | bytes 221192 | tf_op jit(solution)/shard_map/ppermute | solution.py:291
  9.5 2.9 %collective-permute-start.3 = (bf16[8,128,128]{2,1,0:T(8,128)(2,1)S(1)}, bf16[8,128,128]{2,1,0:T(8,128)(2,1)S(1)}, u32[]{:S(2)}, u32[]{:S(2)}) collective-permute-start(bf16[8,128,128]{2,1,0:T(8,128)(2,1)S(1)} %get-tuple-element.39.rest_0_), channel_id=1, source_target_pairs={{0,1},{1,0},{2,3},{3,2},{4,5},{5,4},{6,7},{7,6},{8,9},{9,8},{10,11... | collective-permute-start | bytes 786440 | tf_op jit(solution)/shard_map/ppermute | solution.py:291
  12.3 3.9 %collective-permute-start.2 = (bf16[8,128,128]{2,1,0:T(8,128)(2,1)S(1)}, bf16[8,128,128]{2,1,0:T(8,128)(2,1)S(1)}, u32[]{:S(2)}, u32[]{:S(2)}) collective-permute-start(bf16[8,128,128]{2,1,0:T(8,128)(2,1)S(1)} %get-tuple-element.40.rest_1_), channel_id=1, source_target_pairs={{0,1},{1,0},{2,3},{3,2},{4,5},{5,4},{6,7},{7,6},{8,9},{9,8},{10,11... | collective-permute-start | bytes 786440 | tf_op jit(solution)/shard_map/ppermute | solution.py:291
  14.8 7.7 %collective-permute-start.4 = (bf16[8,128,128]{2,1,0:T(8,128)(2,1)S(1)}, bf16[8,128,128]{2,1,0:T(8,128)(2,1)S(1)}, u32[]{:S(2)}, u32[]{:S(2)}) collective-permute-start(bf16[8,128,128]{2,1,0:T(8,128)(2,1)S(1)} %get-tuple-element.41.rest_1_), channel_id=1, source_target_pairs={{0,2},{1,3},{2,0},{3,1},{4,6},{5,7},{6,4},{7,5},{8,10},{9,11},{10,... | collective-permute-start | bytes 786440 | tf_op jit(solution)/shard_map/ppermute | solution.py:291
  18.5 12.2 %collective-permute-start.6 = (bf16[2,8,128,128]{3,2,1,0:T(8,128)(2,1)S(1)}, bf16[2,8,128,128]{3,2,1,0:T(8,128)(2,1)S(1)}, u32[]{:S(2)}, u32[]{:S(2)}) collective-permute-start(bf16[2,8,128,128]{3,2,1,0:T(8,128)(2,1)S(1)} %pack.2), channel_id=1, source_target_pairs={{0,1},{1,0},{2,3},{3,2},{4,5},{5,4},{6,7},{7,6},{8,9},{9,8},{10,11... | collective-permute-start | bytes 1572872 | tf_op jit(solution)/shard_map/ppermute | solution.py:291
  19.1 11.5 %collective-permute-start.7 = (bf16[8,128,128]{2,1,0:T(8,128)(2,1)S(1)}, bf16[8,128,128]{2,1,0:T(8,128)(2,1)S(1)}, u32[]{:S(2)}, u32[]{:S(2)}) collective-permute-start(bf16[8,128,128]{2,1,0:T(8,128)(2,1)S(1)} %get-tuple-element.42.refs_3_.refs_0_.refs_2_), channel_id=1, source_target_pairs={{0,2},{1,3},{2,0},{3,1},{4,6},{5,7},{6,4},{7,5},{8,10},{9,11},{10,... | collective-permute-start | bytes 786440 | tf_op jit(solution)/shard_map/ppermute | solution.py:291
  22.6 8.0 %collective-permute-start.5 = (bf16[8,128,128]{2,1,0:T(8,128)(2,1)S(1)}, bf16[8,128,128]{2,1,0:T(8,128)(2,1)S(1)}, u32[]{:S(2)}, u32[]{:S(2)}) collective-permute-start(bf16[8,128,128]{2,1,0:T(8,128)(2,1)S(1)} %merge.3.after.refs_0_), channel_id=1, source_target_pairs={{0,4},{1,5},{2,6},{3,7},{4,0},{5,1},{6,2},{7,3},{8,12},{9,13},{10,... | collective-permute-start | bytes 786440 | tf_op jit(solution)/shard_map/ppermute | solution.py:291
  30.8 9.4 %collective-permute-start.8 = (bf16[8,128,128]{2,1,0:T(8,128)(2,1)S(1)}, bf16[8,128,128]{2,1,0:T(8,128)(2,1)S(1)}, u32[]{:S(2)}, u32[]{:S(2)}) collective-permute-start(bf16[8,128,128]{2,1,0:T(8,128)(2,1)S(1)} %merge.4.after), channel_id=1, source_target_pairs={{0,4},{1,5},{2,6},{3,7},{4,8},{5,9},{6,10},{7,11},{8,12},{9,13},{1... | collective-permute-start | bytes 786440 | tf_op jit(solution)/shard_map/ppermute | solution.py:448
  31.1 14.2 %collective-permute-start.9 = (bf16[8,128,128]{2,1,0:T(8,128)(2,1)S(1)}, bf16[8,128,128]{2,1,0:T(8,128)(2,1)S(1)}, u32[]{:S(2)}, u32[]{:S(2)}) collective-permute-start(bf16[8,128,128]{2,1,0:T(8,128)(2,1)S(1)} %merge.4.after), channel_id=1, source_target_pairs={{0,4},{1,5},{2,6},{3,7},{4,12},{5,13},{6,14},{7,15},{8,0},{9,1},{1... | collective-permute-start | bytes 786440 | tf_op jit(solution)/shard_map/ppermute | solution.py:448
  33.5 11.8 %collective-permute-start.10 = (bf16[8,128,128]{2,1,0:T(8,128)(2,1)S(1)}, bf16[8,128,128]{2,1,0:T(8,128)(2,1)S(1)}, u32[]{:S(2)}, u32[]{:S(2)}) collective-permute-start(bf16[8,128,128]{2,1,0:T(8,128)(2,1)S(1)} %collective-permute-done.5.refs_1_.rest_2_), channel_id=1, source_target_pairs={{0,2},{1,3},{2,0},{3,1},{4,6},{5,7},{6,4},{7,5},{8,10},{9,11},{10,... | collective-permute-start | bytes 786440 | tf_op jit(solution)/shard_map/ppermute | solution.py:291
  45.4 5.0 %collective-permute-start.11 = (bf16[5,8,128,128]{3,2,1,0:T(8,128)(2,1)S(1)}, bf16[5,8,128,128]{3,2,1,0:T(8,128)(2,1)S(1)}, u32[]{:S(2)}, u32[]{:S(2)}) collective-permute-start(bf16[5,8,128,128]{3,2,1,0:T(8,128)(2,1)S(1)} %pack.3), channel_id=1, source_target_pairs={{0,1},{1,0},{2,3},{3,2},{4,5},{5,4},{6,7},{7,6},{8,9},{9,8},{10,11... | collective-permute-start | bytes 3932168 | tf_op jit(solution)/shard_map/ppermute | solution.py:291
  46.7 7.9 %collective-permute-start.12 = (bf16[8,128,128]{2,1,0:T(8,128)(2,1)S(1)}, bf16[8,128,128]{2,1,0:T(8,128)(2,1)S(1)}, u32[]{:S(2)}, u32[]{:S(2)}) collective-permute-start(bf16[8,128,128]{2,1,0:T(8,128)(2,1)S(1)} %choose.1.refs_2_.rest_3_), channel_id=1, source_target_pairs={{0,2},{1,3},{2,0},{3,1},{4,6},{5,7},{6,4},{7,5},{8,10},{9,11},{10,... | collective-permute-start | bytes 786440 | tf_op jit(solution)/shard_map/ppermute | solution.py:291
  54.7 3.4 %collective-permute-start.13 = (bf16[8,128,128]{2,1,0:T(8,128)(2,1)S(1)}, bf16[8,128,128]{2,1,0:T(8,128)(2,1)S(1)}, u32[]{:S(2)}, u32[]{:S(2)}) collective-permute-start(bf16[8,128,128]{2,1,0:T(8,128)(2,1)S(1)} %merge.5.rest_3_), channel_id=1, source_target_pairs={{0,1},{1,0},{2,3},{3,2},{4,5},{5,4},{6,7},{7,6},{8,9},{9,8},{10,11... | collective-permute-start | bytes 786440 | tf_op jit(solution)/shard_map/ppermute | solution.py:291
